TPU v7x, 32 devices: a whole 2x2x4 slice. The times are simulated.
32 devices in a mesh: dp: 8 (over y, x, core), tensor: 4 (over z).
Axes of the slice: x: 2, y: 2, z: 4, core: 2. Of those that a mesh axis runs over, the one named last changes fastest.
Arguments:
- inputs: bfloat16 [8192, 2048], P(('dp', 'tensor')), may hold values from -6 to 6
- gain_attn: bfloat16 [2048], P('dp'), may hold values from 0.5 to 1.5
- w_query: bfloat16 [2048, 2048], P('dp', 'tensor'), may hold values from -0.125 to 0.125
- w_key: bfloat16 [2048, 2048], P('dp', 'tensor'), may hold values from -0.125 to 0.125
- w_value: bfloat16 [2048, 4096], P('dp', 'tensor'), may hold values from -0.125 to 0.125
- w_gate: bfloat16 [2048, 4096], P('dp', 'tensor'), may hold values from -0.125 to 0.125
- w_out: bfloat16 [4096, 2048], P('tensor', 'dp'), may hold values from -0.125 to 0.125
- gain_mlp: bfloat16 [2048], P('dp'), may hold values from 0.5 to 1.5
- w_act: bfloat16 [2048, 4096], P('dp', 'tensor'), may hold values from -0.125 to 0.125
- w_lin: bfloat16 [2048, 4096], P('dp', 'tensor'), may hold values from -0.125 to 0.125
- w_down: bfloat16 [4096, 2048], P('tensor', 'dp'), may hold values from -0.125 to 0.125
- cotangent: bfloat16 [8192, 2048], P(('dp', 'tensor')), may hold values from -6 to 6
- lengths: int32 [8, 3], P('dp'), may hold values from 1 to 896, as said below
- offsets: int32 [8, 3], P('dp'), may hold values from 0 to 960, as said below
Outputs:
- outputs: bfloat16 [8192, 2048], P(('dp', 'tensor'))
- grad_inputs: float32 [8192, 2048], P(('dp', 'tensor'))
- grad_gain_attn: float32 [2048], P('dp')
- grad_w_query: float32 [2048, 2048], P('dp', 'tensor')
- grad_w_key: float32 [2048, 2048], P('dp', 'tensor')
- grad_w_value: float32 [2048, 4096], P('dp', 'tensor')
- grad_w_gate: float32 [2048, 4096], P('dp', 'tensor')
- grad_w_out: float32 [4096, 2048], P('tensor', 'dp')
- grad_gain_mlp: float32 [2048], P('dp')
- grad_w_act: float32 [2048, 4096], P('dp', 'tensor')
- grad_w_lin: float32 [2048, 4096], P('dp', 'tensor')
- grad_w_down: float32 [4096, 2048], P('tensor', 'dp')
Inputs may be any that keep to these rules, and one draw needn't show every extreme that they name: `lengths`: each group holds 3 sequences; the first is the longest. `offsets`: multiples of 64; in each group the first sequence starts at 0, later ones start after the earlier ones end, and the last ends at most at 1024.
All inputs are finite; a program needn't handle non-finite values.
Results may differ from a plain program's by a relative error of at most 0.024.
Values may be sent and summed in bfloat16 or wider, within the bound.
No kernel may reach another device: no remote copies, remote signals or barrier semaphores. Data moves between devices by JAX's collectives and lax.ppermute only.
A program may use at most 192 MiB of HBM per device.

v0:
```python
import math

import jax
import jax.numpy as jnp
from jax import lax
from jax.sharding import PartitionSpec as P

KD = 256
BLOCK = 512


epsilon = 1e-05
group_floor = 1.0


def layer_norm(values, floor_value=epsilon):
    center = values - jnp.mean(values, axis=-1, keepdims=True)
    scale_inv = lax.rsqrt(jnp.mean(center * center, axis=-1, keepdims=True) + floor_value)
    return (center * scale_inv, scale_inv)


def norm_back(grad_norm, normed, scale_inv):
    mean_grad = jnp.mean(grad_norm, axis=-1, keepdims=True)
    mean_cross = jnp.mean(grad_norm * normed, axis=-1, keepdims=True)
    return (grad_norm - mean_grad - normed * mean_cross) * scale_inv


def sequence_layout(lengths, offsets, total):
    places = jnp.arange(total, dtype=jnp.int32)[:, None]
    inside = (places >= offsets[None, :]) & (places < offsets[None, :] + lengths[None, :])
    numbers = jnp.arange(1, offsets.shape[0] + 1, dtype=jnp.int32)
    segment = jnp.sum(jnp.where(inside, numbers[None, :], 0), axis=1) - 1
    position = places[:, 0] - jnp.sum(jnp.where(inside, offsets[None, :], 0), axis=1)
    return (segment, position.astype(jnp.float32))


def rotate(values, position, direction):
    half = values.shape[-1] // 2
    frequency = jnp.exp(
        -math.log(10000.0) * jnp.arange(half, dtype=jnp.float32) * 2.0 / values.shape[-1]
    )
    angles = position[:, None] * frequency[None, :]
    cosine = jnp.cos(angles)
    sine = jnp.sin(angles) * direction
    first = values[..., :half]
    second = values[..., half:]
    return jnp.concatenate(
        [first * cosine - second * sine, first * sine + second * cosine], axis=-1
    )


def block_consts(segment, start, log_decay, size):
    seg_block = lax.dynamic_slice_in_dim(segment, start, size)
    before = lax.dynamic_slice_in_dim(segment, jnp.maximum(start - 1, 0), 1)[0]
    before = jnp.where(start > 0, before, -2)
    final = seg_block[size - 1]
    places = jnp.arange(size, dtype=jnp.int32)
    living = seg_block >= 0
    same = (
        (seg_block[:, None] == seg_block[None, :])
        & living[:, None]
        & (places[None, :] <= places[:, None])
    )
    spacing = jnp.maximum(places[:, None] - places[None, :], 0).astype(jnp.float32)
    decay = jnp.where(same[None], jnp.exp(spacing[None] * log_decay[:, None, None]), 0.0)
    inward_state = ((seg_block == before) & living).astype(jnp.float32)[None, :] * jnp.exp(
        (places + 1).astype(jnp.float32)[None, :] * log_decay[:, None]
    )
    outward_state = ((seg_block == final) & living).astype(jnp.float32)[None, :] * jnp.exp(
        (size - 1 - places).astype(jnp.float32)[None, :] * log_decay[:, None]
    )
    carried_state = jnp.where((final == before) & (final >= 0), jnp.exp(size * log_decay), 0.0)
    return (decay, inward_state, outward_state, carried_state)


def split_two(values):
    high_part = values.astype(jnp.bfloat16)
    rest_part = (values - high_part.astype(jnp.float32)).astype(jnp.bfloat16)
    return (high_part, rest_part)


def split_matmul_product(form, left, right):
    if left.dtype == jnp.float32:
        left_high, left_rest = split_two(left)
        return jnp.einsum(form, left_high, right, preferred_element_type=jnp.float32) + jnp.einsum(
            form, left_rest, right, preferred_element_type=jnp.float32
        )
    right_high, right_rest = split_two(right)
    return jnp.einsum(form, left, right_high, preferred_element_type=jnp.float32) + jnp.einsum(
        form, left, right_rest, preferred_element_type=jnp.float32
    )


def split_heads(matrix, heads):
    return matrix.reshape(matrix.shape[0], heads, -1).transpose(1, 0, 2)


def join_heads(tensor):
    return tensor.transpose(1, 0, 2).reshape(tensor.shape[1], -1)


def to_blocks(tensor):
    heads, total, width = tensor.shape
    return tensor.reshape(heads, total // BLOCK, BLOCK, width).transpose(1, 0, 2, 3)


def from_blocks(blocks):
    count, heads, size, width = blocks.shape
    return blocks.transpose(1, 0, 2, 3).reshape(heads, count * size, width)


def retain_forward(query_rot, key_rot, values, segment, log_decay):
    heads, total, key_size = query_rot.shape
    count = total // BLOCK

    def step(recurrent_state, item):
        index, query_block_rows, key_block_rows, value_block_rows = item
        decay, inward_state, outward_state, carried_state = block_consts(
            segment, index * BLOCK, log_decay, BLOCK
        )
        scores = jnp.einsum(
            "hik,hjk->hij", query_block_rows, key_block_rows, preferred_element_type=jnp.float32
        )
        weights = (decay * scores).astype(jnp.bfloat16)
        inner = jnp.einsum(
            "hij,hjv->hiv", weights, value_block_rows, preferred_element_type=jnp.float32
        )
        cross_scores = inward_state[..., None] * split_matmul_product(
            "zpu,zud->zpd", query_block_rows, recurrent_state
        )
        scaled_key_rows = key_block_rows.astype(jnp.float32) * outward_state[..., None]
        updated_state = carried_state[:, None, None] * recurrent_state + split_matmul_product(
            "eaw,eag->ewg", scaled_key_rows, value_block_rows
        )
        return (updated_state, (inner + cross_scores, recurrent_state))

    start_state = jnp.zeros((heads, key_size, values.shape[2]), jnp.float32)
    items = (
        jnp.arange(count, dtype=jnp.int32),
        to_blocks(query_rot),
        to_blocks(key_rot),
        to_blocks(values),
    )
    _, (blocks, states) = lax.scan(step, start_state, items)
    return (from_blocks(blocks), states)


def retain_backward(query_rot, key_rot, values, grad_low, states, segment, log_decay):
    heads, total, key_size = query_rot.shape
    count = total // BLOCK

    def step(state_gradient, item):
        (
            index,
            query_block_rows,
            key_block_rows,
            value_block_rows,
            grad_block_rows,
            incoming_state,
        ) = item
        decay, inward_state, outward_state, carried_state = block_consts(
            segment, index * BLOCK, log_decay, BLOCK
        )
        scores = jnp.einsum(
            "hik,hjk->hij", query_block_rows, key_block_rows, preferred_element_type=jnp.float32
        )
        weights = (decay * scores).astype(jnp.bfloat16)
        grad_weights = jnp.einsum(
            "hiv,hjv->hij", grad_block_rows, value_block_rows, preferred_element_type=jnp.float32
        )
        grad_scores = (grad_weights * decay).astype(jnp.bfloat16)
        grad_query = jnp.einsum(
            "hij,hjk->hik", grad_scores, key_block_rows, preferred_element_type=jnp.float32
        )
        grad_query = grad_query + inward_state[..., None] * split_matmul_product(
            "zup,zep->zue", grad_block_rows, incoming_state
        )
        grad_key = jnp.einsum(
            "hij,hik->hjk", grad_scores, query_block_rows, preferred_element_type=jnp.float32
        )
        grad_key = grad_key + outward_state[..., None] * split_matmul_product(
            "ogx,osx->ogs", value_block_rows, state_gradient
        )
        grad_value = jnp.einsum(
            "hij,hiv->hjv", weights, grad_block_rows, preferred_element_type=jnp.float32
        )
        grad_value = grad_value + outward_state[..., None] * split_matmul_product(
            "oyq,oqb->oyb", key_block_rows, state_gradient
        )
        scaled_query_rows = query_block_rows.astype(jnp.float32) * inward_state[..., None]
        grad_before = carried_state[:, None, None] * state_gradient + split_matmul_product(
            "xtq,xta->xqa", scaled_query_rows, grad_block_rows
        )
        return (grad_before, (grad_query, grad_key, grad_value))

    start_grad = jnp.zeros((heads, key_size, values.shape[2]), jnp.float32)
    items = (
        jnp.arange(count, dtype=jnp.int32),
        to_blocks(query_rot),
        to_blocks(key_rot),
        to_blocks(values),
        to_blocks(grad_low),
        states,
    )
    _, (grad_q, grad_k, grad_v) = lax.scan(step, start_grad, items, reverse=True)
    return (from_blocks(grad_q), from_blocks(grad_k), from_blocks(grad_v))


def shards(
    inputs,
    gain_attn,
    w_query,
    w_key,
    w_value,
    w_gate,
    w_out,
    gain_mlp,
    w_act,
    w_lin,
    w_down,
    cotangent,
    lengths,
    offsets,
):
    rows = inputs.shape[0]
    total = rows * lax.axis_size("tensor")
    heads_here = w_query.shape[1] // KD
    wq_full, wk_full, wv_full, wg_full, wo_full, gain_one = (
        lax.all_gather(w_query, "dp", axis=0, tiled=True),
        lax.all_gather(w_key, "dp", axis=0, tiled=True),
        lax.all_gather(w_value, "dp", axis=0, tiled=True),
        lax.all_gather(w_gate, "dp", axis=0, tiled=True),
        lax.all_gather(w_out, "dp", axis=1, tiled=True),
        lax.all_gather(gain_attn, "dp", axis=0, tiled=True),
    )
    wa_full, wb_full, wd_full, gain_two = (
        lax.all_gather(w_act, "dp", axis=0, tiled=True),
        lax.all_gather(w_lin, "dp", axis=0, tiled=True),
        lax.all_gather(w_down, "dp", axis=1, tiled=True),
        lax.all_gather(gain_mlp, "dp", axis=0, tiled=True),
    )
    gain_one = gain_one.astype(jnp.float32)
    gain_two = gain_two.astype(jnp.float32)
    head_first = lax.axis_index("tensor") * heads_here
    head_numbers = (head_first + jnp.arange(heads_here, dtype=jnp.int32)).astype(jnp.float32)
    log_decay = jnp.log(1.0 - jnp.exp2(-5.0 - head_numbers))
    segment, position = sequence_layout(lengths[0], offsets[0], total)
    scale_query = KD ** (-0.5)
    rows_wide = inputs.astype(jnp.float32)
    normed_one, inv_one = layer_norm(rows_wide)
    h_attn = (normed_one * gain_one).astype(jnp.bfloat16)
    h_group = lax.all_gather(h_attn, "tensor", axis=0, tiled=True)
    query_pre = split_heads(
        jnp.dot(h_group, wq_full, preferred_element_type=jnp.float32), heads_here
    )
    key_pre = split_heads(jnp.dot(h_group, wk_full, preferred_element_type=jnp.float32), heads_here)
    query_rot = (rotate(query_pre, position, 1.0) * scale_query).astype(jnp.bfloat16)
    key_rot = rotate(key_pre, position, 1.0).astype(jnp.bfloat16)
    values = split_heads(
        jnp.dot(h_group, wv_full, preferred_element_type=jnp.float32).astype(jnp.bfloat16),
        heads_here,
    )
    gate_pre = split_heads(
        jnp.dot(h_group, wg_full, preferred_element_type=jnp.float32), heads_here
    )
    retained, states = retain_forward(query_rot, key_rot, values, segment, log_decay)
    grouped, inv_group = layer_norm(retained, group_floor)
    sigmoid_gate = jax.nn.sigmoid(gate_pre)
    swish_gate = gate_pre * sigmoid_gate
    mixed = join_heads(swish_gate * grouped).astype(jnp.bfloat16)
    middle = rows_wide + lax.psum_scatter(
        jnp.dot(mixed, wo_full, preferred_element_type=jnp.float32),
        "tensor",
        scatter_dimension=0,
        tiled=True,
    )
    normed_two, inv_two = layer_norm(middle)
    h_mlp = (normed_two * gain_two).astype(jnp.bfloat16)
    h_group_two = lax.all_gather(h_mlp, "tensor", axis=0, tiled=True)
    act = jnp.dot(h_group_two, wa_full, preferred_element_type=jnp.float32)
    lin = jnp.dot(h_group_two, wb_full, preferred_element_type=jnp.float32)
    gelu_act, gelu_back = jax.vjp(jax.nn.gelu, act)
    hidden = (gelu_act * lin).astype(jnp.bfloat16)
    outputs = (
        middle
        + lax.psum_scatter(
            jnp.dot(hidden, wd_full, preferred_element_type=jnp.float32).astype(jnp.bfloat16),
            "tensor",
            scatter_dimension=0,
            tiled=True,
        ).astype(jnp.float32)
    ).astype(jnp.bfloat16)
    cot_group = lax.all_gather(cotangent, "tensor", axis=0, tiled=True)
    grad_hidden = jnp.dot(cot_group, wd_full.T, preferred_element_type=jnp.float32)
    grad_down = jnp.dot(hidden.T, cot_group, preferred_element_type=jnp.float32)
    grad_act = gelu_back(grad_hidden * lin)[0].astype(jnp.bfloat16)
    grad_lin = (grad_hidden * gelu_act).astype(jnp.bfloat16)
    grad_wa = jnp.dot(h_group_two.T, grad_act, preferred_element_type=jnp.float32)
    grad_wb = jnp.dot(h_group_two.T, grad_lin, preferred_element_type=jnp.float32)
    grad_hmlp = lax.psum_scatter(
        (
            jnp.dot(grad_act, wa_full.T, preferred_element_type=jnp.float32)
            + jnp.dot(grad_lin, wb_full.T, preferred_element_type=jnp.float32)
        ).astype(jnp.bfloat16),
        "tensor",
        scatter_dimension=0,
        tiled=True,
    ).astype(jnp.float32)
    gain_two_term = jnp.sum(grad_hmlp * normed_two, axis=0)
    grad_middle = cotangent.astype(jnp.float32) + norm_back(
        grad_hmlp * gain_two, normed_two, inv_two
    )
    grad_mid_group = lax.all_gather(grad_middle.astype(jnp.bfloat16), "tensor", axis=0, tiled=True)
    grad_wo = jnp.dot(mixed.T, grad_mid_group, preferred_element_type=jnp.float32)
    grad_mixed = split_heads(
        jnp.dot(grad_mid_group, wo_full.T, preferred_element_type=jnp.float32), heads_here
    )
    grad_gate = join_heads(
        grad_mixed * grouped * sigmoid_gate * (1.0 + gate_pre * (1.0 - sigmoid_gate))
    ).astype(jnp.bfloat16)
    grad_retained = norm_back(grad_mixed * swish_gate, grouped, inv_group).astype(jnp.bfloat16)
    grad_qrot, grad_krot, grad_vals = retain_backward(
        query_rot, key_rot, values, grad_retained, states, segment, log_decay
    )
    grad_query = join_heads(rotate(grad_qrot * scale_query, position, -1.0)).astype(jnp.bfloat16)
    grad_key = join_heads(rotate(grad_krot, position, -1.0)).astype(jnp.bfloat16)
    grad_value = join_heads(grad_vals).astype(jnp.bfloat16)
    grad_wq = jnp.dot(h_group.T, grad_query, preferred_element_type=jnp.float32)
    grad_wk = jnp.dot(h_group.T, grad_key, preferred_element_type=jnp.float32)
    grad_wv = jnp.dot(h_group.T, grad_value, preferred_element_type=jnp.float32)
    grad_wg = jnp.dot(h_group.T, grad_gate, preferred_element_type=jnp.float32)
    total_rows = jnp.dot(grad_query, wq_full.T, preferred_element_type=jnp.float32)
    total_rows = total_rows + jnp.dot(grad_key, wk_full.T, preferred_element_type=jnp.float32)
    total_rows = total_rows + jnp.dot(grad_value, wv_full.T, preferred_element_type=jnp.float32)
    grad_hattn = lax.psum_scatter(
        (total_rows + jnp.dot(grad_gate, wg_full.T, preferred_element_type=jnp.float32)).astype(
            jnp.bfloat16
        ),
        "tensor",
        scatter_dimension=0,
        tiled=True,
    ).astype(jnp.float32)
    gain_one_term = jnp.sum(grad_hattn * normed_one, axis=0)
    grad_inputs = grad_middle + norm_back(grad_hattn * gain_one, normed_one, inv_one)
    gain_one_sum, gain_two_sum = lax.psum((gain_one_term, gain_two_term), "tensor")
    (
        grad_wq_own,
        grad_wk_own,
        grad_wv_own,
        grad_wg_own,
        grad_wo_own,
        grad_gain_one,
        grad_gain_two,
        grad_wa_own,
        grad_wb_own,
        grad_wd_own,
    ) = (
        lax.psum_scatter(
            grad_wq.astype(jnp.bfloat16), "dp", scatter_dimension=0, tiled=True
        ).astype(jnp.float32),
        lax.psum_scatter(
            grad_wk.astype(jnp.bfloat16), "dp", scatter_dimension=0, tiled=True
        ).astype(jnp.float32),
        lax.psum_scatter(
            grad_wv.astype(jnp.bfloat16), "dp", scatter_dimension=0, tiled=True
        ).astype(jnp.float32),
        lax.psum_scatter(
            grad_wg.astype(jnp.bfloat16), "dp", scatter_dimension=0, tiled=True
        ).astype(jnp.float32),
        lax.psum_scatter(
            grad_wo.astype(jnp.bfloat16), "dp", scatter_dimension=1, tiled=True
        ).astype(jnp.float32),
        lax.psum_scatter(
            gain_one_sum.astype(jnp.bfloat16), "dp", scatter_dimension=0, tiled=True
        ).astype(jnp.float32),
        lax.psum_scatter(
            gain_two_sum.astype(jnp.bfloat16), "dp", scatter_dimension=0, tiled=True
        ).astype(jnp.float32),
        lax.psum_scatter(
            grad_wa.astype(jnp.bfloat16), "dp", scatter_dimension=0, tiled=True
        ).astype(jnp.float32),
        lax.psum_scatter(
            grad_wb.astype(jnp.bfloat16), "dp", scatter_dimension=0, tiled=True
        ).astype(jnp.float32),
        lax.psum_scatter(
            grad_down.astype(jnp.bfloat16), "dp", scatter_dimension=1, tiled=True
        ).astype(jnp.float32),
    )
    return (
        outputs,
        grad_inputs,
        grad_gain_one,
        grad_wq_own,
        grad_wk_own,
        grad_wv_own,
        grad_wg_own,
        grad_wo_own,
        grad_gain_two,
        grad_wa_own,
        grad_wb_own,
        grad_wd_own,
    )


def solution(mesh):
    return jax.shard_map(
        shards,
        mesh=mesh,
        in_specs=(
            P(("dp", "tensor"), None),
            P("dp"),
            P("dp", "tensor"),
            P("dp", "tensor"),
            P("dp", "tensor"),
            P("dp", "tensor"),
            P("tensor", "dp"),
            P("dp"),
            P("dp", "tensor"),
            P("dp", "tensor"),
            P("tensor", "dp"),
            P(("dp", "tensor"), None),
            P("dp", None),
            P("dp", None),
        ),
        out_specs=(
            P(("dp", "tensor"), None),
            P(("dp", "tensor"), None),
            P("dp"),
            P("dp", "tensor"),
            P("dp", "tensor"),
            P("dp", "tensor"),
            P("dp", "tensor"),
            P("tensor", "dp"),
            P("dp"),
            P("dp", "tensor"),
            P("dp", "tensor"),
            P("tensor", "dp"),
        ),
        check_vma=False,
    )
```

profile of v0, /device:TPU:0, one launch (start us, length us, event | category | flops | bytes accessed | tf_op | source)
XLA Modules:
  0.0 1510.6 jit_solution(14252771305614852570)
XLA Ops:
  8.6 10.3 all-gather
  29.5 11.1 all-gather.23.cloned.1.call-done
  40.5 82.9 %all-gather.15.cloned.1.call-done = bf16[1024,2048]{1,0:T(8,128)(2,1)} async-done(((bf16[256,2048]{1,0:T(8,128)(2,1)}), bf16[1024,2048]{1,0:T(8,128)(2,1)}) %all-gather.15.cloned.1.call-update) | async-done | bytes 4194320 | tf_op jit(solution)/shard_map/all_gather | solution.py:252
  132.0 19.8 %all-gather.19.cloned.1.call-done = bf16[2048,512]{1,0:T(8,128)(2,1)} async-done(((bf16[256,512]{1,0:T(8,128)(2,1)}), bf16[2048,512]{1,0:T(8,128)(2,1)}) %all-gather.19.cloned.1.call-update) | async-done | bytes 2097168 | tf_op jit(solution)/shard_map/all_gather | solution.py:230
  166.2 24.2 %all-gather.21.cloned.1.call-done = bf16[2048,1024]{1,0:T(8,128)(2,1)} async-done(((bf16[256,1024]{1,0:T(8,128)(2,1)}), bf16[2048,1024]{1,0:T(8,128)(2,1)}) %all-gather.21.cloned.1.call-update) | async-done | bytes 4194320 | tf_op jit(solution)/shard_map/all_gather | solution.py:231
  202.7 34.4 %while.41 = (s32[]{:T(128)}, f32[2,256,512]{2,1,0:T(8,128)S(1)}, f32[2,2,512,512]{3,2,0,1:T(8,128)}, f32[2,2,256,512]{3,2,1,0:T(8,128)}, s32[2]{0:T(128)S(1)}, /...) while((s32[]{:T(128)}, f32[2,256,512]{2,1,0:T(8,128)S(1)}, ...), condition=%wide.region_5.6_spmd.clone.clone, body=%wide.region_4.5_spmd.clone.sunk.clone | while | flops 1889806336 | bytes 44617604 | solution.py:144
  241.7 10.0 fusion.182
  268.0 10.7 fusion.185
  288.4 134.9 %reduce-scatter.13.cloned.1.call-done = f32[256,2048]{1,0:T(8,128)} async-done(((f32[1024,2048]{1,0:T(8,128)}), f32[256,2048]{1,0:T(8,128)}) %reduce-scatter.13.cloned.1.call-update) | async-done | bytes 2097168 | tf_op jit(solution)/shard_map/reduce_scatter | solution.py:271
  429.9 32.8 %all-gather.29.cloned.1.call-done = bf16[2048,1024]{1,0:T(8,128)(2,1)} async-done(((bf16[256,1024]{1,0:T(8,128)(2,1)}), bf16[2048,1024]{1,0:T(8,128)(2,1)}) %all-gather.29.cloned.1.call-update) | async-done | bytes 4194320 | tf_op jit(solution)/shard_map/all_gather | solution.py:237
  462.7 82.9 %all-gather.27.cloned.1.call-done = bf16[1024,2048]{1,0:T(8,128)(2,1)} async-done(((bf16[256,2048]{1,0:T(8,128)(2,1)}), bf16[1024,2048]{1,0:T(8,128)(2,1)}) %all-gather.27.cloned.1.call-update) | async-done | bytes 4194320 | tf_op jit(solution)/shard_map/all_gather | solution.py:279
  545.7 9.9 fusion.186
  555.6 27.1 %all-gather.31.cloned.1.call-done = bf16[2048,1024]{1,0:T(8,128)(2,1)} async-done(((bf16[256,1024]{1,0:T(8,128)(2,1)}), bf16[2048,1024]{1,0:T(8,128)(2,1)}) %all-gather.31.cloned.1.call-update) | async-done | bytes 4194320 | tf_op jit(solution)/shard_map/all_gather | solution.py:238
  582.7 10.0 fusion.187
  592.7 72.3 %all-gather.35.cloned.1.call-done = bf16[1024,2048]{1,0:T(8,128)(2,1)} async-done(((bf16[256,2048]{1,0:T(8,128)(2,1)}), bf16[1024,2048]{1,0:T(8,128)(2,1)}) %all-gather.35.cloned.1.call-update) | async-done | bytes 4194320 | tf_op jit(solution)/shard_map/all_gather | solution.py:293
  665.1 37.7 %all-gather.33.cloned.1.call-done = bf16[1024,2048]{1,0:T(8,128)(2,1)} async-done(((bf16[1024,256]{1,0:T(8,128)(2,1)}), bf16[1024,2048]{1,0:T(8,128)(2,1)}) %all-gather.33.cloned.1.call-update) | async-done | bytes 4194320 | tf_op jit(solution)/shard_map/all_gather | solution.py:239
  702.8 13.6 multiply_convert_fusion.4
  737.0 67.2 %reduce-scatter.17.cloned.1.call-done = bf16[256,2048]{1,0:T(8,128)(2,1)} async-done(((bf16[1024,2048]{1,0:T(8,128)(2,1)}), bf16[256,2048]{1,0:T(8,128)(2,1)}) %reduce-scatter.17.cloned.1.call-update) | async-done | bytes 1048592 | tf_op jit(solution)/shard_map/reduce_scatter | solution.py:300
  807.6 76.2 %reduce-scatter.15.cloned.1.call-done = bf16[256,2048]{1,0:T(8,128)(2,1)} async-done(((bf16[1024,2048]{1,0:T(8,128)(2,1)}), bf16[256,2048]{1,0:T(8,128)(2,1)}) %reduce-scatter.15.cloned.1.call-update) | async-done | bytes 1048592 | tf_op jit(solution)/shard_map/reduce_scatter | solution.py:286
  919.7 50.9 %all-gather.37.cloned.1.call-done = bf16[1024,2048]{1,0:T(8,128)(2,1)} async-done(((bf16[256,2048]{1,0:T(8,128)(2,1)}), bf16[1024,2048]{1,0:T(8,128)(2,1)}) %all-gather.37.cloned.1.call-update) | async-done | bytes 4194320 | tf_op jit(solution)/shard_map/all_gather | solution.py:313
  970.5 9.9 fusion.189
  999.6 53.7 %while.42 = (s32[]{:T(128)}, f32[2,256,512]{2,1,0:T(8,128)S(1)}, f32[2,2,512,256]{3,2,0,1:T(8,128)}, f32[2,2,512,256]{3,2,0,1:T(8,128)}, bf16[2,2,512,512]{3,2,0...) while((s32[]{:T(128)}, f32[2,256,512]{2,1,0:T(8,128)S(1)}, ...), condition=%wide.region_18.19_spmd.clone.clone, body=%wide.region_17.18_spmd.clone.sunk.clone | while | flops 4043319296 | bytes 114623608 | solution.py:205
  1085.6 9.8 convolution_convert_fusion.5
  1127.3 11.6 add_convert_fusion.2
  1147.2 30.8 %reduce-scatter.23.cloned.1.call-done = bf16[256,512]{1,0:T(8,128)(2,1)} async-done(((bf16[2048,512]{1,0:T(8,128)(2,1)}), bf16[256,512]{1,0:T(8,128)(2,1)}) %reduce-scatter.23.cloned.1.call-update) | async-done | bytes 262160 | tf_op jit(solution)/shard_map/reduce_scatter | solution.py:361
  1179.8 42.6 %reduce-scatter.21.cloned.1.call-done = bf16[256,512]{1,0:T(8,128)(2,1)} async-done(((bf16[2048,512]{1,0:T(8,128)(2,1)}), bf16[256,512]{1,0:T(8,128)(2,1)}) %reduce-scatter.21.cloned.1.call-update) | async-done | bytes 262160 | tf_op jit(solution)/shard_map/reduce_scatter | solution.py:358
  1224.2 53.3 %reduce-scatter.29.cloned.1.call-done = bf16[1024,256]{1,0:T(8,128)(2,1)} async-done(((bf16[1024,2048]{1,0:T(8,128)(2,1)}), bf16[1024,256]{1,0:T(8,128)(2,1)}) %reduce-scatter.29.cloned.1.call-update) | async-done | bytes 524304 | tf_op jit(solution)/shard_map/reduce_scatter | solution.py:370
  1279.5 52.6 %reduce-scatter.25.cloned.1.call-done = bf16[256,1024]{1,0:T(8,128)(2,1)} async-done(((bf16[2048,1024]{1,0:T(8,128)(2,1)}), bf16[256,1024]{1,0:T(8,128)(2,1)}) %reduce-scatter.25.cloned.1.call-update) | async-done | bytes 524304 | tf_op jit(solution)/shard_map/reduce_scatter | solution.py:364
  1334.3 52.9 %reduce-scatter.27.cloned.1.call-done = bf16[256,1024]{1,0:T(8,128)(2,1)} async-done(((bf16[2048,1024]{1,0:T(8,128)(2,1)}), bf16[256,1024]{1,0:T(8,128)(2,1)}) %reduce-scatter.27.cloned.1.call-update) | async-done | bytes 524304 | tf_op jit(solution)/shard_map/reduce_scatter | solution.py:367
  1389.3 76.8 %reduce-scatter.19.cloned.1.call-done = bf16[256,2048]{1,0:T(8,128)(2,1)} async-done(((bf16[1024,2048]{1,0:T(8,128)(2,1)}), bf16[256,2048]{1,0:T(8,128)(2,1)}) %reduce-scatter.19.cloned.1.call-update) | async-done | bytes 1048592 | tf_op jit(solution)/shard_map/reduce_scatter | solution.py:335
  1468.5 18.0 %all-reduce.2 = (bf16[2048]{0:T(1024)(128)(2,1)S(1)}, bf16[2048]{0:T(1024)(128)(2,1)S(1)}) all-reduce(f32[2048]{0:T(1024)S(1)} %get-tuple-element.632, f32[2048]{0:T(1024)S(1)} %copy-done.33), channel_id=1, replica_groups=mesh['dp'=8,'tensor'=4] {'tensor'}, use_global_device_ids=true, to_apply=%region_23.24 | all-reduce | flops 4096 | bytes 24576 | tf_op jit(solution)/shard_map/psum | solution.py:345
  1486.5 12.0 all-reduce.3
  (346 shorter events, 328.5 us)
Async XLA Ops:
  7.2 33.4 %all-gather.23.cloned.1.call-start = ((), (), s32[]{:S(2)}) async-start(), calls=%async_computation.16 | async-start | bytes 2359296 | tf_op jit(solution)/shard_map/all_gather | solution.py:229
  7.9 115.6 %all-gather.15.cloned.1.call-start = ((), (), s32[]{:S(2)}) async-start(), calls=%async_computation.12 | async-start | bytes 5242880 | tf_op jit(solution)/shard_map/all_gather | solution.py:252
  23.6 128.2 %all-gather.19.cloned.1.call-start = ((), (), s32[]{:S(2)}) async-start(), calls=%async_computation.14 | async-start | bytes 2359296 | tf_op jit(solution)/shard_map/all_gather | solution.py:230
  24.3 166.0 %all-gather.21.cloned.1.call-start = ((), (), s32[]{:S(2)}) async-start(), calls=%async_computation.15 | async-start | bytes 4718592 | tf_op jit(solution)/shard_map/all_gather | solution.py:231
  24.9 216.8 %all-gather.17.cloned.1.call-start = ((), (), s32[]{:S(2)}) async-start(), calls=%async_computation.13 | async-start | bytes 4718592 | tf_op jit(solution)/shard_map/all_gather | solution.py:232
  25.5 242.5 %all-gather.25.cloned.1.call-start = ((), (), s32[]{:S(2)}) async-start(), calls=%async_computation.17 | async-start | bytes 4718592 | tf_op jit(solution)/shard_map/all_gather | solution.py:233
  26.1 397.3 %reduce-scatter.13.cloned.1.call-start = ((), (), s32[]{:S(2)}) async-start(), calls=%async_computation.18 | async-start | bytes 10485760 | tf_op jit(solution)/shard_map/reduce_scatter | solution.py:271
  278.7 144.7 %copy-start.11 = (bf16[256,2048]{1,0:T(8,128)(2,1)S(1)}, bf16[256,2048]{1,0:T(8,128)(2,1)}, u32[]{:S(2)}) copy-start(bf16[256,2048]{1,0:T(8,128)(2,1)} %param.18) | copy-start | bytes 3145732
  278.7 184.0 %all-gather.29.cloned.1.call-start = ((), (), s32[]{:S(2)}) async-start(), calls=%async_computation.20 | async-start | bytes 4718592 | tf_op jit(solution)/shard_map/all_gather | solution.py:237
  279.5 266.2 %all-gather.27.cloned.1.call-start = ((), (), s32[]{:S(2)}) async-start(), calls=%async_computation.19 | async-start | bytes 5242880 | tf_op jit(solution)/shard_map/all_gather | solution.py:279
  427.9 154.8 %all-gather.31.cloned.1.call-start = ((), (), s32[]{:S(2)}) async-start(), calls=%async_computation.21 | async-start | bytes 4718592 | tf_op jit(solution)/shard_map/all_gather | solution.py:238
  428.5 236.5 %all-gather.35.cloned.1.call-start = ((), (), s32[]{:S(2)}) async-start(), calls=%async_computation.24 | async-start | bytes 5242880 | tf_op jit(solution)/shard_map/all_gather | solution.py:293
  429.3 273.5 %all-gather.33.cloned.1.call-start = ((), (), s32[]{:S(2)}) async-start(), calls=%async_computation.22 | async-start | bytes 4718592 | tf_op jit(solution)/shard_map/all_gather | solution.py:239
  429.8 374.3 %reduce-scatter.17.cloned.1.call-start = ((), (), s32[]{:S(2)}) async-start(), calls=%async_computation.25 | async-start | bytes 5242880 | tf_op jit(solution)/shard_map/reduce_scatter | solution.py:300
  727.2 156.5 %reduce-scatter.15.cloned.1.call-start = ((), (), s32[]{:S(2)}) async-start(), calls=%async_computation.23 | async-start | bytes 5242880 | tf_op jit(solution)/shard_map/reduce_scatter | solution.py:286
  736.9 146.8 %copy-start.22 = (bf16[256,2048]{1,0:T(8,128)(2,1)S(1)}, bf16[256,2048]{1,0:T(8,128)(2,1)}, u32[]{:S(2)}) copy-start(bf16[256,2048]{1,0:T(8,128)(2,1)} %param.29) | copy-start | bytes 3145732
  736.9 233.6 %all-gather.37.cloned.1.call-start = ((), (), s32[]{:S(2)}) async-start(), calls=%async_computation.26 | async-start | bytes 5242880 | tf_op jit(solution)/shard_map/all_gather | solution.py:313
  889.1 251.7 %reduce-scatter.31.cloned.1.call-start = ((), (), s32[]{:S(2)}) async-start(), calls=%async_computation.33 | async-start | bytes 4718592 | tf_op jit(solution)/shard_map/reduce_scatter | solution.py:379
  898.6 244.3 %reduce-scatter.33.cloned.1.call-start = ((), (), s32[]{:S(2)}) async-start(), calls=%async_computation.34 | async-start | bytes 4718592 | tf_op jit(solution)/shard_map/reduce_scatter | solution.py:382
  908.8 236.3 %reduce-scatter.35.cloned.1.call-start = ((), (), s32[]{:S(2)}) async-start(), calls=%async_computation.35 | async-start | bytes 4718592 | tf_op jit(solution)/shard_map/reduce_scatter | solution.py:385
  919.6 258.4 %reduce-scatter.23.cloned.1.call-start = ((), (), s32[]{:S(2)}) async-start(), calls=%async_computation.29 | async-start | bytes 2359296 | tf_op jit(solution)/shard_map/reduce_scatter | solution.py:361
  1063.7 158.7 %reduce-scatter.21.cloned.1.call-start = ((), (), s32[]{:S(2)}) async-start(), calls=%async_computation.28 | async-start | bytes 2359296 | tf_op jit(solution)/shard_map/reduce_scatter | solution.py:358
  1071.3 206.2 %reduce-scatter.29.cloned.1.call-start = ((), (), s32[]{:S(2)}) async-start(), calls=%async_computation.32 | async-start | bytes 4718592 | tf_op jit(solution)/shard_map/reduce_scatter | solution.py:370
  1081.2 251.0 %reduce-scatter.25.cloned.1.call-start = ((), (), s32[]{:S(2)}) async-start(), calls=%async_computation.30 | async-start | bytes 4718592 | tf_op jit(solution)/shard_map/reduce_scatter | solution.py:364
  1095.4 291.8 %reduce-scatter.27.cloned.1.call-start = ((), (), s32[]{:S(2)}) async-start(), calls=%async_computation.31 | async-start | bytes 4718592 | tf_op jit(solution)/shard_map/reduce_scatter | solution.py:367
  1108.9 357.3 %reduce-scatter.19.cloned.1.call-start = ((), (), s32[]{:S(2)}) async-start(), calls=%async_computation.27 | async-start | bytes 5242880 | tf_op jit(solution)/shard_map/reduce_scatter | solution.py:335
  1224.2 242.0 %copy-start.12 = (bf16[256,2048]{1,0:T(8,128)(2,1)S(1)}, bf16[256,2048]{1,0:T(8,128)(2,1)}, u32[]{:S(2)}) copy-start(bf16[256,2048]{1,0:T(8,128)(2,1)} %param.18) | copy-start | bytes 3145732
  1224.2 242.0 %copy-start.32 = (f32[8,1,256]{2,1,0:T(1,128)S(1)}, f32[8,1,256]{2,1,0:T(1,128)}, u32[]{:S(2)}) copy-start(f32[8,1,256]{2,1,0:T(1,128)} %copy-done.31) | copy-start | bytes 24580
  1224.2 242.0 %copy-start.35 = (f32[256]{0:T(256)S(1)}, f32[256]{0:T(256)}, u32[]{:S(2)}) copy-start(f32[256]{0:T(256)} %copy-done.34) | copy-start | bytes 3076
  1224.2 242.0 %copy-start.37 = (f32[256]{0:T(256)S(1)}, f32[256]{0:T(256)}, u32[]{:S(2)}) copy-start(f32[256]{0:T(256)} %copy-done.36) | copy-start | bytes 3076
  1334.3 134.2 %copy-start.33 = (f32[2048]{0:T(1024)S(1)}, f32[2048]{0:T(1024)}, u32[]{:S(2)}) copy-start(f32[2048]{0:T(1024)} %get-tuple-element.630) | copy-start | bytes 24580
  1466.2 33.6 %copy-start.25 = (bf16[256,2048]{1,0:T(8,128)(2,1)S(1)}, bf16[256,2048]{1,0:T(8,128)(2,1)}, u32[]{:S(2)}) copy-start(bf16[256,2048]{1,0:T(8,128)(2,1)} %reduce-scatter.19.cloned.1.call-done) | copy-start | bytes 3145732
  (53 other events, 175.3 us)
Sparse Core Ops, SparseCore 0:
  9.9 30.5 all-gather.22
  42.7 80.7 all-gather.14
  125.4 26.4 all-gather.18
  153.6 36.7 all-gather.20
  192.1 36.7 all-gather.16
  230.5 37.4 all-gather.24
  278.9 144.4 reduce-scatter.12
  425.3 37.4 all-gather.28
  464.9 80.7 all-gather.26
  547.4 35.2 all-gather.30
  584.3 80.7 all-gather.34
  666.8 35.9 all-gather.32
  727.3 76.7 reduce-scatter.16
  806.4 77.2 reduce-scatter.14
  889.3 81.2 all-gather.36
  973.8 49.8 reduce-scatter.30
  1027.2 51.3 reduce-scatter.32
  1081.8 51.3 reduce-scatter.34
  1136.8 41.2 reduce-scatter.22
  1181.1 41.1 reduce-scatter.20
  1226.1 51.2 reduce-scatter.28
  1280.8 51.3 reduce-scatter.24
  1335.9 51.2 reduce-scatter.26
  1389.4 76.7 reduce-scatter.18
where the time goes:
time: 1520 us; the launch traced here: 1510 us
  waiting for transfers between devices  1040 us (68%)
  matrix products  253 us (17%)
  other arithmetic  81.6 us (5%)
  local copies, waits for them, and re-layouts  61.6 us (4%)
  blocking collectives  49.2 us (3%)
  between operations  15.9 us (1%)
    reduce_scatter x1, waiting for transfers between devices, shards(): lax.psum_scatter(jnp.dot(mixed, wo_full, preferred_element_type=jnp.float...  135 us
    all_gather x1, waiting for transfers between devices, shards(): h_group_two = lax.all_gather(h_mlp, 'tensor', axis=0, tiled=True)  82.9 us
    all_gather x1, waiting for transfers between devices, shards(): h_group = lax.all_gather(h_attn, 'tensor', axis=0, tiled=True)  82.9 us
    reduce_scatter x1, waiting for transfers between devices, shards(): lax.psum_scatter((total_rows + jnp.dot(grad_gate, wg_full.T, preferred_el...  76.8 us
    reduce_scatter x1, waiting for transfers between devices, shards(): lax.psum_scatter(jnp.dot(hidden, wd_full, preferred_element_type=jnp.floa...  76.2 us
    all_gather x1, waiting for transfers between devices, shards(): cot_group = lax.all_gather(cotangent, 'tensor', axis=0, tiled=True)  72.3 us
    reduce_scatter x1, waiting for transfers between devices, shards(): lax.psum_scatter((jnp.dot(grad_act, wa_full.T, preferred_element_type=jnp...  67.2 us
    reduce_scatter x1, waiting for transfers between devices, shards(): lax.psum_scatter(grad_wo.astype(jnp.bfloat16), 'dp', scatter_dimension=1,...  53.3 us
  transfers between devices with their start and end apart: 24, of which 20 were waited for; matrix products, arithmetic and copies ran while one was open for 22% of the time, Pallas kernels for 0%

commit v1 on v0

v1 whole, which is shorter than its diff:
```python
import functools
import math

import jax
import jax.numpy as jnp
from jax import lax
from jax.experimental import pallas as pl
from jax.experimental.pallas import tpu as pltpu
from jax.sharding import PartitionSpec as P

KD = 256
VD = 512
TILE = 256

epsilon = 1e-05
group_floor = 1.0
f32 = jnp.float32
low = jnp.bfloat16
gelu_slope = math.sqrt(2.0 / math.pi)
gelu_cubic = 0.044715


def layer_norm(values, floor_value=epsilon):
    center = values - jnp.mean(values, axis=-1, keepdims=True)
    scale_inv = lax.rsqrt(jnp.mean(center * center, axis=-1, keepdims=True) + floor_value)
    return (center * scale_inv, scale_inv)


def norm_back(grad_norm, normed, scale_inv):
    mean_grad = jnp.mean(grad_norm, axis=-1, keepdims=True)
    mean_cross = jnp.mean(grad_norm * normed, axis=-1, keepdims=True)
    return (grad_norm - mean_grad - normed * mean_cross) * scale_inv


def sequence_layout(lengths, offsets, total):
    places = jnp.arange(total, dtype=jnp.int32)[:, None]
    inside = (places >= offsets[None, :]) & (places < offsets[None, :] + lengths[None, :])
    numbers = jnp.arange(1, offsets.shape[0] + 1, dtype=jnp.int32)
    segment = jnp.sum(jnp.where(inside, numbers[None, :], 0), axis=1) - 1
    position = places[:, 0] - jnp.sum(jnp.where(inside, offsets[None, :], 0), axis=1)
    return (segment, position.astype(f32))


def rotation(position, size):
    half = size // 2
    frequency = jnp.exp(-math.log(10000.0) * jnp.arange(half, dtype=f32) * 2.0 / size)
    angles = position[:, None] * frequency[None, :]
    return (jnp.cos(angles), jnp.sin(angles))


def dot(left, right):
    return jnp.dot(left, right, preferred_element_type=f32)


def dot_nt(left, right):
    return lax.dot_general(left, right, (((1,), (1,)), ((), ())), preferred_element_type=f32)


def dot_tn(left, right):
    return lax.dot_general(left, right, (((0,), (0,)), ((), ())), preferred_element_type=f32)


def add_low(left, right):
    return (left.astype(f32) + right.astype(f32)).astype(low)


def swap(values, axis, bits, name="swap"):
    size = lax.axis_size(axis)
    with jax.named_scope(f"{name}_{axis}{bits}"):
        return lax.ppermute(values, axis, [(i, i ^ bits) for i in range(size)])


def shift(values, axis, step, name="shift"):
    size = lax.axis_size(axis)
    with jax.named_scope(name):
        return lax.ppermute(values, axis, [(i, (i + step) % size) for i in range(size)])


def tie(values, token):
    return values if token is None else lax.optimization_barrier((values, token))[0]


def pick(tokens, stage):
    return tokens[min(stage, len(tokens) - 1)] if tokens else None


def dp_bits(size):
    bits = [1 << b for b in range(1, size.bit_length() - 1)]
    return list(zip(bits, bits[1:] + bits[:1]))


def feature_order(size):
    same = []
    for half in (0, 1):
        held = [0]
        for bits in dp_bits(size):
            held += [k ^ bits[half] for k in held]
        same += [(k, half) for k in held]
    return same + [(k ^ 1, half) for k, half in same]


def gather_start(block):
    half = block.shape[0] // 2
    return [block[:half], block[half:]]


def gather_step(parts, stage, name):
    bits = dp_bits(lax.axis_size("dp"))[stage]
    return [
        jnp.concatenate([part, swap(part, "dp", bit, name)], axis=0)
        for part, bit in zip(sync(*parts), bits)
    ]


def gather_rest(parts, stage, name):
    for step in range(stage, len(dp_bits(lax.axis_size("dp")))):
        parts = gather_step(parts, step, name)
    return jnp.concatenate(parts, axis=0)


def scatter_step(parts, stage, name):
    bits = dp_bits(lax.axis_size("dp"))[-1 - stage]
    sums = []
    for (kept, sent), bit in zip(sync(*parts), bits):
        came = swap(sent, "dp", bit, name)
        half = kept.shape[0] // 2
        sums.append([add_low(kept[i : i + half], came[i : i + half]) for i in (0, half)])
    return sums


def scatter_rest(parts, stage, name):
    for step in range(stage, len(dp_bits(lax.axis_size("dp")))):
        parts = scatter_step(parts, step, name)
    return jnp.concatenate([half for part in parts for half in part], axis=0)


def sync(*values):
    return lax.optimization_barrier(values)


def gather_ring(rows, name, beside):
    pieces = [rows]
    for step in range(1, lax.axis_size("tensor")):
        came = shift(pieces[-1], "tensor", 1, f"{name}_{step}")
        pieces.append(beside(step, came))
    return pieces


def call(kernel, grid, in_specs, out_specs, out_shape, flops, scratch=(), scalars=0, aliases=None, moved=0, exps=0):
    return pl.pallas_call(
        kernel,
        grid_spec=pltpu.PrefetchScalarGridSpec(
            num_scalar_prefetch=scalars,
            grid=grid,
            in_specs=in_specs,
            out_specs=out_specs,
            scratch_shapes=scratch,
        ),
        out_shape=out_shape,
        input_output_aliases=aliases or {},
        compiler_params=pltpu.CompilerParams(
            dimension_semantics=("arbitrary",) * len(grid), vmem_limit_bytes=48 * 1024 * 1024
        ),
        cost_estimate=pl.CostEstimate(flops=0, bytes_accessed=0, transcendentals=0),
    )


def reorder_kernel(table, values, out):
    count = table.shape[0]
    width = values.shape[1] // count
    for place in range(count):
        start = pl.multiple_of(table[place] * width, width)
        out[:, place * width : (place + 1) * width] = values[:, pl.ds(start, width)]


def reorder(values, table):
    count, (rows, width) = table.shape[0], values.shape
    size = width // count
    if size % 128:
        blocks = [
            lax.dynamic_slice_in_dim(values, table[i] * size, size, axis=1) for i in range(count)
        ]
        return jnp.concatenate(blocks, axis=1)
    part = min(rows, 64)
    spec = pl.BlockSpec((part, width), lambda i, _: (i, 0))
    return call(
        reorder_kernel,
        (rows // part,),
        [spec],
        spec,
        jax.ShapeDtypeStruct(values.shape, values.dtype),
        0,
        scalars=1,
        moved=2 * values.size * values.dtype.itemsize,
    )(table, values)


def project_kernel(count, places, *refs):
    own, other, out = refs[count], refs[count + 1], refs[-1]
    half = own.shape[0]
    for i in range(count):
        rows = refs[i]
        size = rows.shape[0]
        start = pl.multiple_of(places[i] * size, size) if out.shape[0] > size else 0
        out[pl.ds(start, size), :] = dot(rows[:, :half], own[...]) + dot(rows[:, half:], other[...])


def project(pieces, weight, whole, places, chunks):
    own, other = weight
    (count, width), columns = pieces[0].shape, own.shape[1]
    size = 512 if columns % 512 == 0 else TILE
    spec = pl.BlockSpec((width // 2, size), lambda j, _: (0, j))
    rows = pl.BlockSpec((count, width), lambda j, _: (0, 0))
    number = len(pieces)
    if whole is None:
        held, out = [], pl.BlockSpec((count * chunks, size), lambda j, _: (0, j))
    else:
        held, out = [whole], pl.BlockSpec((count, size), lambda j, at: (at[0], j))
    return call(
        functools.partial(project_kernel, number),
        (columns // size,),
        [rows] * number + [spec, spec] + [pl.BlockSpec(memory_space=pl.ANY)] * len(held),
        out,
        jax.ShapeDtypeStruct((count * chunks, columns), f32),
        2 * number * count * width * columns,
        scalars=1,
        aliases={number + 3: 0} if held else None,
        moved=2 * width * columns + 4 * number * count * columns,
    )(jnp.stack(places), *pieces, own, other, *held)


def terms_kernel(count, paired, places, *refs):
    own, other, outs = refs[count], refs[count + 1], refs[count + 2 :]
    pairs, outs = outs[: count * paired], outs[count * paired :]

    def give(weight):
        sums = 0.0
        for i, rows in enumerate(refs[:count]):
            result = dot_nt(rows[...], weight[...])
            outs[i][...] = result.astype(outs[i].dtype)
            if paired:
                sums = sums + jnp.sum(result * pairs[i][...].astype(f32), axis=0, keepdims=True)
        if paired:
            outs[count][...] = sums

    pl.when(pl.program_id(0) == 0)(lambda: give(own))
    pl.when(pl.program_id(0) == 1)(lambda: give(other))


def terms(whole, weight, places, size, kinds, pairs):
    own, other = weight
    half, depth = own.shape
    tile = min(half, 1024 if depth <= 1024 else 512)
    steps = half // tile
    number = len(places)
    rows = [
        pl.BlockSpec((size, depth), lambda i, j, at, n=n: (at[n], 0)) for n in range(number)
    ]
    out = lambda height: pl.BlockSpec((height, tile), lambda i, j, _: (0, i * steps + j))
    paired = 1 if pairs else 0
    return call(
        functools.partial(terms_kernel, number, paired),
        (2, steps),
        rows
        + [
            pl.BlockSpec((tile, depth), lambda i, j, _: (jnp.where(i == 0, j, steps - 1), 0)),
            pl.BlockSpec((tile, depth), lambda i, j, _: (jnp.where(i == 0, 0, j), 0)),
        ]
        + [out(size)] * (number * paired),
        [out(size)] * number + [out(1)] * paired,
        [jax.ShapeDtypeStruct((size, 2 * half), kind) for kind in kinds]
        + [jax.ShapeDtypeStruct((1, 2 * half), f32)] * paired,
        4 * number * size * depth * half,
        scalars=1,
        moved=4 * depth * half + 8 * number * size * half,
    )(jnp.stack(places), *([whole] * number), own, other, *(pairs or []))


def scatter_ring(whole, weight, count, name, beside, pairs=None):
    own, size = lax.axis_index("tensor"), lax.axis_size("tensor")
    places = [(own - step) % size for step in range(1, size + 1)]
    pairs = pairs and pairs[1:] + pairs[:1]
    total, *first = terms(whole, weight, places[:1], count, [low], pairs and pairs[:1])
    late = tie(whole, total)
    rest = terms(late, weight, places[1:], count, [f32] * (size - 1), pairs and pairs[1:])
    more = first[0] + rest[-1] if pairs else None
    for step in range(1, size):
        came = shift(total, "tensor", 1, f"{name}_{step}")
        if step == 1:
            came = tie(came, (rest, more))
        came = beside(step, came, more)
        total = came.astype(f32) + rest[step - 1]
        if step < size - 1:
            total = total.astype(low)
    return total


def norm_kernel(values, added, gain, middle, out):
    rows = values[...].astype(f32) + added[...]
    middle[...] = rows
    out[...] = (layer_norm(rows)[0] * gain[...]).astype(low)


def norm_rows(values, added, gain):
    count, width = values.shape
    size = min(count, 128)
    rows = pl.BlockSpec((size, width), lambda i: (i, 0))
    return call(
        norm_kernel,
        (count // size,),
        [rows, rows, pl.BlockSpec((1, width), lambda i: (0, 0))],
        [rows, rows],
        [jax.ShapeDtypeStruct((count, width), f32), jax.ShapeDtypeStruct((count, width), low)],
        0,
        moved=count * width * 12,
    )(values, added, gain[None])


def norm_back_kernel(added, values, base, gain, grad, *refs):
    outs = refs[added:]
    given = grad[...]
    if added:
        given = given + refs[0][...].astype(f32)
    normed, scale = layer_norm(values[...].astype(f32))
    result = base[...].astype(f32) + norm_back(given * gain[...], normed, scale)
    outs[0][...] = result
    if len(outs) == 1:
        return
    term = jnp.sum(given * normed, axis=0, keepdims=True)

    @pl.when(pl.program_id(0) == 0)
    def _():
        outs[1][...] = term

    @pl.when(pl.program_id(0) != 0)
    def _():
        outs[1][...] += term

    outs[2][...] = result.astype(low)


def norm_back_rows(values, base, gain, grad, came=None):
    count, width = values.shape
    size = min(count, 128)
    rows = pl.BlockSpec((size, width), lambda i: (i, 0))
    line = pl.BlockSpec((1, width), lambda i: (0, 0))
    more = [] if came is None else [came]
    return call(
        functools.partial(norm_back_kernel, len(more)),
        (count // size,),
        [rows, rows, line, rows] + [rows] * len(more),
        [rows] + [line, rows] * len(more),
        [jax.ShapeDtypeStruct((count, width), f32)]
        + [jax.ShapeDtypeStruct((1, width), f32), jax.ShapeDtypeStruct((count, width), low)]
        * len(more),
        0,
        moved=count * width * 16,
    )(values, base, gain[None], grad, *more)


def place_masks(size):
    row = lax.broadcasted_iota(jnp.int32, (size, size), 0)
    column = lax.broadcasted_iota(jnp.int32, (size, size), 1)
    return row, column


def block_decay(powers, head, apart, base, row, column, after, before):
    kept = (after == before) & (after >= 0)
    if apart == 0:
        kept = kept & (column <= row)
        return jnp.where(kept, base, 0.0)
    return jnp.where(kept, base * powers[head, apart], 0.0)


def retain_kernel(powers, logs, pre, cosine, sine, after, before, mixed, kept, grouped, scale):
    head = pl.program_id(0)
    total = pre.shape[0]
    half = KD // 2
    cos, sin = cosine[...], sine[...]
    for first, factor in ((0, KD ** (-0.5)), (KD, 1.0)):
        a, b = pre[:, first : first + half], pre[:, first + half : first + KD]
        kept[:, first : first + half] = ((a * cos - b * sin) * factor).astype(low)
        kept[:, first + half : first + KD] = ((a * sin + b * cos) * factor).astype(low)
    kept[:, 2 * KD :] = pre[:, 2 * KD : 2 * KD + VD].astype(low)
    row, column = place_masks(TILE)
    base = jnp.exp((row - column).astype(f32) * logs[head])
    for i in range(total // TILE):
        rows = slice(i * TILE, (i + 1) * TILE)
        held = jnp.zeros((TILE, VD), f32)
        for j in range(i + 1):
            past = slice(j * TILE, (j + 1) * TILE)
            decay = block_decay(powers, head, i - j, base, row, column, after[rows, :], before[:, past])
            scores = dot_nt(kept[rows, :KD], kept[past, KD : 2 * KD])
            held = held + dot((decay * scores).astype(low), kept[past, 2 * KD :])
        normed, inverse = layer_norm(held, group_floor)
        grouped[rows, :] = normed
        scale[rows, :] = jnp.broadcast_to(inverse, (TILE, 128))
        gate = pre[rows, 2 * KD + VD :]
        mixed[rows, :] = (gate * jax.nn.sigmoid(gate) * normed).astype(low)


def retain(pre, consts, heads):
    total = pre.shape[0]
    powers, logs, cosine, sine, after, before = consts
    whole = lambda a: pl.BlockSpec(a.shape, lambda h: (0, 0))
    smem = pl.BlockSpec(memory_space=pltpu.SMEM)
    by_head = lambda width: pl.BlockSpec((total, width), lambda h: (0, h))
    shape = lambda width, kind: jax.ShapeDtypeStruct((total, heads * width), kind)
    return call(
        retain_kernel,
        (heads,),
        [smem, smem, by_head(2 * KD + 2 * VD), whole(cosine), whole(sine), whole(after), whole(before)],
        [by_head(VD), by_head(2 * KD + VD), by_head(VD), by_head(128)],
        [shape(VD, low), shape(2 * KD + VD, low), shape(VD, f32), shape(128, f32)],
        heads * total * total * (KD + VD) * 5 // 4,
        moved=heads * total * (1536 * 4 + 512 * 2 + 1024 * 2 + 512 * 4 + 512),
        exps=heads * total * 600,
    )(*consts[:2], pre, *consts[2:])


def retain_back_kernel(
    powers, logs, grad, gates, kept, grouped, scale, cosine, sine, after, before, out, grad_low, grad_q, grad_k, grad_v
):
    head = pl.program_id(0)
    total = kept.shape[0]
    half = KD // 2
    blocks = total // TILE
    for i in range(blocks):
        rows = slice(i * TILE, (i + 1) * TILE)
        gate, normed, given = gates[rows, :], grouped[rows, :], grad[rows, :]
        sigmoid = jax.nn.sigmoid(gate)
        out[rows, 2 * KD + VD :] = (
            given * normed * sigmoid * (1.0 + gate * (1.0 - sigmoid))
        ).astype(low)
        grad_low[rows, :] = norm_back(given * (gate * sigmoid), normed, scale[rows, :1]).astype(low)
    row, column = place_masks(TILE)
    base = jnp.exp((row - column).astype(f32) * logs[head])
    for i in range(blocks):
        rows = slice(i * TILE, (i + 1) * TILE)
        query, grad_rows = kept[rows, :KD], grad_low[rows, :]
        held = jnp.zeros((TILE, KD), f32)
        for j in range(i + 1):
            past = slice(j * TILE, (j + 1) * TILE)
            decay = block_decay(powers, head, i - j, base, row, column, after[rows, :], before[:, past])
            key, value = kept[past, KD : 2 * KD], kept[past, 2 * KD :]
            weights = (decay * dot_nt(query, key)).astype(low)
            grad_scores = (dot_nt(grad_rows, value) * decay).astype(low)
            held = held + dot(grad_scores, key)
            key_term, value_term = dot_tn(grad_scores, query), dot_tn(weights, grad_rows)
            if i == j:
                grad_k[past, :], grad_v[past, :] = key_term, value_term
            else:
                grad_k[past, :] += key_term
                grad_v[past, :] += value_term
        grad_q[rows, :] = held
    cos, sin = cosine[...], sine[...]
    for first, source, factor in ((0, grad_q, KD ** (-0.5)), (KD, grad_k, 1.0)):
        a, b = source[:, :half] * factor, source[:, half:] * factor
        out[:, first : first + half] = (a * cos + b * sin).astype(low)
        out[:, first + half : first + KD] = (b * cos - a * sin).astype(low)
    out[:, 2 * KD : 2 * KD + VD] = grad_v[...].astype(low)


def retain_back(grad, pre, kept, grouped, scale, consts, heads):
    total = pre.shape[0]
    powers, logs, cosine, sine, after, before = consts
    whole = lambda a: pl.BlockSpec(a.shape, lambda h: (0, 0))
    smem = pl.BlockSpec(memory_space=pltpu.SMEM)
    by_head = lambda width: pl.BlockSpec((total, width), lambda h: (0, h))
    return call(
        retain_back_kernel,
        (heads,),
        [smem, smem, by_head(VD), pl.BlockSpec((total, VD), lambda h: (0, 3 * h + 2))]
        + [by_head(2 * KD + VD), by_head(VD), by_head(128)]
        + [whole(cosine), whole(sine), whole(after), whole(before)],
        by_head(2 * KD + 2 * VD),
        jax.ShapeDtypeStruct((total, heads * (2 * KD + 2 * VD)), low),
        heads * total * total * (3 * KD + 2 * VD) * 5 // 4,
        scratch=[
            pltpu.VMEM((total, VD), low),
            pltpu.VMEM((total, KD), f32),
            pltpu.VMEM((total, KD), f32),
            pltpu.VMEM((total, VD), f32),
        ],
        moved=heads * total * (512 * 4 * 3 + 1024 * 2 + 1536 * 2),
        exps=heads * total * 600,
    )(*consts[:2], grad, pre, kept, grouped, scale, *consts[2:])


def feed_kernel(held, rows, cot, *refs):
    weights = refs[:6]
    hidden, grad_act, grad_lin, total = refs[6 + held :]
    half = rows.shape[1] // 2
    up, gate, down = ((weights[2 * i][...], weights[2 * i + 1][...]) for i in range(3))

    def into(values, weight):
        return dot(values[:, :half], weight[0]) + dot(values[:, half:], weight[1])

    act, lin, grad_hidden = into(rows, up), into(rows, gate), into(cot, down)
    curve = jnp.tanh(gelu_slope * (act + gelu_cubic * act * act * act))
    gelu = 0.5 * act * (1.0 + curve)
    slope = 0.5 * (1.0 + curve) + (0.5 * gelu_slope) * act * (1.0 - curve * curve) * (
        1.0 + (3.0 * gelu_cubic) * act * act
    )
    hidden[...] = (gelu * lin).astype(low)
    act_low = (grad_hidden * lin * slope).astype(low)
    lin_low = (grad_hidden * gelu).astype(low)
    grad_act[...] = act_low
    grad_lin[...] = lin_low

    for side in range(2):
        columns = slice(side * half, (side + 1) * half)
        add = dot_nt(act_low, up[side]) + dot_nt(lin_low, gate[side])

        @pl.when(pl.program_id(0) == 0)
        def _(add=add, columns=columns):
            total[:, columns] = add + refs[6][:, columns] if held else add

        @pl.when(pl.program_id(0) != 0)
        def _(add=add, columns=columns):
            total[:, columns] += add


def feed(rows, cot, weight, total):
    own, other = weight
    count, width = rows.shape
    columns = own.shape[1] // 3
    size = min(TILE, columns)
    steps = columns // size
    full = pl.BlockSpec((count, width), lambda t: (0, 0))
    tile = pl.BlockSpec((count, size), lambda t: (0, t))
    weights = [
        pl.BlockSpec((width // 2, size), lambda t, part=part: (0, part * steps + t))
        for part in range(3)
        for _ in range(2)
    ]
    shape = jax.ShapeDtypeStruct((count, columns), low)
    held = [] if total is None else [total]
    return call(
        functools.partial(feed_kernel, len(held)),
        (steps,),
        [full, full] + weights + [full] * len(held),
        [tile, tile, tile, full],
        [shape, shape, shape, jax.ShapeDtypeStruct((count, width), f32)],
        10 * count * width * columns,
        moved=6 * width * columns + 8 * count * width + 6 * count * columns,
        exps=count * columns,
    )(rows, cot, *([own, other] * 3), *held)


def gradient_kernel(plan, added, places, *refs):
    number = sum(pieces for pieces, _, _ in plan)
    lefts, rights = refs[:number], refs[number : number + sum(len(r) for _, r, _ in plan)]
    rest = refs[number + len(rights) :]
    came, outs, turned = rest[:added], rest[added:-1], rest[-1]
    step = pl.program_id(0)
    first = left_at = right_at = 0
    for pieces, lengths, size in plan:

        @pl.when(step == first)
        def _(left_at=left_at, pieces=pieces, size=size):
            for i in range(left_at, left_at + pieces):
                start = pl.multiple_of(places[i] * size, size) if pieces > 1 else 0
                turned[:, pl.ds(start, size)] = lefts[i][...].T

        for length in lengths:

            @pl.when((step >= first) & (step < first + length))
            def _(right=rights[right_at]):
                result = dot(turned[...], right[...])
                if added:
                    result = result + came[0][...].astype(f32)
                height = result.shape[0] // len(outs)
                for i, out in enumerate(outs):
                    out[...] = result[i * height : (i + 1) * height].astype(low)

            first, right_at = first + length, right_at + 1
        left_at += pieces


def weight_gradient(groups, side, came=None):
    width = groups[0][0][0].shape[1]
    half = width // 2
    count = groups[0][0][0].shape[0] * len(groups[0][0])
    columns = sum(right.shape[1] for _, _, rights in groups for right in rights)
    size = min(512, min(right.shape[1] for _, _, rights in groups for right in rights))
    plan, lefts, rights, left_specs, right_specs, places, first = [], [], [], [], [], [], 0
    for pieces, at, given in groups:
        plan.append((len(pieces), [right.shape[1] // size for right in given], pieces[0].shape[0]))
        lefts += pieces
        places += at
        left_specs += [pl.BlockSpec((pieces[0].shape[0], half), lambda t, _: (0, side))] * len(pieces)
        for right in given:
            steps = right.shape[1] // size
            right_specs.append(
                pl.BlockSpec(
                    (count, size),
                    lambda t, _, first=first, steps=steps: (0, jnp.clip(t - first, 0, steps - 1)),
                )
            )
            rights.append(right)
            first += steps
    parts = 1 if came is None else 4
    tile = lambda height: pl.BlockSpec((height, size), lambda t, _: (0, t))
    more = [] if came is None else [came]
    outs = call(
        functools.partial(gradient_kernel, plan, len(more)),
        (columns // size,),
        left_specs + right_specs + [tile(half)] * len(more),
        [tile(half // parts)] * parts,
        [jax.ShapeDtypeStruct((half // parts, columns), low)] * parts,
        2 * half * count * columns,
        scratch=[pltpu.VMEM((half, count), low)],
        scalars=1,
        moved=2 * (half * columns * (1 + len(more)) + count * (half + columns)),
    )(jnp.stack(places), *lefts, *rights, *more)
    return outs[0] if came is None else [outs[:2], outs[2:]]


def shards(
    inputs,
    gain_attn,
    w_query,
    w_key,
    w_value,
    w_gate,
    w_out,
    gain_mlp,
    w_act,
    w_lin,
    w_down,
    cotangent,
    lengths,
    offsets,
):
    rows, width = inputs.shape
    dp_size, tensor_size = lax.axis_size("dp"), lax.axis_size("tensor")
    dp_own, tensor_own = lax.axis_index("dp"), lax.axis_index("tensor")
    total = rows * tensor_size
    heads = w_query.shape[1] // KD
    hidden_cols = w_act.shape[1]
    half = width // 2

    order = feature_order(dp_size)
    taken = jnp.array([k for k, _ in order], jnp.int32)
    parts = jnp.array([i for _, i in order], jnp.int32)
    table = (taken ^ dp_own) * 2 + parts
    place = {pair: i for i, pair in enumerate(order)}
    places = jnp.array([[place[k, i] for i in range(2)] for k in range(dp_size)], jnp.int32)
    back = places[jnp.arange(dp_size, dtype=jnp.int32) ^ dp_own].reshape(-1)

    gains = jnp.concatenate([gain_attn.reshape(2, -1), gain_mlp.reshape(2, -1)], axis=1)
    gains = gather_rest(gather_start(gains), 0, "gains")
    gains = jnp.concatenate([gains, swap(gains, "dp", 1, "gains")], axis=0).astype(f32)
    fine = gains.shape[1] // 2
    gain_one, gain_two = gains[:, :fine].reshape(-1), gains[:, fine:].reshape(-1)
    cot_came = swap(cotangent, "tensor", 1, "rows_cot")
    x_low = reorder(inputs, table)
    cot = reorder(cotangent, table)
    h_attn = (layer_norm(x_low.astype(f32))[0] * gain_one).astype(low)

    def per_head(query, key, value, gate):
        columns = []
        for h in range(heads):
            columns += [a[:, h * KD : (h + 1) * KD] for a in (query, key)]
            columns += [a[:, h * VD : (h + 1) * VD] for a in (value, gate)]
        return jnp.concatenate(columns, axis=1)

    block_in = per_head(w_query, w_key, w_value, w_gate)
    block_out = w_out.T
    block_feed = jnp.concatenate([w_act, w_lin, w_down.T], axis=1)
    pair_blocks = range(0, tensor_size, 2)

    head_first = tensor_own * heads
    head_numbers = (head_first + jnp.arange(heads, dtype=jnp.int32)).astype(f32)
    log_decay = jnp.log(1.0 - jnp.exp2(-5.0 - head_numbers))
    segment, position = sequence_layout(lengths[0], offsets[0], total)
    cosine, sine = rotation(position, KD)
    powers = jnp.exp(
        jnp.arange(total // TILE, dtype=f32)[None, :] * TILE * log_decay[:, None]
    )
    consts = (powers, log_decay, cosine, sine, segment[:, None], segment[None, :])
    ring_places = [(tensor_own - step) % tensor_size for step in range(tensor_size)]

    w_in = gather_step(gather_start(tie(block_in, gains)), 0, "w_in")
    w_in_other = pre = wo = None
    held = [h_attn]

    def beside_attn(step, came):
        nonlocal w_in, w_in_other, cot_came, pre, wo, consts, block_feed, block_out
        if step == 1:
            came, w_in, cot_came, block_feed, block_out = sync(
                came, w_in, cot_came, block_feed, block_out
            )
            w_in = gather_rest(w_in, 1, "w_in")
        if step == 2:
            came, w_in, consts = sync(came, w_in, consts)
            w_in_other = swap(w_in, "dp", 1, "w_in")
            wo = gather_step(gather_start(tie(block_out, w_in)), 0, "w_out")
        if step == tensor_size - 1:
            pre = project(held, (w_in, w_in_other), None, ring_places[:step], tensor_size)
            came, pre, wo = sync(came, pre, wo)
        held.append(came)
        return came

    h_pieces = gather_ring(h_attn, "rows_attn", beside_attn)
    rows_here = h_pieces[-1]
    w_in = (w_in, w_in_other)
    cot_pair = jnp.concatenate([cot, reorder(cot_came, table)], axis=0)

    block_feed, wo = tie((block_feed, wo), rows_here)
    feed_parts = gather_start(block_feed)
    far_feeds = {k: [swap(feed_parts[0], "tensor", k, "w_feed_far")] for k in pair_blocks[1:]}
    near_feed = gather_step(feed_parts, 0, "w_feed_near")
    wo = gather_rest(wo, 1, "w_out")
    pre = project([rows_here], w_in, pre, ring_places[-1:], tensor_size)
    pre, wo = sync(pre, wo)
    wo = (wo, swap(wo, "dp", 1, "w_out"))
    mixed, kept, grouped, scale = retain(pre, consts, heads)
    mixed, near_feed, far_feeds, late_part, cot_pair = sync(
        mixed, near_feed, far_feeds, feed_parts[1], cot_pair
    )
    near_feed = gather_rest(near_feed, 1, "w_feed_near")
    far_feeds = {
        k: v + [swap(late_part, "tensor", k, "w_feed_far")] for k, v in far_feeds.items()
    }

    def beside_out(step, came, _):
        nonlocal near_feed, far_feeds
        if step == 1:
            came, far_feeds = sync(came, far_feeds)
            far_feeds = {k: gather_step(v, 0, "w_feed_far") for k, v in far_feeds.items()}
        if step == 2:
            came, near_feed, far_feeds = sync(came, near_feed, far_feeds)
            near_feed = (near_feed, swap(near_feed, "dp", 1, "w_feed_near"))
            far_feeds = {k: gather_rest(v, 1, "w_feed_far") for k, v in far_feeds.items()}
        return came

    attended = scatter_ring(mixed, wo, rows, "sum_attn", beside_out)

    middle, h_mlp = norm_rows(x_low, attended, gain_two)
    h_came = swap(h_mlp, "tensor", 1, "rows_mlp")
    h_came, far_feeds = sync(h_came, far_feeds)
    far_feeds = {k: (v, swap(v, "dp", 1, "w_feed_far")) for k, v in far_feeds.items()}
    feeds = [near_feed] + [far_feeds[k] for k in pair_blocks[1:]]
    h_pair = jnp.concatenate([h_mlp, h_came], axis=0)
    results, grad_h = [], None
    for weight in feeds:
        *result, grad_h = feed(h_pair, cot_pair, weight, grad_h)
        results.append(result)
    grad_send = grad_h[rows:].astype(low)
    grad_came = swap(grad_send, "tensor", 1, "sum_grad_mlp")

    results, late_rows, late_cot = tie((results, h_pair, cot_pair), grad_send)
    origin = jnp.zeros((), jnp.int32)

    def feed_groups(result):
        hidden, grad_act, grad_lin = result
        return [([late_rows], [origin], [grad_act, grad_lin]), ([late_cot], [origin], [hidden])]

    far = {k: weight_gradient(feed_groups(results[k // 2]), 1) for k in pair_blocks[1:]}
    near_other = weight_gradient(feed_groups(results[0]), 1)
    grad_came, far, near_other = sync(grad_came, far, near_other)
    far_came = {k: swap(other, "dp", 1, "grad_feed_far") for k, other in far.items()}
    near_came = swap(near_other, "dp", 1, "grad_feed_near")
    grad_middle, gain_two_term, grad_mid_low = norm_back_rows(
        middle, cot, gain_two, grad_h[:rows], grad_came
    )

    grad_mixed = out_own = out_send = None
    mid_pieces = [grad_mid_low]

    def beside_mid(step, came):
        nonlocal far, near_came, grad_mixed, out_own, out_send
        if step == 1:
            late = tie(results, grad_mid_low)
            far = {
                k: weight_gradient(feed_groups(late[k // 2]), 0, far_came[k])
                for k in pair_blocks[1:]
            }
            came, far = sync(came, far)
            far = {k: scatter_step(v, 0, "grad_feed_far") for k, v in far.items()}
        if step == 2:
            late, weights = tie((results, feeds), mid_pieces[1])
            sums = [
                jnp.concatenate(
                    [dot_nt(result[0], weight[side][:, 2 * hidden_cols :]) for side in range(2)],
                    axis=1,
                )
                for result, weight in zip(late, weights)
            ]
            out_own, out_send = sum(sums)[:rows], sum(sums)[rows:].astype(low)
            came, out_own, out_send = sync(came, out_own, out_send)
        if step == tensor_size - 1:
            late, late_result = tie((mid_pieces, results[0]), mid_pieces[-1])
            near_came = weight_gradient(feed_groups(late_result), 0, near_came)
            grad_mixed = project(late, wo, None, ring_places[:step], tensor_size)
            came, far, grad_mixed, near_came = sync(came, far, grad_mixed, near_came)
        mid_pieces.append(came)
        return came

    mid_pieces = gather_ring(grad_mid_low, "rows_grad_mid", beside_mid)
    out_came = swap(tie(out_send, mid_pieces[-1]), "tensor", 1, "sum_out")
    far = {k: scatter_rest(v, 1, "grad_feed_far") for k, v in far.items()}

    grad_mixed = project(mid_pieces[-1:], wo, grad_mixed, ring_places[-1:], tensor_size)
    grad_in = retain_back(grad_mixed, pre, kept, grouped, scale, consts, heads)

    grad_in, out_came, far, near = sync(grad_in, out_came, far, near_came)
    far_sent = {k: [part[: part.shape[0] // 2], part[part.shape[0] // 2 :]] for k, part in far.items()}
    far = {k: [swap(part[0], "tensor", k, "grad_feed_far")] for k, part in far_sent.items()}
    near = scatter_step(near, 0, "grad_feed_near")
    in_other = out_other = more = None
    grads_in = grads_out = gain_sum = None

    def gain_total(gain_one_term):
        gain_terms = jnp.concatenate(
            [gain_one_term.reshape(-1, fine), gain_two_term.reshape(-1, fine)], axis=1
        )
        size = gain_terms.shape[0] // 2
        gain_sum = gain_terms[:size] + swap(gain_terms[size:], "dp", 1, "gains")
        sums = [gain_sum[: size // 2], gain_sum[size // 2 :]]
        for bits in reversed(dp_bits(dp_size)):
            size = sums[0].shape[0] // 2
            sums = [
                part[:size] + swap(part[size:], "dp", bit, "gains") for part, bit in zip(sums, bits)
            ]
        gain_sum = jnp.concatenate(sums, axis=0)
        for b in range(tensor_size.bit_length() - 1):
            gain_sum = gain_sum + swap(gain_sum, "tensor", 1 << b, "gains")
        return gain_sum

    def beside_sum(step, came, terms_sum):
        nonlocal near, far, far_sent, in_other, out_other, more, grads_in, grads_out, gain_sum
        if step == 1:
            late, late_mixed = tie((grad_in, mixed), terms_sum)
            in_other = weight_gradient([(h_pieces, ring_places, [late])], 1)
            out_other = weight_gradient([(mid_pieces, ring_places, [late_mixed])], 1)
            came, more, in_other, out_other, far, far_sent, near = sync(
                came, terms_sum, in_other, out_other, far, far_sent, near
            )
            in_other = swap(in_other, "dp", 1, "grad_w_in")
            out_other = swap(out_other, "dp", 1, "grad_w_out")
            far = {
                k: v + [swap(far_sent[k][1], "tensor", k, "grad_feed_far")] for k, v in far.items()
            }
            near = scatter_rest(near, 1, "grad_feed_near")
        if step == 2:
            grads_in = weight_gradient([(h_pieces, ring_places, [grad_in])], 0, in_other)
            grads_out = weight_gradient([(mid_pieces, ring_places, [mixed])], 0, out_other)
            came, grads_in, grads_out, far, near = sync(came, grads_in, grads_out, far, near)
            grads_in = scatter_step(grads_in, 0, "grad_w_in")
            gain_sum = gain_total(more / gain_one)
        if step == tensor_size - 1:
            came, gain_sum = sync(came, gain_sum)
        return came

    grad_hattn = scatter_ring(grad_in, w_in, rows, "sum_grad_attn", beside_sum, h_pieces)
    grad_wo_own = scatter_rest(grads_out, 0, "grad_w_out").astype(f32)
    grad_in_own = scatter_rest(grads_in, 1, "grad_w_in").astype(f32)
    far = [jnp.concatenate(part, axis=0).astype(f32) for part in far.values()]
    grad_feed = near.astype(f32) + sum(far)
    outputs = middle + out_own + out_came.astype(f32)
    (grad_inputs,) = norm_back_rows(x_low, grad_middle, gain_one, grad_hattn)

    def heads_back(first, size):
        stride = 2 * KD + 2 * VD
        return jnp.concatenate(
            [grad_in_own[:, h * stride + first : h * stride + first + size] for h in range(heads)],
            axis=1,
        )

    return (
        reorder(outputs.astype(low), back),
        reorder(grad_inputs, back),
        gain_sum[:, :fine].reshape(-1),
        heads_back(0, KD),
        heads_back(KD, KD),
        heads_back(2 * KD, VD),
        heads_back(2 * KD + VD, VD),
        grad_wo_own.T,
        gain_sum[:, fine:].reshape(-1),
        grad_feed[:, :hidden_cols],
        grad_feed[:, hidden_cols : 2 * hidden_cols],
        grad_feed[:, 2 * hidden_cols :].T,
    )


def solution(mesh):
    return jax.shard_map(
        shards,
        mesh=mesh,
        in_specs=(
            P(("dp", "tensor"), None),
            P("dp"),
            P("dp", "tensor"),
            P("dp", "tensor"),
            P("dp", "tensor"),
            P("dp", "tensor"),
            P("tensor", "dp"),
            P("dp"),
            P("dp", "tensor"),
            P("dp", "tensor"),
            P("tensor", "dp"),
            P(("dp", "tensor"), None),
            P("dp", None),
            P("dp", None),
        ),
        out_specs=(
            P(("dp", "tensor"), None),
            P(("dp", "tensor"), None),
            P("dp"),
            P("dp", "tensor"),
            P("dp", "tensor"),
            P("dp", "tensor"),
            P("dp", "tensor"),
            P("tensor", "dp"),
            P("dp"),
            P("dp", "tensor"),
            P("dp", "tensor"),
            P("tensor", "dp"),
        ),
        check_vma=False,
    )
```

time: 1520 us -> 780 us (0.51)
  waiting for transfers between devices: 1040 us -> 337 us
  Pallas kernels: 0 us -> 240 us
  matrix products: 253 us -> 14.3 us
  starting transfers between devices: 1.75 us -> 58.7 us
  blocking collectives: 49.2 us -> 0 us
  local copies, waits for them, and re-layouts: 61.6 us -> 35.6 us
    reduce_scatter x12 -> x0, waiting for transfers between devices: 587 us -> none  [the longest x1 135 us: shards(): lax.psum_scatter(jnp.dot(mixed, wo_full, preferred_element_type=jnp.float...]
    all_gather x12 -> x0, waiting for transfers between devices: 443 us -> none  [the longest x1 82.9 us: shards(): h_group_two = lax.all_gather(h_mlp, 'tensor', axis=0, tiled=True)]
    ppermute x0 -> x72, waiting for transfers between devices: none -> 337 us  [the longest x60 261 us: swap(): return lax.ppermute(values, axis, [(i, i ^ bits) for i in range(size)])]
    pallas_call x0 -> x28, Pallas kernels: none -> 240 us  [the longest x8 75 us: weight_gradient(): call(functools.partial(gradient_kernel, plan, len(more)), (columns // siz...]
    dot_general x58 -> x4, matrix products: 253 us -> 14.3 us  [dot_nt(): lax.dot_general(left, right, (((1,), (1,)), ((), ())), preferred_element_...]
    ppermute x0 -> x72, starting transfers between devices: none -> 58.7 us  [the longest x60 54.4 us: swap(): return lax.ppermute(values, axis, [(i, i ^ bits) for i in range(size)])]
    concatenate x0 -> x24, other arithmetic: none -> 33.3 us  [the longest x5 15.5 us: gather_rest(): return jnp.concatenate(parts, axis=0)]
    all_gather x2 -> x0, blocking collectives: 19.2 us -> none  [the longest x1 10.3 us: shards(): lax.all_gather(gain_attn, 'dp', axis=0, tiled=True)]
  transfers between devices with their start and end apart: 24 -> 72, of which waited for: 20 -> 41; matrix products, arithmetic and copies ran while one was open for 22% -> 14% of each run, Pallas kernels for 0% -> 28%
where the time goes in v1:
time: 780 us; the launch traced here: 764 us
  waiting for transfers between devices  337 us (43%)
  Pallas kernels  240 us (31%)
  other arithmetic  76.4 us (10%)
  starting transfers between devices  58.7 us (8%)
  local copies, waits for them, and re-layouts  35.6 us (5%)
  matrix products  14.3 us (2%)
    ppermute x60, waiting for transfers between devices, swap(): return lax.ppermute(values, axis, [(i, i ^ bits) for i in range(size)])  261 us
    ppermute x12, waiting for transfers between devices, shift(): lax.ppermute(values, axis, [(i, (i + step) % size) for i in range(size)])  76.1 us
    pallas_call x8, Pallas kernels, weight_gradient(): call(functools.partial(gradient_kernel, plan, len(more)), (columns // siz...  75 us
    ppermute x60, starting transfers between devices, swap(): return lax.ppermute(values, axis, [(i, i ^ bits) for i in range(size)])  54.4 us
    pallas_call x2, Pallas kernels, feed(): call(functools.partial(feed_kernel, len(held)), (steps,), [full, full] +...  49.8 us
    pallas_call x4, Pallas kernels, terms(): call(functools.partial(terms_kernel, number, paired), (2, steps), rows +...  38.2 us
    pallas_call x4, Pallas kernels, project(): call(functools.partial(project_kernel, number), (columns // size,), [rows...  36.3 us
    unnamed x146, local copies, waits for them, and re-layouts  19.8 us
  transfers between devices with their start and end apart: 72, of which 41 were waited for; matrix products, arithmetic and copies ran while one was open for 14% of the time, Pallas kernels for 28%

profile of v1, /device:TPU:0, one launch (start us, length us, event | category | flops | bytes accessed | tf_op | source)
XLA Modules:
  0.0 764.1 jit_solution(17773839989406489474)
XLA Ops:
  28.8 15.7 %collective-permute-done.6 = bf16[128,3072]{1,0:T(8,128)(2,1)S(1)} collective-permute-done((bf16[128,3072]{1,0:T(8,128)(2,1)S(1)}, bf16[128,3072]{1,0:T(8,128)(2,1)S(1)}, u32[]{:S(2)}, u32[]{:S(2)}) %collective-permute-start.6) | collective-permute-done | bytes 786464 | tf_op jit(solution)/shard_map/w_in_dp2/ppermute | solution.py:70
  44.9 10.1 %collective-permute-done.5.refs_1_.refs_3_ = bf16[256,2048]{1,0:T(8,128)(2,1)S(1)} collective-permute-done((bf16[256,2048]{1,0:T(8,128)(2,1)S(1)}, bf16[256,2048]{1,0:T(8,128)(2,1)S(1)}, u32[]{:S(2)}, u32[]{:S(2)}) %collective-permute-start.5) | collective-permute-done | bytes 1048608 | tf_op jit(solution)/shard_map/rows_attn_1/ppermute | solution.py:76
  59.3 31.0 %collective-permute-done.10 = bf16[256,3072]{1,0:T(8,128)(2,1)S(1)} collective-permute-done((bf16[256,3072]{1,0:T(8,128)(2,1)S(1)}, bf16[256,3072]{1,0:T(8,128)(2,1)S(1)}, u32[]{:S(2)}, u32[]{:S(2)}) %collective-permute-start.10) | collective-permute-done | bytes 1572896 | tf_op jit(solution)/shard_map/w_in_dp4/ppermute | solution.py:70
  107.3 15.8 %shard_map.257.refs_3_ = f32[1024,3072]{1,0:T(8,128)} custom-call(s32[3]{0:T(128)S(1)} %pad_add_fusion.places, bf16[256,2048]{1,0:T(8,128)(2,1)S(1)} %fusion.4.refs_0_.refs_7_, bf16[256,2048]{1,0:T(8,128)(2,1)S(1)} %copy-done.7, bf16[256,2048]{1,0:T(8,128)(2,1)} %collective-permute-done.9.refs_2_.refs_5_, ...), custom_call_target="tpu_custom_call" | custom-call | tf_op jit(solution)/shard_map/pallas_call | solution.py:219
  125.3 9.2 %shard_map.258.pre.gates = f32[1024,3072]{1,0:T(8,128)} custom-call(s32[1]{0:T(128)} %bitcast.11.places, bf16[256,2048]{1,0:T(8,128)(2,1)S(1)} %collective-permute-done.12.refs_0_.refs_6_.refs_3_, bf16[1024,3072]{1,0:T(8,128)(2,1)} %pad_maximum_fusion.refs_3_.refs_1_, ...), custom_call_target="tpu_custom_call", output_to_operand_aliasing={{}: (4, {})} | custom-call | tf_op jit(solution)/shard_map/pallas_call | solution.py:219
  148.2 10.4 %shard_map.259 = (bf16[1024,1024]{1,0:T(8,128)(2,1)S(1)}, bf16[1024,2048]{1,0:T(8,128)(2,1)}, f32[1024,1024]{1,0:T(8,128)}, f32[1024,256]{1,0:T(8,128)S(1)}) custom-call(f32[2,4]{1,0:T(2,128)S(1)} %multiply_exponential_fusion.powers, f32[2]{0:T(128)S(1)} %subtract_log_fusion.logs, f32[1024,3072]{1,0:T(8,128)} %shard_map.258.pre.gates, ...), custom_call_target="tpu_custom_call" | custom-call | tf_op jit(solution)/shard_map/pallas_call | solution.py:409
  167.1 15.2 %collective-permute-done.20 = bf16[128,3072]{1,0:T(8,128)(2,1)} collective-permute-done((bf16[128,3072]{1,0:T(8,128)(2,1)}, bf16[128,3072]{1,0:T(8,128)(2,1)}, u32[]{:S(2)}, u32[]{:S(2)}) %collective-permute-start.20) | collective-permute-done | bytes 786464 | tf_op jit(solution)/shard_map/w_feed_far_tensor2/ppermute | solution.py:70
  192.4 8.2 %shard_map.263 = (f32[256,2048]{1,0:T(8,128)S(1)}, f32[256,2048]{1,0:T(8,128)S(1)}, f32[256,2048]{1,0:T(8,128)}) custom-call(s32[3]{0:T(128)S(1)} %pad_add_fusion.1.places, bf16[1024,1024]{1,0:T(8,128)(2,1)} %copy-done.1, bf16[1024,1024]{1,0:T(8,128)(2,1)} %copy-done.1, bf16[1024,1024]{1,0:T(8,128)(2,1)} %copy-done.1, ...), custom_call_target="tpu_custom_call" | custom-call | tf_op jit(solution)/shard_map/pallas_call | solution.py:261
  200.6 14.9 %collective-permute-done.22 = bf16[256,2048]{1,0:T(8,128)(2,1)} collective-permute-done((bf16[256,2048]{1,0:T(8,128)(2,1)}, bf16[256,2048]{1,0:T(8,128)(2,1)}, u32[]{:S(2)}, u32[]{:S(2)}) %collective-permute-start.22) | collective-permute-done | bytes 1048608 | tf_op jit(solution)/shard_map/sum_attn_1/ppermute | solution.py:76
  215.4 32.0 %collective-permute-done.23 = bf16[128,3072]{1,0:T(8,128)(2,1)} collective-permute-done((bf16[128,3072]{1,0:T(8,128)(2,1)S(1)}, bf16[128,3072]{1,0:T(8,128)(2,1)}, u32[]{:S(2)}, u32[]{:S(2)}) %collective-permute-start.23) | collective-permute-done | bytes 786464 | tf_op jit(solution)/shard_map/w_feed_far_tensor2/ppermute | solution.py:70
  258.5 8.7 %collective-permute-done.27 = bf16[128,3072]{1,0:T(8,128)(2,1)S(1)} collective-permute-done((bf16[128,3072]{1,0:T(8,128)(2,1)}, bf16[128,3072]{1,0:T(8,128)(2,1)S(1)}, u32[]{:S(2)}, u32[]{:S(2)}) %collective-permute-start.27) | collective-permute-done | bytes 786464 | tf_op jit(solution)/shard_map/w_feed_far_dp2/ppermute | solution.py:70
  279.9 24.2 %collective-permute-done.29 = bf16[256,2048]{1,0:T(8,128)(2,1)S(1)} collective-permute-done((bf16[256,2048]{1,0:T(8,128)(2,1)S(1)}, bf16[256,2048]{1,0:T(8,128)(2,1)S(1)}, u32[]{:S(2)}, u32[]{:S(2)}) %collective-permute-start.29) | collective-permute-done | bytes 1048608 | tf_op jit(solution)/shard_map/sum_attn_3/ppermute | solution.py:76
  317.0 13.4 %collective-permute-done.30 = bf16[256,2048]{1,0:T(8,128)(2,1)S(1)} collective-permute-done((bf16[256,2048]{1,0:T(8,128)(2,1)S(1)}, bf16[256,2048]{1,0:T(8,128)(2,1)S(1)}, u32[]{:S(2)}, u32[]{:S(2)}) %collective-permute-start.30) | collective-permute-done | bytes 1048608 | tf_op jit(solution)/shard_map/rows_mlp_tensor1/ppermute | solution.py:70
  330.6 24.7 %shard_map.265 = (bf16[512,1024]{1,0:T(8,128)(2,1)S(1)}, bf16[512,1024]{1,0:T(8,128)(2,1)S(1)}, bf16[512,1024]{1,0:T(8,128)(2,1)S(1)}, f32[512,2048]{1,0:T(8,128)}) custom-call(bf16[512,2048]{1,0:T(8,128)(2,1)S(1)} %constant_dynamic-update-slice_fusion.rows.refs_0_, bf16[512,2048]{1,0:T(8,128)(2,1)} %pad_maximum_fusion.4.cot.refs_1_, ...), custom_call_target="tpu_custom_call" | custom-call | tf_op jit(solution)/shard_map/pallas_call | solution.py:539
  355.4 25.0 %shard_map.266 = (bf16[512,1024]{1,0:T(8,128)(2,1)S(1)}, bf16[512,1024]{1,0:T(8,128)(2,1)S(1)}, bf16[512,1024]{1,0:T(8,128)(2,1)S(1)}, f32[512,2048]{1,0:T(8,128)}) custom-call(bf16[512,2048]{1,0:T(8,128)(2,1)S(1)} %constant_dynamic-update-slice_fusion.rows.refs_0_, bf16[512,2048]{1,0:T(8,128)(2,1)} %pad_maximum_fusion.4.cot.refs_1_, ...), custom_call_target="tpu_custom_call" | custom-call | tf_op jit(solution)/shard_map/pallas_call | solution.py:539
  382.5 8.8 %shard_map.267 = bf16[1024,3072]{1,0:T(8,128)(2,1)} custom-call(s32[2]{0:T(128)S(1)} %broadcast_10_places.2.places, bf16[512,2048]{1,0:T(8,128)(2,1)S(1)} %constant_dynamic-update-slice_fusion.rows.refs_0_, bf16[512,2048]{1,0:T(8,128)(2,1)} %pad_maximum_fusion.4.cot.refs_1_, bf16[512,1024]{1,0:T(8,128)(2,1)S(1)} %get-tuple-element.314.refs_2_, ...), custom_call_target="tpu_custom_call" | custom-call | tf_op jit(solution)/shard_map/pallas_call | solution.py:606
  391.3 8.9 %shard_map.268 = bf16[1024,3072]{1,0:T(8,128)(2,1)} custom-call(s32[2]{0:T(128)S(1)} %broadcast_10_places.2.places, bf16[512,2048]{1,0:T(8,128)(2,1)S(1)} %constant_dynamic-update-slice_fusion.rows.refs_0_, bf16[512,2048]{1,0:T(8,128)(2,1)} %pad_maximum_fusion.4.cot.refs_1_, bf16[512,1024]{1,0:T(8,128)(2,1)S(1)} %get-tuple-element.342.refs_2_, ...), custom_call_target="tpu_custom_call" | custom-call | tf_op jit(solution)/shard_map/pallas_call | solution.py:606
  418.3 10.3 %shard_map.270 = (bf16[256,3072]{1,0:T(8,128)(2,1)S(1)}, bf16[256,3072]{1,0:T(8,128)(2,1)}, bf16[256,3072]{1,0:T(8,128)(2,1)}, bf16[256,3072]{1,0:T(8,128)(2,1)}) custom-call(s32[2]{0:T(128)S(1)} %broadcast_10_places.2.places, bf16[512,2048]{1,0:T(8,128)(2,1)} %copy-done, bf16[512,2048]{1,0:T(8,128)(2,1)} %pad_maximum_fusion.4.cot.refs_1_, ...), custom_call_target="tpu_custom_call" | custom-call | tf_op jit(solution)/shard_map/pallas_call | solution.py:606
  429.7 13.4 %collective-permute-done.36.refs_1_ = bf16[256,2048]{1,0:T(8,128)(2,1)S(1)} collective-permute-done((bf16[256,2048]{1,0:T(8,128)(2,1)S(1)}, bf16[256,2048]{1,0:T(8,128)(2,1)S(1)}, u32[]{:S(2)}, u32[]{:S(2)}) %collective-permute-start.36) | collective-permute-done | bytes 1048608 | tf_op jit(solution)/shard_map/rows_grad_mid_1/ppermute | solution.py:76
  476.5 10.3 %shard_map.272 = (bf16[256,3072]{1,0:T(8,128)(2,1)S(1)}, bf16[256,3072]{1,0:T(8,128)(2,1)}, bf16[256,3072]{1,0:T(8,128)(2,1)}, bf16[256,3072]{1,0:T(8,128)(2,1)}) custom-call(s32[2]{0:T(128)S(1)} %broadcast_10_places.2.places, bf16[512,2048]{1,0:T(8,128)(2,1)} %copy-done, bf16[512,2048]{1,0:T(8,128)(2,1)} %pad_maximum_fusion.4.cot.refs_1_, ...), custom_call_target="tpu_custom_call" | custom-call | tf_op jit(solution)/shard_map/pallas_call | solution.py:606
  499.2 15.2 %shard_map.274.refs_0_.refs_1_.refs_2_.refs_4_ = bf16[1024,3072]{1,0:T(8,128)(2,1)} custom-call(f32[2,4]{1,0:T(2,128)S(1)} %multiply_exponential_fusion.powers, f32[2]{0:T(128)S(1)} %subtract_log_fusion.logs, f32[1024,1024]{1,0:T(8,128)} %shard_map.273.grad, f32[1024,3072]{1,0:T(8,128)} %shard_map.258.pre.gates, bf16[1024,2048]{1,0:T(8,128)(2,1)} %get-tuple-element.352.kept, ...), custom_call_target="tpu_custom_call" | custom-call | tf_op jit(solution)/shard_map/pallas_call | solution.py:470
  519.0 8.5 %shard_map.276 = (bf16[256,2048]{1,0:T(8,128)(2,1)S(1)}, f32[1,2048]{1,0:T(1,128)S(1)}) custom-call(s32[1]{0:T(128)} %bitcast.1.places, bf16[1024,3072]{1,0:T(8,128)(2,1)} %shard_map.274.refs_0_.refs_1_.refs_2_.refs_4_, bf16[1024,3072]{1,0:T(8,128)(2,1)} %pad_maximum_fusion.refs_3_.refs_1_, bf16[1024,3072]{1,0:T(8,128)(2,1)} %collective-permute-done.13.refs_4_.refs_2_, ...), custom_call_target="tpu_custom_call" | custom-call | tf_op jit(solution)/shard_map/pallas_call | solution.py:261
  530.1 17.0 %shard_map.277 = (f32[256,2048]{1,0:T(8,128)S(1)}, f32[256,2048]{1,0:T(8,128)}, f32[256,2048]{1,0:T(8,128)}, f32[1,2048]{1,0:T(1,128)S(1)}) custom-call(s32[3]{0:T(128)S(1)} %pad_add_fusion.1.places, bf16[1024,3072]{1,0:T(8,128)(2,1)} %shard_map.274.refs_0_.refs_1_.refs_2_.refs_4_, bf16[1024,3072]{1,0:T(8,128)(2,1)} %shard_map.274.refs_0_.refs_1_.refs_2_.refs_4_, ...), custom_call_target="tpu_custom_call" | custom-call | tf_op jit(solution)/shard_map/pallas_call | solution.py:261
  558.5 12.1 %shard_map.278 = bf16[1024,3072]{1,0:T(8,128)(2,1)} custom-call(s32[4]{0:T(128)S(1)} %pad_add_fusion.2.places, bf16[256,2048]{1,0:T(8,128)(2,1)S(1)} %copy-done.3, bf16[256,2048]{1,0:T(8,128)(2,1)S(1)} %copy-done.8, bf16[256,2048]{1,0:T(8,128)(2,1)} %collective-permute-done.9.refs_2_.refs_5_, bf16[256,2048]{1,0:T(8,128)(2,1)S(1)} %copy-done.5, ...), custom_call_target="tpu_custom_call" | custom-call | tf_op jit(solution)/shard_map/pallas_call | solution.py:606
  575.5 8.8 %collective-permute-done.47 = bf16[128,3072]{1,0:T(8,128)(2,1)S(1)} collective-permute-done((bf16[128,3072]{1,0:T(8,128)(2,1)S(1)}, bf16[128,3072]{1,0:T(8,128)(2,1)S(1)}, u32[]{:S(2)}, u32[]{:S(2)}) %collective-permute-start.47) | collective-permute-done | bytes 786464 | tf_op jit(solution)/shard_map/grad_feed_far_tensor2/ppermute | solution.py:70
  616.0 7.8 %collective-permute-done.54 = bf16[128,3072]{1,0:T(8,128)(2,1)S(1)} collective-permute-done((bf16[128,3072]{1,0:T(8,128)(2,1)S(1)}, bf16[128,3072]{1,0:T(8,128)(2,1)S(1)}, u32[]{:S(2)}, u32[]{:S(2)}) %collective-permute-start.54) | collective-permute-done | bytes 786464 | tf_op jit(solution)/shard_map/grad_feed_near_dp2/ppermute | solution.py:70
  625.9 7.8 %collective-permute-done.55 = bf16[128,3072]{1,0:T(8,128)(2,1)S(1)} collective-permute-done((bf16[128,3072]{1,0:T(8,128)(2,1)S(1)}, bf16[128,3072]{1,0:T(8,128)(2,1)S(1)}, u32[]{:S(2)}, u32[]{:S(2)}) %collective-permute-start.55) | collective-permute-done | bytes 786464 | tf_op jit(solution)/shard_map/grad_feed_near_dp4/ppermute | solution.py:70
  642.2 12.9 %shard_map.280 = (bf16[256,3072]{1,0:T(8,128)(2,1)S(1)}, bf16[256,3072]{1,0:T(8,128)(2,1)}, bf16[256,3072]{1,0:T(8,128)(2,1)}, bf16[256,3072]{1,0:T(8,128)(2,1)}) custom-call(s32[4]{0:T(128)S(1)} %pad_add_fusion.2.places, bf16[256,2048]{1,0:T(8,128)(2,1)S(1)} %copy-done.3, bf16[256,2048]{1,0:T(8,128)(2,1)S(1)} %copy-done.9, ...), custom_call_target="tpu_custom_call" | custom-call | tf_op jit(solution)/shard_map/pallas_call | solution.py:606
  655.2 19.6 %collective-permute-done.53 = bf16[128,3072]{1,0:T(8,128)(2,1)} collective-permute-done((bf16[128,3072]{1,0:T(8,128)(2,1)}, bf16[128,3072]{1,0:T(8,128)(2,1)}, u32[]{:S(2)}, u32[]{:S(2)}) %collective-permute-start.53) | collective-permute-done | bytes 786464 | tf_op jit(solution)/shard_map/grad_feed_far_tensor2/ppermute | solution.py:70
  682.9 9.1 %collective-permute-done.68 = bf16[256,1024]{1,0:T(8,128)(2,1)S(1)} collective-permute-done((bf16[256,1024]{1,0:T(8,128)(2,1)S(1)}, bf16[256,1024]{1,0:T(8,128)(2,1)S(1)}, u32[]{:S(2)}, u32[]{:S(2)}) %collective-permute-start.68) | collective-permute-done | bytes 524320 | tf_op jit(solution)/shard_map/grad_w_out_dp4/ppermute | solution.py:70
  698.6 32.3 %collective-permute-done.70 = bf16[128,1024]{1,0:T(8,128)(2,1)S(1)} collective-permute-done((bf16[128,1024]{1,0:T(8,128)(2,1)S(1)}, bf16[128,1024]{1,0:T(8,128)(2,1)S(1)}, u32[]{:S(2)}, u32[]{:S(2)}) %collective-permute-start.70) | collective-permute-done | bytes 262176 | tf_op jit(solution)/shard_map/grad_w_out_dp2/ppermute | solution.py:70
  749.4 7.9 %collective-permute-done.66 = bf16[128,3072]{1,0:T(8,128)(2,1)S(1)} collective-permute-done((bf16[128,3072]{1,0:T(8,128)(2,1)S(1)}, bf16[128,3072]{1,0:T(8,128)(2,1)S(1)}, u32[]{:S(2)}, u32[]{:S(2)}) %collective-permute-start.66) | collective-permute-done | bytes 786464 | tf_op jit(solution)/shard_map/grad_w_in_dp2/ppermute | solution.py:70
  (395 shorter events, 293.1 us)
Async XLA Ops:
  5.9 39.0 %collective-permute-start.8 = (bf16[256,2048]{1,0:T(8,128)(2,1)}, bf16[256,2048]{1,0:T(8,128)(2,1)S(1)}, u32[]{:S(2)}, u32[]{:S(2)}) collective-permute-start(bf16[256,2048]{1,0:T(8,128)(2,1)} %values.3), channel_id=1, source_target_pairs={{0,1},{1,0},{2,3},{3,2},{4,5},{5,4},{6,7},{7,6},{8,9},{9,8},{10,11... | collective-permute-start | bytes 3145736 | tf_op jit(solution)/shard_map/rows_cot_tensor1/ppermute | solution.py:70
  27.0 27.9 %collective-permute-start.5 = (bf16[256,2048]{1,0:T(8,128)(2,1)S(1)}, bf16[256,2048]{1,0:T(8,128)(2,1)S(1)}, u32[]{:S(2)}, u32[]{:S(2)}) collective-permute-start(bf16[256,2048]{1,0:T(8,128)(2,1)S(1)} %fusion.4.refs_0_.refs_7_), channel_id=1, source_target_pairs={{0,1},{1,2},{2,3},{3,0},{4,5},{5,6},{6,7},{7,4},{8,9},{9,10},{10,1... | collective-permute-start | bytes 3145736 | tf_op jit(solution)/shard_map/rows_attn_1/ppermute | solution.py:76
  55.0 35.4 %collective-permute-start.10 = (bf16[256,3072]{1,0:T(8,128)(2,1)S(1)}, bf16[256,3072]{1,0:T(8,128)(2,1)S(1)}, u32[]{:S(2)}, u32[]{:S(2)}) collective-permute-start(bf16[256,3072]{1,0:T(8,128)(2,1)S(1)} %pad_maximum_fusion.5), channel_id=1, source_target_pairs={{0,16},{4,20},{8,24},{12,28},{16,0},{20,4},{24,8},{28,12},{1,17},{... | collective-permute-start | bytes 4718600 | tf_op jit(solution)/shard_map/w_in_dp4/ppermute | solution.py:70
  55.5 35.1 %collective-permute-start.11 = (bf16[256,3072]{1,0:T(8,128)(2,1)S(1)}, bf16[256,3072]{1,0:T(8,128)(2,1)S(1)}, u32[]{:S(2)}, u32[]{:S(2)}) collective-permute-start(bf16[256,3072]{1,0:T(8,128)(2,1)S(1)} %pad_maximum_fusion.6), channel_id=1, source_target_pairs={{0,8},{4,12},{8,0},{12,4},{16,24},{20,28},{24,16},{28,20},{1,9},{5... | collective-permute-start | bytes 4718600 | tf_op jit(solution)/shard_map/w_in_dp2/ppermute | solution.py:70
  56.2 37.5 %collective-permute-start.9 = (bf16[256,2048]{1,0:T(8,128)(2,1)S(1)}, bf16[256,2048]{1,0:T(8,128)(2,1)}, u32[]{:S(2)}, u32[]{:S(2)}) collective-permute-start(bf16[256,2048]{1,0:T(8,128)(2,1)S(1)} %collective-permute-done.5.refs_1_.refs_3_), channel_id=1, source_target_pairs={{0,1},{1,2},{2,3},{3,0},{4,5},{5,6},{6,7},{7,4},{8,9},{9,10},{10,1... | collective-permute-start | bytes 3145736 | tf_op jit(solution)/shard_map/rows_attn_2/ppermute | solution.py:76
  93.8 29.3 %collective-permute-start.12 = (bf16[256,2048]{1,0:T(8,128)(2,1)}, bf16[256,2048]{1,0:T(8,128)(2,1)S(1)}, u32[]{:S(2)}, u32[]{:S(2)}) collective-permute-start(bf16[256,2048]{1,0:T(8,128)(2,1)} %collective-permute-done.9.refs_2_.refs_5_), channel_id=1, source_target_pairs={{0,1},{1,2},{2,3},{3,0},{4,5},{5,6},{6,7},{7,4},{8,9},{9,10},{10,1... | collective-permute-start | bytes 3145736 | tf_op jit(solution)/shard_map/rows_attn_3/ppermute | solution.py:76
  140.8 41.5 %collective-permute-start.21 = (bf16[1024,1024]{1,0:T(8,128)(2,1)}, bf16[1024,1024]{1,0:T(8,128)(2,1)}, u32[]{:S(2)}, u32[]{:S(2)}) collective-permute-start(bf16[1024,1024]{1,0:T(8,128)(2,1)} %pad_maximum_fusion.3.refs_1_.refs_3_), channel_id=1, source_target_pairs={{0,4},{4,0},{8,12},{12,8},{16,20},{20,16},{24,28},{28,24},{1,5},{5... | collective-permute-start | bytes 6291464 | tf_op jit(solution)/shard_map/w_out_dp1/ppermute | solution.py:70
  144.7 37.5 %collective-permute-start.20 = (bf16[128,3072]{1,0:T(8,128)(2,1)}, bf16[128,3072]{1,0:T(8,128)(2,1)}, u32[]{:S(2)}, u32[]{:S(2)}) collective-permute-start(bf16[128,3072]{1,0:T(8,128)(2,1)} %get-tuple-element.264), channel_id=1, source_target_pairs={{0,2},{1,3},{2,0},{3,1},{4,6},{5,7},{6,4},{7,5},{8,10},{9,11},{10,... | collective-permute-start | bytes 2359304 | tf_op jit(solution)/shard_map/w_feed_far_tensor2/ppermute | solution.py:70
  186.8 28.6 %collective-permute-start.22 = (bf16[256,2048]{1,0:T(8,128)(2,1)}, bf16[256,2048]{1,0:T(8,128)(2,1)}, u32[]{:S(2)}, u32[]{:S(2)}) collective-permute-start(bf16[256,2048]{1,0:T(8,128)(2,1)} %shard_map.262), channel_id=1, source_target_pairs={{0,1},{1,2},{2,3},{3,0},{4,5},{5,6},{6,7},{7,4},{8,9},{9,10},{10,1... | collective-permute-start | bytes 3145736 | tf_op jit(solution)/shard_map/sum_attn_1/ppermute | solution.py:76
  187.1 64.9 %collective-permute-start.25 = (bf16[256,3072]{1,0:T(8,128)(2,1)}, bf16[256,3072]{1,0:T(8,128)(2,1)}, u32[]{:S(2)}, u32[]{:S(2)}) collective-permute-start(bf16[256,3072]{1,0:T(8,128)(2,1)} %pad_maximum_fusion.8), channel_id=1, source_target_pairs={{0,16},{4,20},{8,24},{12,28},{16,0},{20,4},{24,8},{28,12},{1,17},{... | collective-permute-start | bytes 4718600 | tf_op jit(solution)/shard_map/w_feed_near_dp4/ppermute | solution.py:70
  188.7 63.3 %collective-permute-start.26 = (bf16[256,3072]{1,0:T(8,128)(2,1)}, bf16[256,3072]{1,0:T(8,128)(2,1)}, u32[]{:S(2)}, u32[]{:S(2)}) collective-permute-start(bf16[256,3072]{1,0:T(8,128)(2,1)} %pad_maximum_fusion.9), channel_id=1, source_target_pairs={{0,8},{4,12},{8,0},{12,4},{16,24},{20,28},{24,16},{28,20},{1,9},{5... | collective-permute-start | bytes 4718600 | tf_op jit(solution)/shard_map/w_feed_near_dp2/ppermute | solution.py:70
  190.1 57.3 %collective-permute-start.23 = (bf16[128,3072]{1,0:T(8,128)(2,1)S(1)}, bf16[128,3072]{1,0:T(8,128)(2,1)}, u32[]{:S(2)}, u32[]{:S(2)}) collective-permute-start(bf16[128,3072]{1,0:T(8,128)(2,1)S(1)} %get-tuple-element.275), channel_id=1, source_target_pairs={{0,2},{1,3},{2,0},{3,1},{4,6},{5,7},{6,4},{7,5},{8,10},{9,11},{10,... | collective-permute-start | bytes 2359304 | tf_op jit(solution)/shard_map/w_feed_far_tensor2/ppermute | solution.py:70
  252.0 26.3 %collective-permute-start.24 = (bf16[256,2048]{1,0:T(8,128)(2,1)S(1)}, bf16[256,2048]{1,0:T(8,128)(2,1)S(1)}, u32[]{:S(2)}, u32[]{:S(2)}) collective-permute-start(bf16[256,2048]{1,0:T(8,128)(2,1)S(1)} %add_convert_fusion.4), channel_id=1, source_target_pairs={{0,1},{1,2},{2,3},{3,0},{4,5},{5,6},{6,7},{7,4},{8,9},{9,10},{10,1... | collective-permute-start | bytes 3145736 | tf_op jit(solution)/shard_map/sum_attn_2/ppermute | solution.py:76
  278.7 34.9 %collective-permute-start.31 = (bf16[256,3072]{1,0:T(8,128)(2,1)S(1)}, bf16[256,3072]{1,0:T(8,128)(2,1)S(1)}, u32[]{:S(2)}, u32[]{:S(2)}) collective-permute-start(bf16[256,3072]{1,0:T(8,128)(2,1)S(1)} %pad_maximum_fusion.10), channel_id=1, source_target_pairs={{0,16},{4,20},{8,24},{12,28},{16,0},{20,4},{24,8},{28,12},{1,17},{... | collective-permute-start | bytes 4718600 | tf_op jit(solution)/shard_map/w_feed_far_dp4/ppermute | solution.py:70
  279.2 34.6 %collective-permute-start.32 = (bf16[256,3072]{1,0:T(8,128)(2,1)S(1)}, bf16[256,3072]{1,0:T(8,128)(2,1)S(1)}, u32[]{:S(2)}, u32[]{:S(2)}) collective-permute-start(bf16[256,3072]{1,0:T(8,128)(2,1)S(1)} %pad_maximum_fusion.11), channel_id=1, source_target_pairs={{0,8},{4,12},{8,0},{12,4},{16,24},{20,28},{24,16},{28,20},{1,9},{5... | collective-permute-start | bytes 4718600 | tf_op jit(solution)/shard_map/w_feed_far_dp2/ppermute | solution.py:70
  407.8 68.7 %collective-permute-start.42 = (bf16[1024,3072]{1,0:T(8,128)(2,1)}, bf16[1024,3072]{1,0:T(8,128)(2,1)}, u32[]{:S(2)}, u32[]{:S(2)}) collective-permute-start(bf16[1024,3072]{1,0:T(8,128)(2,1)} %shard_map.268), channel_id=1, source_target_pairs={{0,4},{4,0},{8,12},{12,8},{16,20},{20,16},{24,28},{28,24},{1,5},{5... | collective-permute-start | bytes 18874376 | tf_op jit(solution)/shard_map/grad_feed_near_dp1/ppermute | solution.py:70
  416.2 26.9 %collective-permute-start.36 = (bf16[256,2048]{1,0:T(8,128)(2,1)S(1)}, bf16[256,2048]{1,0:T(8,128)(2,1)S(1)}, u32[]{:S(2)}, u32[]{:S(2)}) collective-permute-start(bf16[256,2048]{1,0:T(8,128)(2,1)S(1)} %get-tuple-element.339.refs_0_), channel_id=1, source_target_pairs={{0,1},{1,2},{2,3},{3,0},{4,5},{5,6},{6,7},{7,4},{8,9},{9,10},{10,1... | collective-permute-start | bytes 3145736 | tf_op jit(solution)/shard_map/rows_grad_mid_1/ppermute | solution.py:76
  443.1 26.0 %collective-permute-start.38 = (bf16[256,2048]{1,0:T(8,128)(2,1)S(1)}, bf16[256,2048]{1,0:T(8,128)(2,1)S(1)}, u32[]{:S(2)}, u32[]{:S(2)}) collective-permute-start(bf16[256,2048]{1,0:T(8,128)(2,1)S(1)} %collective-permute-done.36.refs_1_), channel_id=1, source_target_pairs={{0,1},{1,2},{2,3},{3,0},{4,5},{5,6},{6,7},{7,4},{8,9},{9,10},{10,1... | collective-permute-start | bytes 3145736 | tf_op jit(solution)/shard_map/rows_grad_mid_2/ppermute | solution.py:76
  443.1 43.7 %collective-permute-start.40 = (bf16[256,3072]{1,0:T(8,128)(2,1)}, bf16[256,3072]{1,0:T(8,128)(2,1)S(1)}, u32[]{:S(2)}, u32[]{:S(2)}) collective-permute-start(bf16[256,3072]{1,0:T(8,128)(2,1)} %get-tuple-element.336), channel_id=1, source_target_pairs={{0,16},{4,20},{8,24},{12,28},{16,0},{20,4},{24,8},{28,12},{1,17},{... | collective-permute-start | bytes 4718600 | tf_op jit(solution)/shard_map/grad_feed_far_dp4/ppermute | solution.py:70
  443.6 46.5 %collective-permute-start.41 = (bf16[256,3072]{1,0:T(8,128)(2,1)}, bf16[256,3072]{1,0:T(8,128)(2,1)}, u32[]{:S(2)}, u32[]{:S(2)}) collective-permute-start(bf16[256,3072]{1,0:T(8,128)(2,1)} %get-tuple-element.338), channel_id=1, source_target_pairs={{0,8},{4,12},{8,0},{12,4},{16,24},{20,28},{24,16},{28,20},{1,9},{5... | collective-permute-start | bytes 4718600 | tf_op jit(solution)/shard_map/grad_feed_far_dp2/ppermute | solution.py:70
  517.5 53.2 %collective-permute-start.48 = (bf16[256,3072]{1,0:T(8,128)(2,1)}, bf16[256,3072]{1,0:T(8,128)(2,1)S(1)}, u32[]{:S(2)}, u32[]{:S(2)}) collective-permute-start(bf16[256,3072]{1,0:T(8,128)(2,1)} %get-tuple-element.388), channel_id=1, source_target_pairs={{0,16},{4,20},{8,24},{12,28},{16,0},{20,4},{24,8},{28,12},{1,17},{... | collective-permute-start | bytes 4718600 | tf_op jit(solution)/shard_map/grad_feed_near_dp4/ppermute | solution.py:70
  527.4 43.2 %collective-permute-start.46 = (bf16[256,2048]{1,0:T(8,128)(2,1)S(1)}, bf16[256,2048]{1,0:T(8,128)(2,1)}, u32[]{:S(2)}, u32[]{:S(2)}) collective-permute-start(bf16[256,2048]{1,0:T(8,128)(2,1)S(1)} %get-tuple-element.372), channel_id=1, source_target_pairs={{0,1},{1,2},{2,3},{3,0},{4,5},{5,6},{6,7},{7,4},{8,9},{9,10},{10,1... | collective-permute-start | bytes 3145736 | tf_op jit(solution)/shard_map/sum_grad_attn_1/ppermute | solution.py:76
  528.6 43.7 %collective-permute-start.49 = (bf16[256,3072]{1,0:T(8,128)(2,1)}, bf16[256,3072]{1,0:T(8,128)(2,1)}, u32[]{:S(2)}, u32[]{:S(2)}) collective-permute-start(bf16[256,3072]{1,0:T(8,128)(2,1)} %get-tuple-element.390), channel_id=1, source_target_pairs={{0,8},{4,12},{8,0},{12,4},{16,24},{20,28},{24,16},{28,20},{1,9},{5... | collective-permute-start | bytes 4718600 | tf_op jit(solution)/shard_map/grad_feed_near_dp2/ppermute | solution.py:70
  549.5 34.8 %collective-permute-start.47 = (bf16[128,3072]{1,0:T(8,128)(2,1)S(1)}, bf16[128,3072]{1,0:T(8,128)(2,1)S(1)}, u32[]{:S(2)}, u32[]{:S(2)}) collective-permute-start(bf16[128,3072]{1,0:T(8,128)(2,1)S(1)} %get-tuple-element.514), channel_id=1, source_target_pairs={{0,2},{1,3},{2,0},{3,1},{4,6},{5,7},{6,4},{7,5},{8,10},{9,11},{10,... | collective-permute-start | bytes 2359304 | tf_op jit(solution)/shard_map/grad_feed_far_tensor2/ppermute | solution.py:70
  584.3 57.9 %collective-permute-start.51 = (bf16[1024,3072]{1,0:T(8,128)(2,1)}, bf16[1024,3072]{1,0:T(8,128)(2,1)}, u32[]{:S(2)}, u32[]{:S(2)}) collective-permute-start(bf16[1024,3072]{1,0:T(8,128)(2,1)} %shard_map.278), channel_id=1, source_target_pairs={{0,4},{4,0},{8,12},{12,8},{16,20},{20,16},{24,28},{28,24},{1,5},{5... | collective-permute-start | bytes 18874376 | tf_op jit(solution)/shard_map/grad_w_in_dp1/ppermute | solution.py:70
  615.3 59.4 %collective-permute-start.53 = (bf16[128,3072]{1,0:T(8,128)(2,1)}, bf16[128,3072]{1,0:T(8,128)(2,1)}, u32[]{:S(2)}, u32[]{:S(2)}) collective-permute-start(bf16[128,3072]{1,0:T(8,128)(2,1)} %get-tuple-element.403), channel_id=1, source_target_pairs={{0,2},{1,3},{2,0},{3,1},{4,6},{5,7},{6,4},{7,5},{8,10},{9,11},{10,... | collective-permute-start | bytes 2359304 | tf_op jit(solution)/shard_map/grad_feed_far_tensor2/ppermute | solution.py:70
  623.8 50.9 %collective-permute-start.50 = (bf16[256,2048]{1,0:T(8,128)(2,1)}, bf16[256,2048]{1,0:T(8,128)(2,1)}, u32[]{:S(2)}, u32[]{:S(2)}) collective-permute-start(bf16[256,2048]{1,0:T(8,128)(2,1)} %add_convert_fusion.1), channel_id=1, source_target_pairs={{0,1},{1,2},{2,3},{3,0},{4,5},{5,6},{6,7},{7,4},{8,9},{9,10},{10,1... | collective-permute-start | bytes 3145736 | tf_op jit(solution)/shard_map/sum_grad_attn_2/ppermute | solution.py:76
  678.6 56.1 %collective-permute-start.56 = (bf16[256,2048]{1,0:T(8,128)(2,1)}, bf16[256,2048]{1,0:T(8,128)(2,1)}, u32[]{:S(2)}, u32[]{:S(2)}) collective-permute-start(bf16[256,2048]{1,0:T(8,128)(2,1)} %add_convert_fusion), channel_id=1, source_target_pairs={{0,1},{1,2},{2,3},{3,0},{4,5},{5,6},{6,7},{7,4},{8,9},{9,10},{10,1... | collective-permute-start | bytes 3145736 | tf_op jit(solution)/shard_map/sum_grad_attn_3/ppermute | solution.py:76
  678.6 56.1 %collective-permute-start.64 = (bf16[256,3072]{1,0:T(8,128)(2,1)}, bf16[256,3072]{1,0:T(8,128)(2,1)}, u32[]{:S(2)}, u32[]{:S(2)}) collective-permute-start(bf16[256,3072]{1,0:T(8,128)(2,1)} %get-tuple-element.422), channel_id=1, source_target_pairs={{0,16},{4,20},{8,24},{12,28},{16,0},{20,4},{24,8},{28,12},{1,17},{... | collective-permute-start | bytes 4718600 | tf_op jit(solution)/shard_map/grad_w_in_dp4/ppermute | solution.py:70
  679.9 56.9 %collective-permute-start.65 = (bf16[256,3072]{1,0:T(8,128)(2,1)}, bf16[256,3072]{1,0:T(8,128)(2,1)}, u32[]{:S(2)}, u32[]{:S(2)}) collective-permute-start(bf16[256,3072]{1,0:T(8,128)(2,1)} %get-tuple-element.424), channel_id=1, source_target_pairs={{0,8},{4,12},{8,0},{12,4},{16,24},{20,28},{24,16},{28,20},{1,9},{5... | collective-permute-start | bytes 4718600 | tf_op jit(solution)/shard_map/grad_w_in_dp2/ppermute | solution.py:70
  693.7 37.2 %collective-permute-start.70 = (bf16[128,1024]{1,0:T(8,128)(2,1)S(1)}, bf16[128,1024]{1,0:T(8,128)(2,1)S(1)}, u32[]{:S(2)}, u32[]{:S(2)}) collective-permute-start(bf16[128,1024]{1,0:T(8,128)(2,1)S(1)} %get-tuple-element.438), channel_id=1, source_target_pairs={{0,8},{4,12},{8,0},{12,4},{16,24},{20,28},{24,16},{28,20},{1,9},{5... | collective-permute-start | bytes 786440 | tf_op jit(solution)/shard_map/grad_w_out_dp2/ppermute | solution.py:70
  694.3 36.6 %collective-permute-start.71 = (bf16[128,1024]{1,0:T(8,128)(2,1)}, bf16[128,1024]{1,0:T(8,128)(2,1)S(1)}, u32[]{:S(2)}, u32[]{:S(2)}) collective-permute-start(bf16[128,1024]{1,0:T(8,128)(2,1)} %get-tuple-element.440), channel_id=1, source_target_pairs={{0,16},{4,20},{8,24},{12,28},{16,0},{20,4},{24,8},{28,12},{1,17},{... | collective-permute-start | bytes 786440 | tf_op jit(solution)/shard_map/grad_w_out_dp4/ppermute | solution.py:70
  (107 other events, 1714.9 us)

commit v2 on v1

v2 whole, which is shorter than its diff:
```python
import functools
import math

import jax
import jax.numpy as jnp
from jax import lax
from jax.experimental import pallas as pl
from jax.experimental.pallas import tpu as pltpu
from jax.sharding import PartitionSpec as P

KD = 256
VD = 512
TILE = 256

epsilon = 1e-05
group_floor = 1.0
f32 = jnp.float32
low = jnp.bfloat16
gelu_slope = math.sqrt(2.0 / math.pi)
gelu_cubic = 0.044715


def layer_norm(values, floor_value=epsilon):
    center = values - jnp.mean(values, axis=-1, keepdims=True)
    scale_inv = lax.rsqrt(jnp.mean(center * center, axis=-1, keepdims=True) + floor_value)
    return (center * scale_inv, scale_inv)


def norm_back(grad_norm, normed, scale_inv):
    mean_grad = jnp.mean(grad_norm, axis=-1, keepdims=True)
    mean_cross = jnp.mean(grad_norm * normed, axis=-1, keepdims=True)
    return (grad_norm - mean_grad - normed * mean_cross) * scale_inv


def sequence_layout(lengths, offsets, total):
    places = jnp.arange(total, dtype=jnp.int32)[:, None]
    inside = (places >= offsets[None, :]) & (places < offsets[None, :] + lengths[None, :])
    numbers = jnp.arange(1, offsets.shape[0] + 1, dtype=jnp.int32)
    segment = jnp.sum(jnp.where(inside, numbers[None, :], 0), axis=1) - 1
    position = places[:, 0] - jnp.sum(jnp.where(inside, offsets[None, :], 0), axis=1)
    return (segment, position.astype(f32))


def rotation(position, size):
    half = size // 2
    frequency = jnp.exp(-math.log(10000.0) * jnp.arange(half, dtype=f32) * 2.0 / size)
    angles = position[:, None] * frequency[None, :]
    return (jnp.cos(angles), jnp.sin(angles))


def dot(left, right):
    return jnp.dot(left, right, preferred_element_type=f32)


def dot_nt(left, right):
    return lax.dot_general(left, right, (((1,), (1,)), ((), ())), preferred_element_type=f32)


def dot_tn(left, right):
    return lax.dot_general(left, right, (((0,), (0,)), ((), ())), preferred_element_type=f32)


def swap(values, axis, bits, name="swap"):
    size = lax.axis_size(axis)
    with jax.named_scope(f"{name}_{axis}{bits}"):
        return lax.ppermute(values, axis, [(i, i ^ bits) for i in range(size)])


def shift(values, axis, step, name="shift"):
    size = lax.axis_size(axis)
    with jax.named_scope(name):
        return lax.ppermute(values, axis, [(i, (i + step) % size) for i in range(size)])


def tie(values, token):
    return values if token is None else lax.optimization_barrier((values, token))[0]


def dp_bits(size):
    bits = [1 << b for b in range(1, size.bit_length() - 1)]
    return list(zip(bits, bits[1:] + bits[:1]))


def feature_order(size):
    same = []
    for half in (0, 1):
        held = [0]
        for bits in dp_bits(size):
            held += [k ^ bits[half] for k in held]
        same += [(k, half) for k in held]
    return same + [(k ^ 1, half) for k, half in same]


def gather_step(parts, stage, name, after=None):
    bits = dp_bits(lax.axis_size("dp"))[stage]
    parts = sync(*parts)
    came = tie([swap(part, "dp", bit, name) for part, bit in zip(parts, bits)], after)
    return [join(*pair) for pair in zip(parts, came)]


def gather_rest(parts, stage, name, after=None):
    for step in range(stage, len(dp_bits(lax.axis_size("dp")))):
        parts = gather_step(parts, step, name, after)
    return parts


def gather_core(parts, name):
    return [*parts, *(swap(part, "dp", 1, name) for part in sync(*parts))]


def scatter_step(parts, stage, name, after=None):
    bits = dp_bits(lax.axis_size("dp"))[-1 - stage]
    parts = sync(*parts)
    came = tie([swap(sent, "dp", bit, name) for (_, sent), bit in zip(parts, bits)], after)
    return [add_split(kept, part) for (kept, _), part in zip(parts, came)]


def scatter_rest(parts, stage, name):
    for step in range(stage, len(dp_bits(lax.axis_size("dp")))):
        parts = scatter_step(parts, step, name)
    return [half for part in parts for half in part]


def sync(*values):
    return lax.optimization_barrier(values)


def gather_ring(rows, name, beside):
    pieces = [rows]
    for step in range(1, lax.axis_size("tensor")):
        came = shift(pieces[-1], "tensor", 1, f"{name}_{step}")
        pieces.append(beside(step, came))
    return pieces


def call(kernel, grid, in_specs, out_specs, out_shape, vmem=40, scratch=(), scalars=0, aliases=None):
    return pl.pallas_call(
        kernel,
        grid_spec=pltpu.PrefetchScalarGridSpec(
            num_scalar_prefetch=scalars,
            grid=grid,
            in_specs=in_specs,
            out_specs=out_specs,
            scratch_shapes=scratch,
        ),
        out_shape=out_shape,
        input_output_aliases=aliases or {},
        compiler_params=pltpu.CompilerParams(
            dimension_semantics=("arbitrary",) * len(grid), vmem_limit_bytes=vmem * 1024 * 1024
        ),
        cost_estimate=pl.CostEstimate(flops=0, bytes_accessed=0, transcendentals=0),
    )


def join_kernel(steps, *refs):
    step, first = pl.program_id(0), 0
    for ref, length in zip(refs[:-1], steps):

        @pl.when((step >= first) & (step < first + length))
        def _(ref=ref):
            refs[-1][...] = ref[...]

        first += length


def join(*parts):
    columns = parts[0].shape[1]
    height = min(min(part.shape[0] for part in parts), 256)
    steps, specs, first = [], [], 0
    for part in parts:
        length = part.shape[0] // height
        specs.append(
            pl.BlockSpec(
                (height, columns),
                lambda t, first=first, length=length: (jnp.clip(t - first, 0, length - 1), 0),
            )
        )
        steps.append(length)
        first += length
    return call(
        functools.partial(join_kernel, steps),
        (first,),
        specs,
        pl.BlockSpec((height, columns), lambda t: (t, 0)),
        jax.ShapeDtypeStruct((first * height, columns), parts[0].dtype),
        40,
    )(*parts)


def column_blocks_kernel(places, *refs):
    for ref, (column, first, size) in zip(refs[:-2], places):
        half = ref.shape[0] // 2
        refs[-2][:, first : first + size] = ref[:half, column : column + size]
        refs[-1][:, first : first + size] = ref[half:, column : column + size]


def column_blocks(sources):
    height = sources[0][0].shape[0]
    places, specs, first = [], [], 0
    for array, column, size in sources:
        places.append((column, first, size))
        specs.append(pl.BlockSpec(array.shape, lambda t: (0, 0)))
        first += size
    half = pl.BlockSpec((height // 2, first), lambda t: (0, 0))
    shape = jax.ShapeDtypeStruct((height // 2, first), sources[0][0].dtype)
    return call(
        functools.partial(column_blocks_kernel, places), (1,), specs, [half, half], [shape, shape]
    )(*[array for array, _, _ in sources])


def add_split_kernel(left, right, upper, lower):
    half = upper.shape[0]
    for i, out in enumerate((upper, lower)):
        rows = slice(i * half, (i + 1) * half)
        out[...] = (left[rows, :].astype(f32) + right[rows, :].astype(f32)).astype(low)


def add_split(left, right):
    count, columns = left.shape
    size = columns // 2 if columns % 256 == 0 else columns
    whole = pl.BlockSpec((count, size), lambda t: (0, t))
    half = pl.BlockSpec((count // 2, size), lambda t: (0, t))
    return call(
        add_split_kernel,
        (columns // size,),
        [whole, whole],
        [half, half],
        [jax.ShapeDtypeStruct((count // 2, columns), low)] * 2,
        40,
    )(left, right)


def add_kernel(left, right, out):
    out[...] = (left[...].astype(f32) + right[...].astype(f32)).astype(out.dtype)


def add_rows(left, right, kind):
    count, width = left.shape
    rows = pl.BlockSpec((count // 2, width), lambda i: (i, 0))
    shape = jax.ShapeDtypeStruct((count, width), kind)
    return call(add_kernel, (2,), [rows, rows], rows, shape)(left, right)


def scale_kernel(rows, gain, out):
    out[...] = (rows[...].astype(f32) * gain[...]).astype(low)


def scale_rows(values, gain):
    count, width = values.shape
    rows = pl.BlockSpec((count // 2, width), lambda i: (i, 0))
    line = pl.BlockSpec((1, width), lambda i: (0, 0))
    shape = jax.ShapeDtypeStruct((count, width), low)
    return call(scale_kernel, (2,), [rows, line], rows, shape)(values, gain[None])


def normed_kernel(values, out):
    out[...] = layer_norm(values[...].astype(f32))[0].astype(low)


def normed_rows(values):
    count, width = values.shape
    rows = pl.BlockSpec((count // 2, width), lambda i: (i, 0))
    shape = jax.ShapeDtypeStruct((count, width), low)
    return call(normed_kernel, (2,), [rows], rows, shape)(values)


def reorder_kernel(table, values, out):
    count = table.shape[0]
    width = values.shape[1] // count
    for place in range(count):
        start = pl.multiple_of(table[place] * width, width)
        out[:, place * width : (place + 1) * width] = values[:, pl.ds(start, width)]


def reorder(values, table):
    count, (rows, width) = table.shape[0], values.shape
    size = width // count
    if size % 128:
        blocks = [
            lax.dynamic_slice_in_dim(values, table[i] * size, size, axis=1) for i in range(count)
        ]
        return jnp.concatenate(blocks, axis=1)
    part = min(rows, 64)
    spec = pl.BlockSpec((part, width), lambda i, _: (i, 0))
    return call(
        reorder_kernel,
        (rows // part,),
        [spec],
        spec,
        jax.ShapeDtypeStruct(values.shape, values.dtype),
        40,
        scalars=1,
    )(table, values)


def project_kernel(count, places, *refs):
    weights, out = refs[count : count + 4], refs[-1]
    depth = weights[0].shape[0]
    for i in range(count):
        rows = refs[i]
        size = rows.shape[0]
        start = pl.multiple_of(places[i] * size, size) if out.shape[0] > size else 0
        out[pl.ds(start, size), :] = sum(
            dot(rows[:, q * depth : (q + 1) * depth], weights[q][...]) for q in range(4)
        )


def project(pieces, weight, whole, places, chunks):
    (count, width), columns = pieces[0].shape, weight[0].shape[1]
    size = 512 if columns % 512 == 0 else TILE
    spec = pl.BlockSpec((width // 4, size), lambda j, _: (0, j))
    rows = pl.BlockSpec((count, width), lambda j, _: (0, 0))
    number = len(pieces)
    if whole is None:
        held, out = [], pl.BlockSpec((count * chunks, size), lambda j, _: (0, j))
    else:
        held, out = [whole], pl.BlockSpec((count, size), lambda j, at: (at[0], j))
    return call(
        functools.partial(project_kernel, number),
        (columns // size,),
        [rows] * number + [spec] * 4 + [pl.BlockSpec(memory_space=pl.ANY)] * len(held),
        out,
        jax.ShapeDtypeStruct((count * chunks, columns), f32),
        56,
        scalars=1,
        aliases={number + 5: 0} if held else None,
    )(jnp.stack(places), *pieces, *weight, *held)


def part_specs(shape, steps, column):
    def spec(part):
        def index(i, j, *_):
            return (jnp.where(i == part, j, jnp.where(i < part, 0, steps - 1)), column)

        return pl.BlockSpec(shape, index)

    return [spec(part) for part in range(4)]


def terms_kernel(count, paired, places, *refs):
    weights, outs = refs[count : count + 4], refs[count + 4 :]
    pairs, outs = outs[: count * paired], outs[count * paired :]

    def give(weight):
        sums = 0.0
        for i, rows in enumerate(refs[:count]):
            result = dot_nt(rows[...], weight[...])
            outs[i][...] = result.astype(outs[i].dtype)
            if paired:
                sums = sums + jnp.sum(result * pairs[i][...].astype(f32), axis=0, keepdims=True)
        if paired:
            outs[count][...] = sums

    for part, weight in enumerate(weights):
        pl.when(pl.program_id(0) == part)(functools.partial(give, weight))


def terms(whole, weight, places, size, kinds, pairs):
    quarter, depth = weight[0].shape
    tile = min(quarter, 512 if depth <= 1024 else 256)
    steps = quarter // tile
    number = len(places)
    rows = [
        pl.BlockSpec((size, depth), lambda i, j, at, n=n: (at[n], 0)) for n in range(number)
    ]
    out = lambda height: pl.BlockSpec((height, tile), lambda i, j, _: (0, i * steps + j))
    paired = 1 if pairs else 0
    return call(
        functools.partial(terms_kernel, number, paired),
        (4, steps),
        rows + part_specs((tile, depth), steps, 0) + [out(size)] * (number * paired),
        [out(size)] * number + [out(1)] * paired,
        [jax.ShapeDtypeStruct((size, 4 * quarter), kind) for kind in kinds]
        + [jax.ShapeDtypeStruct((1, 4 * quarter), f32)] * paired,
        56,
        scalars=1,
    )(jnp.stack(places), *([whole] * number), *weight, *(pairs or []))


def scatter_places():
    own, size = lax.axis_index("tensor"), lax.axis_size("tensor")
    return [(own - step) % size for step in range(1, size + 1)]


def scatter_ring(total, rest, name, beside):
    for step, own in enumerate(rest, 1):
        came = shift(total, "tensor", 1, f"{name}_{step}")
        if step == len(rest):
            return beside(step, came), own
        total = beside(step, add_rows(came, own, low))


def norm_kernel(values, came, added, gain, middle, out):
    rows = values[...].astype(f32) + (came[...].astype(f32) + added[...])
    middle[...] = rows
    out[...] = (layer_norm(rows)[0] * gain[...]).astype(low)


def norm_rows(values, came, added, gain):
    count, width = values.shape
    size = min(count, 128)
    rows = pl.BlockSpec((size, width), lambda i: (i, 0))
    return call(
        norm_kernel,
        (count // size,),
        [rows, rows, rows, pl.BlockSpec((1, width), lambda i: (0, 0))],
        [rows, rows],
        [jax.ShapeDtypeStruct((count, width), f32), jax.ShapeDtypeStruct((count, width), low)],
        40,
    )(values, came, added, gain[None])


def norm_back_kernel(values, base, gain, grad, came, out, *more):
    given = grad[...] + came[...].astype(f32)
    normed, scale = layer_norm(values[...].astype(f32))
    result = base[...].astype(f32) + norm_back(given * gain[...], normed, scale)
    out[...] = result
    if not more:
        return
    more[1][...] = result.astype(low)
    term = jnp.sum(given * normed, axis=0, keepdims=True)

    @pl.when(pl.program_id(0) == 0)
    def _():
        more[0][...] = term

    @pl.when(pl.program_id(0) != 0)
    def _():
        more[0][...] += term


def norm_back_rows(values, base, gain, grad, came, more):
    count, width = values.shape
    size = min(count, 128)
    rows = pl.BlockSpec((size, width), lambda i: (i, 0))
    line = pl.BlockSpec((1, width), lambda i: (0, 0))
    shape = lambda height, kind: jax.ShapeDtypeStruct((height, width), kind)
    return call(
        norm_back_kernel,
        (count // size,),
        [rows, rows, line, rows, rows],
        [rows] + [line, rows] * more,
        [shape(count, f32)] + [shape(1, f32), shape(count, low)] * more,
        40,
    )(values, base, gain[None], grad, came)


def place_masks(size):
    row = lax.broadcasted_iota(jnp.int32, (size, size), 0)
    column = lax.broadcasted_iota(jnp.int32, (size, size), 1)
    return row, column


def block_decay(powers, head, apart, base, row, column, after, before):
    kept = (after == before) & (after >= 0)
    if apart == 0:
        kept = kept & (column <= row)
        return jnp.where(kept, base, 0.0)
    return jnp.where(kept, base * powers[head, apart], 0.0)


def retain_kernel(powers, logs, pre, cosine, sine, after, before, mixed, kept, grouped, scale):
    head = pl.program_id(0)
    total = pre.shape[0]
    half = KD // 2
    cos, sin = cosine[...], sine[...]
    for first, factor in ((0, KD ** (-0.5)), (KD, 1.0)):
        a, b = pre[:, first : first + half], pre[:, first + half : first + KD]
        kept[:, first : first + half] = ((a * cos - b * sin) * factor).astype(low)
        kept[:, first + half : first + KD] = ((a * sin + b * cos) * factor).astype(low)
    kept[:, 2 * KD :] = pre[:, 2 * KD : 2 * KD + VD].astype(low)
    row, column = place_masks(TILE)
    base = jnp.exp((row - column).astype(f32) * logs[head])
    for i in range(total // TILE):
        rows = slice(i * TILE, (i + 1) * TILE)
        held = jnp.zeros((TILE, VD), f32)
        for j in range(i + 1):
            past = slice(j * TILE, (j + 1) * TILE)
            decay = block_decay(powers, head, i - j, base, row, column, after[rows, :], before[:, past])
            scores = dot_nt(kept[rows, :KD], kept[past, KD : 2 * KD])
            held = held + dot((decay * scores).astype(low), kept[past, 2 * KD :])
        normed, inverse = layer_norm(held, group_floor)
        grouped[rows, :] = normed
        scale[rows, :] = jnp.broadcast_to(inverse, (TILE, 128))
        gate = pre[rows, 2 * KD + VD :]
        mixed[rows, :] = (gate * jax.nn.sigmoid(gate) * normed).astype(low)


def retain(pre, consts, heads):
    total = pre.shape[0]
    powers, logs, cosine, sine, after, before = consts
    whole = lambda a: pl.BlockSpec(a.shape, lambda h: (0, 0))
    smem = pl.BlockSpec(memory_space=pltpu.SMEM)
    by_head = lambda width: pl.BlockSpec((total, width), lambda h: (0, h))
    shape = lambda width, kind: jax.ShapeDtypeStruct((total, heads * width), kind)
    return call(
        retain_kernel,
        (heads,),
        [smem, smem, by_head(2 * KD + 2 * VD), whole(cosine), whole(sine), whole(after), whole(before)],
        [by_head(VD), by_head(2 * KD + VD), by_head(VD), by_head(128)],
        [shape(VD, low), shape(2 * KD + VD, low), shape(VD, f32), shape(128, f32)],
        56,
    )(*consts[:2], pre, *consts[2:])


def retain_back_kernel(
    powers, logs, grad, gates, kept, grouped, scale, cosine, sine, after, before, out, grad_low, grad_q, grad_k, grad_v
):
    head = pl.program_id(0)
    total = kept.shape[0]
    half = KD // 2
    blocks = total // TILE
    for i in range(blocks):
        rows = slice(i * TILE, (i + 1) * TILE)
        gate, normed, given = gates[rows, :], grouped[rows, :], grad[rows, :]
        sigmoid = jax.nn.sigmoid(gate)
        out[rows, 2 * KD + VD :] = (
            given * normed * sigmoid * (1.0 + gate * (1.0 - sigmoid))
        ).astype(low)
        grad_low[rows, :] = norm_back(given * (gate * sigmoid), normed, scale[rows, :1]).astype(low)
    row, column = place_masks(TILE)
    base = jnp.exp((row - column).astype(f32) * logs[head])
    for i in range(blocks):
        rows = slice(i * TILE, (i + 1) * TILE)
        query, grad_rows = kept[rows, :KD], grad_low[rows, :]
        held = jnp.zeros((TILE, KD), f32)
        for j in range(i + 1):
            past = slice(j * TILE, (j + 1) * TILE)
            decay = block_decay(powers, head, i - j, base, row, column, after[rows, :], before[:, past])
            key, value = kept[past, KD : 2 * KD], kept[past, 2 * KD :]
            weights = (decay * dot_nt(query, key)).astype(low)
            grad_scores = (dot_nt(grad_rows, value) * decay).astype(low)
            held = held + dot(grad_scores, key)
            key_term, value_term = dot_tn(grad_scores, query), dot_tn(weights, grad_rows)
            if i == j:
                grad_k[past, :], grad_v[past, :] = key_term, value_term
            else:
                grad_k[past, :] += key_term
                grad_v[past, :] += value_term
        grad_q[rows, :] = held
    cos, sin = cosine[...], sine[...]
    for first, source, factor in ((0, grad_q, KD ** (-0.5)), (KD, grad_k, 1.0)):
        a, b = source[:, :half] * factor, source[:, half:] * factor
        out[:, first : first + half] = (a * cos + b * sin).astype(low)
        out[:, first + half : first + KD] = (b * cos - a * sin).astype(low)
    out[:, 2 * KD : 2 * KD + VD] = grad_v[...].astype(low)


def retain_back(grad, pre, kept, grouped, scale, consts, heads):
    total = pre.shape[0]
    powers, logs, cosine, sine, after, before = consts
    whole = lambda a: pl.BlockSpec(a.shape, lambda h: (0, 0))
    smem = pl.BlockSpec(memory_space=pltpu.SMEM)
    by_head = lambda width: pl.BlockSpec((total, width), lambda h: (0, h))
    return call(
        retain_back_kernel,
        (heads,),
        [smem, smem, by_head(VD), pl.BlockSpec((total, VD), lambda h: (0, 3 * h + 2))]
        + [by_head(2 * KD + VD), by_head(VD), by_head(128)]
        + [whole(cosine), whole(sine), whole(after), whole(before)],
        by_head(2 * KD + 2 * VD),
        jax.ShapeDtypeStruct((total, heads * (2 * KD + 2 * VD)), low),
        56,
        scratch=[
            pltpu.VMEM((total, VD), low),
            pltpu.VMEM((total, KD), f32),
            pltpu.VMEM((total, KD), f32),
            pltpu.VMEM((total, VD), f32),
        ],
    )(*consts[:2], grad, pre, kept, grouped, scale, *consts[2:])


def feed_kernel(feeds, steps, *refs):
    given, weights = refs[:4], refs[4 : 4 + 4 * feeds]
    outs = refs[4 + 4 * feeds : 4 + 7 * feeds]
    own, sent = refs[4 + 7 * feeds : 6 + 7 * feeds]
    rows, cots, held, grads, total, row_sems, sems = refs[6 + 7 * feeds :]
    count, width = rows.shape
    depth, size = width // 4, held.shape[2] // 3
    step = pl.program_id(0)

    def row_copies():
        places = [(buffer, first) for buffer in (rows, cots) for first in (0, count // 2)]
        return [
            pltpu.make_async_copy(ref, buffer.at[pl.ds(first, count // 2)], row_sems.at[i])
            for i, (ref, (buffer, first)) in enumerate(zip(given, places))
        ]

    def weight_copies(number, tile, slot):
        columns = weights[0].shape[1] // 3
        return [
            pltpu.make_async_copy(
                weights[4 * number + part].at[:, pl.ds(pl.multiple_of(kind * columns + tile * size, size), size)],
                held.at[slot, pl.ds(part * depth, depth), pl.ds(kind * size, size)],
                sems.at[slot, 4 * kind + part],
            )
            for kind in range(3)
            for part in range(4)
        ]

    def for_step(at, act):
        for number in range(feeds):

            @pl.when((at >= number * steps) & (at < (number + 1) * steps))
            def _(number=number):
                for copy in weight_copies(number, at - number * steps, lax.rem(at, 2)):
                    act(copy)

    @pl.when(step == 0)
    def _():
        for copy in row_copies():
            copy.start()
        for_step(step, lambda copy: copy.start())

    for_step(step + 1, lambda copy: copy.start())

    @pl.when(step == 0)
    def _():
        for copy in row_copies():
            copy.wait()

    for_step(step, lambda copy: copy.wait())
    weight = held.at[lax.rem(step, 2)]
    up = weight[:, : 2 * size]
    both, grad_hidden = dot(rows[...], up), dot(cots[...], weight[:, 2 * size :])
    act, lin = both[:, :size], both[:, size:]
    curve = jnp.tanh(gelu_slope * (act + gelu_cubic * act * act * act))
    gelu = 0.5 * act * (1.0 + curve)
    slope = 0.5 * (1.0 + curve) + (0.5 * gelu_slope) * act * (1.0 - curve * curve) * (
        1.0 + (3.0 * gelu_cubic) * act * act
    )
    hidden = (gelu * lin).astype(low)
    grads[:, :size] = (grad_hidden * lin * slope).astype(low)
    grads[:, size:] = (grad_hidden * gelu).astype(low)
    for number in range(feeds):

        @pl.when((step >= number * steps) & (step < (number + 1) * steps))
        def _(number=number):
            outs[3 * number][...] = hidden
            outs[3 * number + 1][...] = grads[:, :size]
            outs[3 * number + 2][...] = grads[:, size:]

    add = dot_nt(grads[...], up)

    @pl.when(step == 0)
    def _():
        total[...] = add

    @pl.when(step != 0)
    def _():
        total[...] += add

    @pl.when(step == pl.num_programs(0) - 1)
    def _():
        own[...] = total[: count // 2, :]
        sent[...] = total[count // 2 :, :].astype(low)


def feed(rows, cots, feeds):
    count, width = rows[0].shape
    columns = feeds[0][0].shape[1] // 3
    size = min(512, columns)
    steps, number = columns // size, len(feeds)
    full = pl.BlockSpec((count, width), lambda t: (0, 0))
    anywhere = pl.BlockSpec(memory_space=pl.ANY)
    tiles = [
        pl.BlockSpec((2 * count, size), lambda t, k=k: (0, jnp.clip(t - k * steps, 0, steps - 1)))
        for k in range(number)
    ]
    shape = jax.ShapeDtypeStruct((2 * count, columns), low)
    outs = call(
        functools.partial(feed_kernel, number, steps),
        (number * steps,),
        [anywhere] * (4 + 4 * number),
        [tile for tile in tiles for _ in range(3)] + [full, full],
        [shape] * (3 * number)
        + [jax.ShapeDtypeStruct((count, width), f32), jax.ShapeDtypeStruct((count, width), low)],
        56,
        scratch=[
            pltpu.VMEM((2 * count, width), low),
            pltpu.VMEM((2 * count, width), low),
            pltpu.VMEM((2, width, 3 * size), low),
            pltpu.VMEM((2 * count, 2 * size), low),
            pltpu.VMEM((2 * count, width), f32),
            pltpu.SemaphoreType.DMA((4,)),
            pltpu.SemaphoreType.DMA((2, 12)),
        ],
    )(*rows, *cots, *[part for weight in feeds for part in weight])
    return [outs[3 * k : 3 * k + 3] for k in range(number)], outs[-2], outs[-1]


def out_kernel(number, *refs):
    hiddens, weights, base = refs[:number], refs[number : 5 * number], refs[5 * number]
    own, sent = refs[5 * number + 1 :]
    half = own.shape[0]

    def give(part):
        total = sum(dot_nt(hiddens[i][...], weights[4 * i + part][...]) for i in range(number))
        own[...] = base[...] + total[:half]
        sent[...] = total[half:].astype(low)

    for part in range(4):
        pl.when(pl.program_id(0) == part)(functools.partial(give, part))


def out_rows(hiddens, feeds, base):
    count, width = base.shape
    columns = hiddens[0].shape[1]
    size = min(256, width // 4)
    steps = width // 4 // size
    tile = pl.BlockSpec((count, size), lambda i, j: (0, i * steps + j))
    return call(
        functools.partial(out_kernel, len(hiddens)),
        (4, steps),
        [pl.BlockSpec((2 * count, columns), lambda i, j: (0, 0))] * len(hiddens)
        + part_specs((size, columns), steps, 2) * len(hiddens)
        + [tile],
        [tile, tile],
        [jax.ShapeDtypeStruct((count, width), f32), jax.ShapeDtypeStruct((count, width), low)],
        56,
    )(*hiddens, *[weight for parts in feeds for weight in parts], base)


def gradient_kernel(plan, added, places, *refs):
    number = sum(pieces for pieces, _, _ in plan)
    lefts, rights = refs[:number], refs[number : number + sum(len(r) for _, r, _ in plan)]
    rest = refs[number + len(rights) :]
    came, outs, turned = rest[:added], rest[added:-1], rest[-1]
    step = pl.program_id(0)
    first = left_at = right_at = 0
    for pieces, lengths, size in plan:

        @pl.when(step == first)
        def _(left_at=left_at, pieces=pieces, size=size):
            for i in range(left_at, left_at + pieces):
                start = pl.multiple_of(places[i] * size, size) if pieces > 1 else 0
                turned[:, pl.ds(start, size)] = lefts[i][...].T

        for length in lengths:

            @pl.when((step >= first) & (step < first + length))
            def _(right=rights[right_at], depth=pieces * size):
                result = dot(turned[:, :depth], right[...])
                if added:
                    result = result + came[0][...].astype(f32)
                height = result.shape[0] // len(outs)
                for i, out in enumerate(outs):
                    out[...] = result[i * height : (i + 1) * height].astype(low)

            first, right_at = first + length, right_at + 1
        left_at += pieces


def weight_gradient(groups, side, came=None, pieces_out=4):
    width = groups[0][0][0].shape[1]
    half = width // 2
    count = max(pieces[0].shape[0] * len(pieces) for pieces, _, _ in groups)
    columns = sum(right.shape[1] for _, _, rights in groups for right in rights)
    size = min(512, min(right.shape[1] for _, _, rights in groups for right in rights))
    plan, lefts, rights, left_specs, right_specs, places, first = [], [], [], [], [], [], 0
    for pieces, at, given in groups:
        plan.append((len(pieces), [right.shape[1] // size for right in given], pieces[0].shape[0]))
        lefts += pieces
        places += at
        left_specs += [pl.BlockSpec((pieces[0].shape[0], half), lambda t, _: (0, side))] * len(pieces)
        for right in given:
            steps = right.shape[1] // size
            right_specs.append(
                pl.BlockSpec(
                    (right.shape[0], size),
                    lambda t, _, first=first, steps=steps: (0, jnp.clip(t - first, 0, steps - 1)),
                )
            )
            rights.append(right)
            first += steps
    parts = 1 if came is None else pieces_out
    tile = lambda height: pl.BlockSpec((height, size), lambda t, _: (0, t))
    more = [] if came is None else [came]
    outs = call(
        functools.partial(gradient_kernel, plan, len(more)),
        (columns // size,),
        left_specs + right_specs + [tile(half)] * len(more),
        [tile(half // parts)] * parts,
        [jax.ShapeDtypeStruct((half // parts, columns), low)] * parts,
        56,
        scratch=[pltpu.VMEM((half, count), low)],
        scalars=1,
    )(jnp.stack(places), *lefts, *rights, *more)
    return outs[0] if came is None else [outs[: parts // 2], outs[parts // 2 :]]


def shards(
    inputs,
    gain_attn,
    w_query,
    w_key,
    w_value,
    w_gate,
    w_out,
    gain_mlp,
    w_act,
    w_lin,
    w_down,
    cotangent,
    lengths,
    offsets,
):
    rows, width = inputs.shape
    dp_size, tensor_size = lax.axis_size("dp"), lax.axis_size("tensor")
    dp_own, tensor_own = lax.axis_index("dp"), lax.axis_index("tensor")
    total = rows * tensor_size
    heads = w_query.shape[1] // KD
    hidden_cols = w_act.shape[1]
    half = width // 2

    order = feature_order(dp_size)
    taken = jnp.array([k for k, _ in order], jnp.int32)
    parts = jnp.array([i for _, i in order], jnp.int32)
    table = (taken ^ dp_own) * 2 + parts
    place = {pair: i for i, pair in enumerate(order)}
    places = jnp.array([[place[k, i] for i in range(2)] for k in range(dp_size)], jnp.int32)
    back = places[jnp.arange(dp_size, dtype=jnp.int32) ^ dp_own].reshape(-1)

    x_low = reorder(inputs, table)
    normed_one = normed_rows(x_low)
    cot = reorder(cotangent, table)

    stride = 2 * KD + 2 * VD
    head_blocks = []
    for h in range(heads):
        head_blocks += [(w_query, h * KD, KD), (w_key, h * KD, KD)]
        head_blocks += [(w_value, h * VD, VD), (w_gate, h * VD, VD)]
    pair_blocks = range(0, tensor_size, 2)

    head_first = tensor_own * heads
    head_numbers = (head_first + jnp.arange(heads, dtype=jnp.int32)).astype(f32)
    log_decay = jnp.log(1.0 - jnp.exp2(-5.0 - head_numbers))
    segment, position = sequence_layout(lengths[0], offsets[0], total)
    cosine, sine = rotation(position, KD)
    powers = jnp.exp(
        jnp.arange(total // TILE, dtype=f32)[None, :] * TILE * log_decay[:, None]
    )
    consts = (powers, log_decay, cosine, sine, segment[:, None], segment[None, :])
    ring_places = [(tensor_own - step) % tensor_size for step in range(tensor_size)]

    gains = jnp.concatenate([gain_attn.reshape(2, -1), gain_mlp.reshape(2, -1)], axis=1)
    parts = [gains[:1], gains[1:]]
    for bits in dp_bits(dp_size):
        parts = [
            jnp.concatenate([part, swap(part, "dp", bit, "gains")], axis=0)
            for part, bit in zip(sync(*parts), bits)
        ]
    gains_same = jnp.concatenate(parts, axis=0)
    gains = jnp.concatenate([gains_same, swap(gains_same, "dp", 1, "gains")], axis=0).astype(f32)
    fine = gains.shape[1] // 2
    gain_one, gain_two = gains[:, :fine].reshape(-1), gains[:, fine:].reshape(-1)

    w_in = gather_step(tie(column_blocks(head_blocks), gains_same), 0, "w_in")
    feed_parts = column_blocks(
        [(w_act, 0, hidden_cols), (w_lin, 0, hidden_cols), (w_down.T, 0, hidden_cols)]
    )
    wo = column_blocks([(w_out.T, 0, w_out.shape[0])])

    def beside_attn(step, came):
        nonlocal w_in, wo, cot, feed_parts, consts
        if step == 1:
            came, w_in, wo, cot, feed_parts, consts = sync(came, w_in, wo, cot, feed_parts, consts)
            w_in = gather_rest(w_in, 1, "w_in", consts)
        return came

    pieces = gather_ring(normed_one, "rows_attn", beside_attn)
    rows_here, w_in, wo = sync(pieces[-1], w_in, wo)
    pieces[-1] = rows_here

    def swap_far(part):
        return {k: swap(part, "tensor", k, "w_feed_far") for k in pair_blocks[1:]}

    cot_came = swap(tie(cotangent, rows_here), "tensor", 1, "rows_cot")
    w_in = gather_core(w_in, "w_in")
    wo = gather_step(wo, 0, "w_out")
    h_pieces = [scale_rows(piece, gain_one) for piece in pieces]
    cot_came, wo, w_in, h_pieces, feed_parts = sync(cot_came, wo, w_in, h_pieces, feed_parts)

    upper = swap_far(feed_parts[0])
    wo = gather_rest(wo, 1, "w_out", upper)
    near_feed = gather_step(feed_parts, 0, "w_feed_near", upper)
    cots = [cot, reorder(cot_came, table)]
    pre = project(h_pieces[:-1], w_in, None, ring_places[:-1], tensor_size)
    pre = project(h_pieces[-1:], w_in, pre, ring_places[-1:], tensor_size)
    pre, upper, wo, near_feed, cots = sync(pre, upper, wo, near_feed, cots)

    lower = swap_far(tie(feed_parts[1], upper))
    wo = gather_core(wo, "w_out")
    near_feed = gather_rest(near_feed, 1, "w_feed_near", lower)
    mixed, kept, grouped, scale = retain(pre, consts, heads)
    sum_places = scatter_places()
    (total_out,) = terms(mixed, wo, sum_places[:1], rows, [low], None)
    rest_out = terms(tie(mixed, total_out), wo, sum_places[1:], rows, [f32] * (tensor_size - 1), None)
    total_out, lower, rest_out, near_feed = sync(total_out, lower, rest_out, near_feed)
    near_feed = gather_core(near_feed, "w_feed_near")
    far_feeds = {k: gather_step([upper[k], lower[k]], 0, "w_feed_far") for k in upper}

    def beside_out(step, total):
        nonlocal far_feeds
        if step == 1:
            total, far_feeds = sync(total, far_feeds)
            far_feeds = {k: gather_rest(v, 1, "w_feed_far") for k, v in far_feeds.items()}
        if step == tensor_size - 1:
            total, far_feeds = sync(total, far_feeds)
            far_feeds = {k: gather_core(v, "w_feed_far") for k, v in far_feeds.items()}
        return total

    attn_came, attn_own = scatter_ring(total_out, rest_out, "sum_attn", beside_out)

    middle, h_mlp = norm_rows(x_low, attn_came, attn_own, gain_two)
    h_came = swap(h_mlp, "tensor", 1, "rows_mlp")
    feeds = [near_feed] + [far_feeds[k] for k in pair_blocks[1:]]
    h_pair = [h_mlp, h_came]
    results, grad_h, grad_send = feed(h_pair, cots, feeds)
    grad_came = swap(grad_send, "tensor", 1, "sum_grad_mlp")

    late, late_rows, late_cots = tie((results, h_pair, cots), grad_send)
    pair_places = [jnp.zeros((), jnp.int32), jnp.ones((), jnp.int32)]

    def feed_groups(result):
        hidden, grad_act, grad_lin = result
        return [
            (late_rows, pair_places, [grad_act, grad_lin]),
            (late_cots, pair_places, [hidden]),
        ]

    far = {k: weight_gradient(feed_groups(late[k // 2]), 1) for k in pair_blocks[1:]}
    near_other = weight_gradient(feed_groups(late[0]), 1)
    grad_came, far, near_other = sync(grad_came, far, near_other)
    far_came = {k: swap(other, "dp", 1, "grad_feed_far") for k, other in far.items()}
    near_came = swap(near_other, "dp", 1, "grad_feed_near")
    grad_middle, gain_two_term, grad_mid_low = norm_back_rows(
        middle, cot, gain_two, grad_h, grad_came, True
    )

    grad_mixed = out_own = out_send = None
    mid_pieces = [grad_mid_low]

    def beside_mid(step, came):
        nonlocal far, near_came, grad_mixed, out_own, out_send
        if step == 1:
            late = tie(results, grad_mid_low)
            far = {
                k: weight_gradient(feed_groups(late[k // 2]), 0, far_came[k])
                for k in pair_blocks[1:]
            }
            came, far = sync(came, far)
            far = {k: scatter_step(v, 0, "grad_feed_far") for k, v in far.items()}
        if step == 2:
            late, weights = tie((results, feeds), mid_pieces[1])
            out_own, out_send = out_rows([result[0] for result in late], weights, middle)
            near_came = weight_gradient(feed_groups(late[0]), 0, near_came)
            came, out_own, out_send, near_came = sync(came, out_own, out_send, near_came)
        if step == tensor_size - 1:
            late = tie(mid_pieces, mid_pieces[-1])
            grad_mixed = project(late, wo, None, ring_places[:step], tensor_size)
            came, far, grad_mixed = sync(came, far, grad_mixed)
        mid_pieces.append(came)
        return came

    mid_pieces = gather_ring(grad_mid_low, "rows_grad_mid", beside_mid)
    out_came = swap(tie(out_send, mid_pieces[-1]), "tensor", 1, "sum_out")
    far = {k: scatter_rest(v, 1, "grad_feed_far") for k, v in far.items()}

    grad_mixed = project(mid_pieces[-1:], wo, grad_mixed, ring_places[-1:], tensor_size)
    grad_in = retain_back(grad_mixed, pre, kept, grouped, scale, consts, heads)

    grad_in, out_came, far, near = sync(grad_in, out_came, far, near_came)
    near = scatter_step(near, 0, "grad_feed_near")
    upper = {k: join(*parts[:2]) for k, parts in far.items()}
    lower = {k: join(*parts[2:]) for k, parts in far.items()}
    gain_places = [jnp.zeros((), jnp.int32)]
    gain_columns = jnp.eye(16, TILE, dtype=low)

    def out_groups(right):
        return [(mid_pieces, ring_places, [right]), ([gain_rows], gain_places, [gain_columns])]

    def swap_grad(parts):
        return {k: swap(part, "tensor", k, "grad_feed_far") for k, part in parts.items()}

    upper, lower_sent = swap_grad(upper), lower
    first_pairs, rest_pairs = h_pieces[1:2], h_pieces[2:] + h_pieces[:1]
    total_in, more = terms(grad_in, w_in, sum_places[:1], rows, [low], first_pairs)
    late_in = tie(grad_in, total_in)
    in_other = weight_gradient([(h_pieces, ring_places, [late_in])], 1)
    total_in, upper, in_other, near, lower_sent = sync(total_in, upper, in_other, near, lower_sent)
    lower = swap_grad(lower_sent)
    in_other = swap(in_other, "dp", 1, "grad_w_in")
    *rest_in, more_rest = terms(
        tie(grad_in, total_in), w_in, sum_places[1:], rows, [f32] * (tensor_size - 1), rest_pairs
    )
    late_in = tie(grad_in, more_rest)
    grads_in = weight_gradient([(h_pieces, ring_places, [late_in])], 0, in_other, 8)
    near = scatter_step(near, 1, "grad_feed_near", grads_in)
    total_in, lower, rest_in, grads_in, near = sync(total_in, lower, rest_in, grads_in, near)
    first_bits = dp_bits(dp_size)[-1]
    sent_on = [
        swap(part[3], "dp", bit, "grad_w_in") for part, bit in zip(grads_in, first_bits)
    ]
    gain_rows = jnp.concatenate(
        [(more + more_rest) / gain_one, gain_two_term, jnp.zeros((14, width), f32)], axis=0
    ).astype(low)
    out_other = weight_gradient(out_groups(tie(mixed, total_in)), 1)
    grads_out = None

    def beside_sum(step, total):
        nonlocal grads_in, grads_out, out_other, sent_on
        if step == 1:
            total, out_other, sent_on = sync(total, out_other, sent_on)
            kept_on = [
                swap(part[2], "dp", bit, "grad_w_in") for part, bit in zip(grads_in, first_bits)
            ]
            out_other = swap(out_other, "dp", 1, "grad_w_out")
            grads_in, sent_on, kept_on = tie((grads_in, sent_on, kept_on), total)
            grads_out = weight_gradient(out_groups(mixed), 0, out_other)
            sent_on = [
                add_rows(part[1], came, low) for part, came in zip(grads_in, sent_on)
            ]
            grads_in = [
                [add_rows(part[0], came, low), sent]
                for part, came, sent in zip(grads_in, kept_on, sent_on)
            ]
        if step == 2:
            total, grads_in, grads_out = sync(total, grads_in, grads_out)
            grads_in = scatter_rest(grads_in, 1, "grad_w_in")
            grads_out = scatter_rest(grads_out, 0, "grad_w_out")
        return total

    hattn_came, hattn_own = scatter_ring(total_in, rest_in, "sum_grad_attn", beside_sum)
    near = scatter_rest(near, 2, "grad_feed_near")
    grad_out_own = jnp.concatenate(grads_out, axis=0).astype(f32)
    columns = w_out.shape[0]
    grad_wo_own, gain_sum = grad_out_own[:, :columns], grad_out_own[:, columns : columns + 128]
    hattn_came, gain_sum = sync(hattn_came, gain_sum)
    for b in range(tensor_size.bit_length() - 1):
        gain_sum = gain_sum + swap(gain_sum, "tensor", 1 << b, "gains")
    grad_in_own = jnp.concatenate(grads_in, axis=0).astype(f32)
    grad_feed = jnp.concatenate(near, axis=0).astype(f32)
    for k in pair_blocks[1:]:
        grad_feed = grad_feed + jnp.concatenate([upper[k], lower[k]], axis=0).astype(f32)
    outputs = out_own + out_came.astype(f32)
    (grad_inputs,) = norm_back_rows(x_low, grad_middle, gain_one, hattn_own, hattn_came, False)

    def heads_back(first, size):
        return jnp.concatenate(
            [grad_in_own[:, h * stride + first : h * stride + first + size] for h in range(heads)],
            axis=1,
        )

    return (
        reorder(outputs.astype(low), back),
        reorder(grad_inputs, back),
        gain_sum[:, 0],
        heads_back(0, KD),
        heads_back(KD, KD),
        heads_back(2 * KD, VD),
        heads_back(2 * KD + VD, VD),
        grad_wo_own.T,
        gain_sum[:, 1],
        grad_feed[:, :hidden_cols],
        grad_feed[:, hidden_cols : 2 * hidden_cols],
        grad_feed[:, 2 * hidden_cols :].T,
    )


def solution(mesh):
    return jax.shard_map(
        shards,
        mesh=mesh,
        in_specs=(
            P(("dp", "tensor"), None),
            P("dp"),
            P("dp", "tensor"),
            P("dp", "tensor"),
            P("dp", "tensor"),
            P("dp", "tensor"),
            P("tensor", "dp"),
            P("dp"),
            P("dp", "tensor"),
            P("dp", "tensor"),
            P("tensor", "dp"),
            P(("dp", "tensor"), None),
            P("dp", None),
            P("dp", None),
        ),
        out_specs=(
            P(("dp", "tensor"), None),
            P(("dp", "tensor"), None),
            P("dp"),
            P("dp", "tensor"),
            P("dp", "tensor"),
            P("dp", "tensor"),
            P("dp", "tensor"),
            P("tensor", "dp"),
            P("dp"),
            P("dp", "tensor"),
            P("dp", "tensor"),
            P("tensor", "dp"),
        ),
        check_vma=False,
    )
```

time: 780 us -> 699 us (0.90); the launches traced: 764 us -> 693 us
  other arithmetic: 76.4 us -> 14.6 us
  Pallas kernels: 240 us -> 300 us
  waiting for transfers between devices: 337 us -> 277 us
  matrix products: 14.3 us -> 0 us
  local copies, waits for them, and re-layouts: 35.6 us -> 43.8 us
    ppermute x60 -> x61, waiting for transfers between devices: 261 us -> 165 us  [swap(): return lax.ppermute(values, axis, [(i, i ^ bits) for i in range(size)])]
    pallas_call x9 -> x57, Pallas kernels: 96 us -> 137 us  [the longest x4 44.7 us: terms(): call(functools.partial(terms_kernel, number, paired), (4, steps), rows +...]
    ppermute x12, waiting for transfers between devices: 76.1 us -> 111 us  [shift(): lax.ppermute(values, axis, [(i, (i + step) % size) for i in range(size)])]
    concatenate x21 -> x4, other arithmetic: 30 us -> 0.74 us  [the longest x1 0.7 us: shards(): jnp.concatenate([(more + more_rest) / gain_one, gain_two_term, jnp.zeros(...]
    convert_element_type x22 -> x1, other arithmetic: 24.4 us -> 0.6 us  [shards(): gain_columns = jnp.eye(16, TILE, dtype=low)]
    unnamed x146 -> x180, local copies, waits for them, and re-layouts: 19.8 us -> 38.8 us
    dot_general x4 -> x0, matrix products: 14.3 us -> none  [dot_nt(): lax.dot_general(left, right, (((1,), (1,)), ((), ())), preferred_element_...]
    slice x12 -> x2, local copies, waits for them, and re-layouts: 11.8 us -> 0.8 us  [the longest x1 0.79 us: shards(): gain_sum[:, 1]]
  transfers between devices with their start and end apart: 72 -> 73, of which waited for: 41 -> 37; matrix products, arithmetic and copies ran while one was open for 14% -> 4% of each run, Pallas kernels for 28% -> 36%
where the time goes in v2:
time: 699 us; the launch traced here: 693 us
  Pallas kernels  300 us (43%)
  waiting for transfers between devices  277 us (40%)
  starting transfers between devices  55.7 us (8%)
  local copies, waits for them, and re-layouts  43.8 us (6%)
  other arithmetic  14.6 us (2%)
    ppermute x61, waiting for transfers between devices, swap(): return lax.ppermute(values, axis, [(i, i ^ bits) for i in range(size)])  165 us
    ppermute x12, waiting for transfers between devices, shift(): lax.ppermute(values, axis, [(i, (i + step) % size) for i in range(size)])  111 us
    pallas_call x8, Pallas kernels, weight_gradient(): call(functools.partial(gradient_kernel, plan, len(more)), (columns // siz...  85.7 us
    ppermute x61, starting transfers between devices, swap(): return lax.ppermute(values, axis, [(i, i ^ bits) for i in range(size)])  51.4 us
    pallas_call x4, Pallas kernels, terms(): call(functools.partial(terms_kernel, number, paired), (4, steps), rows +...  44.7 us
    pallas_call x4, Pallas kernels, project(): call(functools.partial(project_kernel, number), (columns // size,), [rows...  39.1 us
    unnamed x180, local copies, waits for them, and re-layouts  38.8 us
    pallas_call x1, Pallas kernels, feed(): call(functools.partial(feed_kernel, number, steps), (number * steps,), [a...  33.5 us
  transfers between devices with their start and end apart: 73, of which 37 were waited for; matrix products, arithmetic and copies ran while one was open for 4% of the time, Pallas kernels for 36%

profile of v2, /device:TPU:0, one launch (start us, length us, event | category | flops | bytes accessed | tf_op | source)
XLA Modules:
  0.0 692.7 jit_solution(7050914284834290326)
XLA Ops:
  29.8 11.8 %collective-permute-done.6.refs_1_ = bf16[128,3072]{1,0:T(8,128)(2,1)S(1)} collective-permute-done((bf16[128,3072]{1,0:T(8,128)(2,1)S(1)}, bf16[128,3072]{1,0:T(8,128)(2,1)S(1)}, u32[]{:S(2)}, u32[]{:S(2)}) %collective-permute-start.6) | collective-permute-done | bytes 786464 | tf_op jit(solution)/shard_map/w_in_dp4/ppermute | solution.py:66
  46.6 20.7 %collective-permute-done.7.rows = bf16[256,2048]{1,0:T(8,128)(2,1)S(1)} collective-permute-done((bf16[256,2048]{1,0:T(8,128)(2,1)}, bf16[256,2048]{1,0:T(8,128)(2,1)S(1)}, u32[]{:S(2)}, u32[]{:S(2)}) %collective-permute-start.7) | collective-permute-done | bytes 1048608 | tf_op jit(solution)/shard_map/rows_attn_2/ppermute | solution.py:72
  67.6 10.2 %collective-permute-done.10.refs_1_ = bf16[256,3072]{1,0:T(8,128)(2,1)S(1)} collective-permute-done((bf16[256,3072]{1,0:T(8,128)(2,1)S(1)}, bf16[256,3072]{1,0:T(8,128)(2,1)S(1)}, u32[]{:S(2)}, u32[]{:S(2)}) %collective-permute-start.10) | collective-permute-done | bytes 1572896 | tf_op jit(solution)/shard_map/w_in_dp2/ppermute | solution.py:66
  81.2 9.5 %collective-permute-done.8.rows = bf16[256,2048]{1,0:T(8,128)(2,1)S(1)} collective-permute-done((bf16[256,2048]{1,0:T(8,128)(2,1)S(1)}, bf16[256,2048]{1,0:T(8,128)(2,1)S(1)}, u32[]{:S(2)}, u32[]{:S(2)}) %collective-permute-start.8) | collective-permute-done | bytes 1048608 | tf_op jit(solution)/shard_map/rows_attn_3/ppermute | solution.py:72
  93.2 8.5 %collective-permute-done.16 = bf16[8,256]{1,0:T(8,128)(2,1)S(1)} collective-permute-done((bf16[8,256]{1,0:T(8,128)(2,1)S(1)}, bf16[8,256]{1,0:T(8,128)(2,1)S(1)}, u32[]{:S(2)}, u32[]{:S(2)}) %collective-permute-start.16) | collective-permute-done | bytes 4128 | tf_op jit(solution)/shard_map/gains_dp1/ppermute | solution.py:66
  126.2 16.7 %shard_map.272.refs_5_ = f32[1024,3072]{1,0:T(8,128)} custom-call(s32[3]{0:T(128)} %pad_add_fusion.places, bf16[256,2048]{1,0:T(8,128)(2,1)} %copy-done.9, bf16[256,2048]{1,0:T(8,128)(2,1)} %copy-done.10, bf16[256,2048]{1,0:T(8,128)(2,1)} %copy-done.11, bf16[512,3072]{1,0:T(8,128)(2,1)} %shard_map.264.refs_3_.refs_1_, bf16[512,3072]{1,0:T(8,128)(2,1)} %copy-done, ...), custom_call_target="tpu_custom_call" | custom-call | tf_op jit(solution)/shard_map/pallas_call | solution.py:318
  142.9 9.7 %shard_map.273.pre.gates = f32[1024,3072]{1,0:T(8,128)} custom-call(s32[1]{0:T(128)} %bitcast.10.places, bf16[256,2048]{1,0:T(8,128)(2,1)} %copy-done.8, bf16[512,3072]{1,0:T(8,128)(2,1)} %shard_map.264.refs_3_.refs_1_, bf16[512,3072]{1,0:T(8,128)(2,1)} %copy-done, ...), custom_call_target="tpu_custom_call", output_to_operand_aliasing={{}: (6, {})} | custom-call | tf_op jit(solution)/shard_map/pallas_call | solution.py:318
  168.7 10.4 %shard_map.279 = (bf16[1024,1024]{1,0:T(8,128)(2,1)}, bf16[1024,2048]{1,0:T(8,128)(2,1)}, f32[1024,1024]{1,0:T(8,128)}, f32[1024,256]{1,0:T(8,128)}) custom-call(f32[2,4]{1,0:T(2,128)} %multiply_exponential_fusion.powers, f32[2]{0:T(128)} %copy-done.85, f32[1024,3072]{1,0:T(8,128)} %shard_map.273.pre.gates, f32[1024,128]{1,0:T(8,128)} %get-tuple-element.351.cosine, ...), custom_call_target="tpu_custom_call" | custom-call | tf_op jit(solution)/shard_map/pallas_call | solution.py:496
  184.4 8.8 %shard_map.281 = (f32[256,2048]{1,0:T(8,128)}, f32[256,2048]{1,0:T(8,128)}, f32[256,2048]{1,0:T(8,128)}) custom-call(s32[3]{0:T(128)} %pad_add_fusion.1.places, bf16[1024,1024]{1,0:T(8,128)(2,1)} %get-tuple-element.581.refs_0_.refs_1_.refs_2_.refs_5_, bf16[1024,1024]{1,0:T(8,128)(2,1)} %get-tuple-element.581.refs_0_.refs_1_.refs_2_.refs_5_, ...), custom_call_target="tpu_custom_call" | custom-call | tf_op jit(solution)/shard_map/pallas_call | solution.py:368
  193.2 8.9 %collective-permute-done.24.refs_0_ = bf16[128,3072]{1,0:T(8,128)(2,1)} collective-permute-done((bf16[128,3072]{1,0:T(8,128)(2,1)}, bf16[128,3072]{1,0:T(8,128)(2,1)}, u32[]{:S(2)}, u32[]{:S(2)}) %collective-permute-start.24) | collective-permute-done | bytes 786464 | tf_op jit(solution)/shard_map/w_feed_far_tensor2/ppermute | solution.py:66
  210.4 17.2 %collective-permute-done.29.refs_1_ = bf16[128,3072]{1,0:T(8,128)(2,1)S(1)} collective-permute-done((bf16[128,3072]{1,0:T(8,128)(2,1)}, bf16[128,3072]{1,0:T(8,128)(2,1)S(1)}, u32[]{:S(2)}, u32[]{:S(2)}) %collective-permute-start.29) | collective-permute-done | bytes 786464 | tf_op jit(solution)/shard_map/w_feed_far_dp4/ppermute | solution.py:66
  237.6 23.4 %collective-permute-done.30.left = bf16[256,2048]{1,0:T(8,128)(2,1)S(1)} collective-permute-done((bf16[256,2048]{1,0:T(8,128)(2,1)S(1)}, bf16[256,2048]{1,0:T(8,128)(2,1)S(1)}, u32[]{:S(2)}, u32[]{:S(2)}) %collective-permute-start.30) | collective-permute-done | bytes 1048608 | tf_op jit(solution)/shard_map/sum_attn_2/ppermute | solution.py:72
  261.9 8.6 %collective-permute-done.33.refs_1_ = bf16[256,3072]{1,0:T(8,128)(2,1)S(1)} collective-permute-done((bf16[256,3072]{1,0:T(8,128)(2,1)S(1)}, bf16[256,3072]{1,0:T(8,128)(2,1)S(1)}, u32[]{:S(2)}, u32[]{:S(2)}) %collective-permute-start.33) | collective-permute-done | bytes 1572896 | tf_op jit(solution)/shard_map/w_feed_far_dp2/ppermute | solution.py:66
  272.0 14.3 %collective-permute-done.31.came = bf16[256,2048]{1,0:T(8,128)(2,1)S(1)} collective-permute-done((bf16[256,2048]{1,0:T(8,128)(2,1)S(1)}, bf16[256,2048]{1,0:T(8,128)(2,1)S(1)}, u32[]{:S(2)}, u32[]{:S(2)}) %collective-permute-start.31) | collective-permute-done | bytes 1048608 | tf_op jit(solution)/shard_map/sum_attn_3/ppermute | solution.py:72
  290.7 25.1 %collective-permute-done.34.refs_1_ = bf16[256,2048]{1,0:T(8,128)(2,1)S(1)} collective-permute-done((bf16[256,2048]{1,0:T(8,128)(2,1)S(1)}, bf16[256,2048]{1,0:T(8,128)(2,1)S(1)}, u32[]{:S(2)}, u32[]{:S(2)}) %collective-permute-start.34) | collective-permute-done | bytes 1048608 | tf_op jit(solution)/shard_map/rows_mlp_tensor1/ppermute | solution.py:66
  316.8 33.5 %shard_map.291 = (bf16[512,1024]{1,0:T(8,128)(2,1)}, bf16[512,1024]{1,0:T(8,128)(2,1)}, bf16[512,1024]{1,0:T(8,128)(2,1)}, bf16[512,1024]{1,0:T(8,128)(2,1)}, bf...) custom-call(bf16[256,2048]{1,0:T(8,128)(2,1)} %copy-done.14, ...), custom_call_target="tpu_custom_call" | custom-call | tf_op jit(solution)/shard_map/pallas_call | solution.py:671
  350.6 9.8 %shard_map.293 = bf16[1024,3072]{1,0:T(8,128)(2,1)} custom-call(s32[4]{0:T(128)} %constant.90.clone.1.places, bf16[256,2048]{1,0:T(8,128)(2,1)} %copy-done.14, bf16[256,2048]{1,0:T(8,128)(2,1)} %copy-done.71, bf16[256,2048]{1,0:T(8,128)(2,1)} %copy-done.1, bf16[256,2048]{1,0:T(8,128)(2,1)} %copy-done.3, bf16[512,1024]{1,0:T(8,128)(2,1)} %get-tuple-element.477.refs_4_, ...), custom_call_target="tpu_custom_call" | custom-call | tf_op jit(solution)/shard_map/pallas_call | solution.py:779
  360.4 10.4 %shard_map.292 = bf16[1024,3072]{1,0:T(8,128)(2,1)} custom-call(s32[4]{0:T(128)} %constant.90.clone.1.places, bf16[256,2048]{1,0:T(8,128)(2,1)} %copy-done.14, bf16[256,2048]{1,0:T(8,128)(2,1)} %copy-done.71, bf16[256,2048]{1,0:T(8,128)(2,1)} %copy-done.1, bf16[256,2048]{1,0:T(8,128)(2,1)} %copy-done.3, bf16[512,1024]{1,0:T(8,128)(2,1)} %get-tuple-element.456.refs_4_, ...), custom_call_target="tpu_custom_call" | custom-call | tf_op jit(solution)/shard_map/pallas_call | solution.py:779
  385.2 11.2 %shard_map.295 = (bf16[256,3072]{1,0:T(8,128)(2,1)}, bf16[256,3072]{1,0:T(8,128)(2,1)}, bf16[256,3072]{1,0:T(8,128)(2,1)}, bf16[256,3072]{1,0:T(8,128)(2,1)}) custom-call(s32[4]{0:T(128)} %constant.90.clone.1.places, bf16[256,2048]{1,0:T(8,128)(2,1)} %copy-done.14, bf16[256,2048]{1,0:T(8,128)(2,1)} %copy-done.71, bf16[256,2048]{1,0:T(8,128)(2,1)} %copy-done.1, ...), custom_call_target="tpu_custom_call" | custom-call | tf_op jit(solution)/shard_map/pallas_call | solution.py:779
  396.4 8.8 %collective-permute-done.40.refs_1_ = bf16[256,2048]{1,0:T(8,128)(2,1)S(1)} collective-permute-done((bf16[256,2048]{1,0:T(8,128)(2,1)S(1)}, bf16[256,2048]{1,0:T(8,128)(2,1)S(1)}, u32[]{:S(2)}, u32[]{:S(2)}) %collective-permute-start.40) | collective-permute-done | bytes 1048608 | tf_op jit(solution)/shard_map/rows_grad_mid_1/ppermute | solution.py:72
  407.9 12.0 %shard_map.296 = (f32[256,2048]{1,0:T(8,128)}, bf16[256,2048]{1,0:T(8,128)(2,1)}) custom-call(bf16[512,1024]{1,0:T(8,128)(2,1)} %get-tuple-element.465.refs_6_.refs_0_, bf16[512,1024]{1,0:T(8,128)(2,1)} %get-tuple-element.466.refs_6_.refs_1_, bf16[512,3072]{1,0:T(8,128)(2,1)} %copy-done.5, bf16[512,3072]{1,0:T(8,128)(2,1)} %copy-done.4, ...), custom_call_target="tpu_custom_call" | custom-call | tf_op jit(solution)/shard_map/pallas_call | solution.py:712
  419.9 11.0 %shard_map.297 = (bf16[256,3072]{1,0:T(8,128)(2,1)}, bf16[256,3072]{1,0:T(8,128)(2,1)}, bf16[256,3072]{1,0:T(8,128)(2,1)}, bf16[256,3072]{1,0:T(8,128)(2,1)}) custom-call(s32[4]{0:T(128)} %constant.90.clone.1.places, bf16[256,2048]{1,0:T(8,128)(2,1)} %copy-done.14, bf16[256,2048]{1,0:T(8,128)(2,1)} %copy-done.71, bf16[256,2048]{1,0:T(8,128)(2,1)} %copy-done.1, ...), custom_call_target="tpu_custom_call" | custom-call | tf_op jit(solution)/shard_map/pallas_call | solution.py:779
  443.1 13.6 %collective-permute-done.44.refs_0_.refs_3_ = bf16[256,2048]{1,0:T(8,128)(2,1)} collective-permute-done((bf16[256,2048]{1,0:T(8,128)(2,1)S(1)}, bf16[256,2048]{1,0:T(8,128)(2,1)}, u32[]{:S(2)}, u32[]{:S(2)}) %collective-permute-start.44) | collective-permute-done | bytes 1048608 | tf_op jit(solution)/shard_map/rows_grad_mid_3/ppermute | solution.py:72
  464.2 16.9 %shard_map.302.refs_0_.refs_4_.refs_1_.refs_2_ = bf16[1024,3072]{1,0:T(8,128)(2,1)} custom-call(f32[2,4]{1,0:T(2,128)} %multiply_exponential_fusion.powers, f32[2]{0:T(128)} %copy-done.85, f32[1024,1024]{1,0:T(8,128)} %shard_map.301.grad, f32[1024,3072]{1,0:T(8,128)} %shard_map.273.pre.gates, bf16[1024,2048]{1,0:T(8,128)(2,1)} %get-tuple-element.503.kept, ...), custom_call_target="tpu_custom_call" | custom-call | tf_op jit(solution)/shard_map/pallas_call | solution.py:555
  485.8 11.7 %shard_map.306 = (bf16[256,2048]{1,0:T(8,128)(2,1)}, f32[1,2048]{1,0:T(1,128)}) custom-call(s32[1]{0:T(128)} %bitcast.1.places, bf16[1024,3072]{1,0:T(8,128)(2,1)} %shard_map.302.refs_0_.refs_4_.refs_1_.refs_2_, bf16[512,3072]{1,0:T(8,128)(2,1)} %shard_map.264.refs_3_.refs_1_, bf16[512,3072]{1,0:T(8,128)(2,1)} %copy-done, ...), custom_call_target="tpu_custom_call" | custom-call | tf_op jit(solution)/shard_map/pallas_call | solution.py:368
  497.6 12.7 %shard_map.308 = bf16[1024,3072]{1,0:T(8,128)(2,1)} custom-call(s32[4]{0:T(128)} %pad_add_fusion.2.places, bf16[256,2048]{1,0:T(8,128)(2,1)} %copy-done.9, bf16[256,2048]{1,0:T(8,128)(2,1)} %copy-done.10, bf16[256,2048]{1,0:T(8,128)(2,1)} %copy-done.11, bf16[256,2048]{1,0:T(8,128)(2,1)} %copy-done.8, ...), custom_call_target="tpu_custom_call" | custom-call | tf_op jit(solution)/shard_map/pallas_call | solution.py:779
  519.9 18.9 %shard_map.312 = (f32[256,2048]{1,0:T(8,128)}, f32[256,2048]{1,0:T(8,128)}, f32[256,2048]{1,0:T(8,128)}, f32[1,2048]{1,0:T(1,128)}) custom-call(s32[3]{0:T(128)} %pad_add_fusion.1.places, bf16[1024,3072]{1,0:T(8,128)(2,1)} %shard_map.302.refs_0_.refs_4_.refs_1_.refs_2_, bf16[1024,3072]{1,0:T(8,128)(2,1)} %shard_map.302.refs_0_.refs_4_.refs_1_.refs_2_, ...), custom_call_target="tpu_custom_call" | custom-call | tf_op jit(solution)/shard_map/pallas_call | solution.py:368
  538.9 13.7 %shard_map.313 = (bf16[128,3072]{1,0:T(8,128)(2,1)}, bf16[128,3072]{1,0:T(8,128)(2,1)}, bf16[128,3072]{1,0:T(8,128)(2,1)}, bf16[128,3072]{1,0:T(8,128)(2,1)}, bf...) custom-call(s32[4]{0:T(128)} %pad_add_fusion.2.places, ...), custom_call_target="tpu_custom_call" | custom-call | tf_op jit(solution)/shard_map/pallas_call | solution.py:779
  569.4 14.4 %collective-permute-done.57.left = bf16[256,2048]{1,0:T(8,128)(2,1)S(1)} collective-permute-done((bf16[256,2048]{1,0:T(8,128)(2,1)}, bf16[256,2048]{1,0:T(8,128)(2,1)S(1)}, u32[]{:S(2)}, u32[]{:S(2)}) %collective-permute-start.57) | collective-permute-done | bytes 1048608 | tf_op jit(solution)/shard_map/sum_grad_attn_1/ppermute | solution.py:72
  588.7 17.2 %collective-permute-done.61.right = bf16[128,3072]{1,0:T(8,128)(2,1)S(1)} collective-permute-done((bf16[128,3072]{1,0:T(8,128)(2,1)}, bf16[128,3072]{1,0:T(8,128)(2,1)S(1)}, u32[]{:S(2)}, u32[]{:S(2)}) %collective-permute-start.61) | collective-permute-done | bytes 786464 | tf_op jit(solution)/shard_map/grad_w_in_dp4/ppermute | solution.py:66
  615.5 8.8 %shard_map.323 = (bf16[256,1280]{1,0:T(8,128)(2,1)}, bf16[256,1280]{1,0:T(8,128)(2,1)}, bf16[256,1280]{1,0:T(8,128)(2,1)}, bf16[256,1280]{1,0:T(8,128)(2,1)}) custom-call(s32[5]{0:T(128)} %stack.26.places, bf16[256,2048]{1,0:T(8,128)(2,1)} %copy-done.18, bf16[256,2048]{1,0:T(8,128)(2,1)} %copy-done.72, bf16[256,2048]{1,0:T(8,128)(2,1)} %copy-done.73, ...), custom_call_target="tpu_custom_call" | custom-call | tf_op jit(solution)/shard_map/pallas_call | solution.py:779
  637.0 21.0 %collective-permute-done.66.right = bf16[256,1280]{1,0:T(8,128)(2,1)} collective-permute-done((bf16[256,1280]{1,0:T(8,128)(2,1)}, bf16[256,1280]{1,0:T(8,128)(2,1)}, u32[]{:S(2)}, u32[]{:S(2)}) %collective-permute-start.66) | collective-permute-done | bytes 655392 | tf_op jit(solution)/shard_map/grad_w_out_dp2/ppermute | solution.py:66
  (414 shorter events, 240.9 us)
Async XLA Ops:
  10.4 32.5 %collective-permute-start = (bf16[256,2048]{1,0:T(8,128)(2,1)S(1)}, bf16[256,2048]{1,0:T(8,128)(2,1)}, u32[]{:S(2)}, u32[]{:S(2)}) collective-permute-start(bf16[256,2048]{1,0:T(8,128)(2,1)S(1)} %shard_map.257.rows), channel_id=1, source_target_pairs={{0,1},{1,2},{2,3},{3,0},{4,5},{5,6},{6,7},{7,4},{8,9},{9,10},{10,1... | collective-permute-start | bytes 3145736 | tf_op jit(solution)/shard_map/rows_attn_1/ppermute | solution.py:72
  44.6 33.2 %collective-permute-start.10 = (bf16[256,3072]{1,0:T(8,128)(2,1)S(1)}, bf16[256,3072]{1,0:T(8,128)(2,1)S(1)}, u32[]{:S(2)}, u32[]{:S(2)}) collective-permute-start(bf16[256,3072]{1,0:T(8,128)(2,1)S(1)} %shard_map.260.refs_0_), channel_id=1, source_target_pairs={{0,8},{4,12},{8,0},{12,4},{16,24},{20,28},{24,16},{28,20},{1,9},{5... | collective-permute-start | bytes 4718600 | tf_op jit(solution)/shard_map/w_in_dp2/ppermute | solution.py:66
  46.1 33.0 %collective-permute-start.9 = (bf16[256,3072]{1,0:T(8,128)(2,1)S(1)}, bf16[256,3072]{1,0:T(8,128)(2,1)S(1)}, u32[]{:S(2)}, u32[]{:S(2)}) collective-permute-start(bf16[256,3072]{1,0:T(8,128)(2,1)S(1)} %shard_map.259.refs_0_), channel_id=1, source_target_pairs={{0,16},{4,20},{8,24},{12,28},{16,0},{20,4},{24,8},{28,12},{1,17},{... | collective-permute-start | bytes 4718600 | tf_op jit(solution)/shard_map/w_in_dp4/ppermute | solution.py:66
  117.6 35.0 %collective-permute-start.20 = (bf16[128,3072]{1,0:T(8,128)(2,1)}, bf16[128,3072]{1,0:T(8,128)(2,1)S(1)}, u32[]{:S(2)}, u32[]{:S(2)}) collective-permute-start(bf16[128,3072]{1,0:T(8,128)(2,1)} %get-tuple-element.387.refs_0_), channel_id=1, source_target_pairs={{0,8},{4,12},{8,0},{12,4},{16,24},{20,28},{24,16},{28,20},{1,9},{5... | collective-permute-start | bytes 2359304 | tf_op jit(solution)/shard_map/w_feed_near_dp2/ppermute | solution.py:66
  119.1 33.4 %collective-permute-start.21 = (bf16[128,3072]{1,0:T(8,128)(2,1)}, bf16[128,3072]{1,0:T(8,128)(2,1)S(1)}, u32[]{:S(2)}, u32[]{:S(2)}) collective-permute-start(bf16[128,3072]{1,0:T(8,128)(2,1)} %get-tuple-element.388.refs_0_), channel_id=1, source_target_pairs={{0,16},{4,20},{8,24},{12,28},{16,0},{20,4},{24,8},{28,12},{1,17},{... | collective-permute-start | bytes 2359304 | tf_op jit(solution)/shard_map/w_feed_near_dp4/ppermute | solution.py:66
  120.1 36.0 %collective-permute-start.17 = (bf16[128,3072]{1,0:T(8,128)(2,1)}, bf16[128,3072]{1,0:T(8,128)(2,1)S(1)}, u32[]{:S(2)}, u32[]{:S(2)}) collective-permute-start(bf16[128,3072]{1,0:T(8,128)(2,1)} %get-tuple-element.379), channel_id=1, source_target_pairs={{0,2},{1,3},{2,0},{3,1},{4,6},{5,7},{6,4},{7,5},{8,10},{9,11},{10,... | collective-permute-start | bytes 2359304 | tf_op jit(solution)/shard_map/w_feed_far_tensor2/ppermute | solution.py:66
  120.1 40.8 %collective-permute-start.18 = (bf16[256,1024]{1,0:T(8,128)(2,1)}, bf16[256,1024]{1,0:T(8,128)(2,1)S(1)}, u32[]{:S(2)}, u32[]{:S(2)}) collective-permute-start(bf16[256,1024]{1,0:T(8,128)(2,1)} %shard_map.266.refs_0_), channel_id=1, source_target_pairs={{0,16},{4,20},{8,24},{12,28},{16,0},{20,4},{24,8},{28,12},{1,17},{... | collective-permute-start | bytes 1572872 | tf_op jit(solution)/shard_map/w_out_dp4/ppermute | solution.py:66
  121.2 40.6 %collective-permute-start.19 = (bf16[256,1024]{1,0:T(8,128)(2,1)}, bf16[256,1024]{1,0:T(8,128)(2,1)}, u32[]{:S(2)}, u32[]{:S(2)}) collective-permute-start(bf16[256,1024]{1,0:T(8,128)(2,1)} %shard_map.267.refs_0_), channel_id=1, source_target_pairs={{0,8},{4,12},{8,0},{12,4},{16,24},{20,28},{24,16},{28,20},{1,9},{5... | collective-permute-start | bytes 1572872 | tf_op jit(solution)/shard_map/w_out_dp2/ppermute | solution.py:66
  164.7 37.4 %collective-permute-start.25 = (bf16[256,3072]{1,0:T(8,128)(2,1)}, bf16[256,3072]{1,0:T(8,128)(2,1)}, u32[]{:S(2)}, u32[]{:S(2)}) collective-permute-start(bf16[256,3072]{1,0:T(8,128)(2,1)} %shard_map.276.refs_0_), channel_id=1, source_target_pairs={{0,16},{4,20},{8,24},{12,28},{16,0},{20,4},{24,8},{28,12},{1,17},{... | collective-permute-start | bytes 4718600 | tf_op jit(solution)/shard_map/w_feed_near_dp4/ppermute | solution.py:66
  165.8 36.3 %collective-permute-start.26 = (bf16[256,3072]{1,0:T(8,128)(2,1)}, bf16[256,3072]{1,0:T(8,128)(2,1)}, u32[]{:S(2)}, u32[]{:S(2)}) collective-permute-start(bf16[256,3072]{1,0:T(8,128)(2,1)} %shard_map.277.refs_0_), channel_id=1, source_target_pairs={{0,8},{4,12},{8,0},{12,4},{16,24},{20,28},{24,16},{28,20},{1,9},{5... | collective-permute-start | bytes 4718600 | tf_op jit(solution)/shard_map/w_feed_near_dp2/ppermute | solution.py:66
  166.9 35.2 %collective-permute-start.24 = (bf16[128,3072]{1,0:T(8,128)(2,1)}, bf16[128,3072]{1,0:T(8,128)(2,1)}, u32[]{:S(2)}, u32[]{:S(2)}) collective-permute-start(bf16[128,3072]{1,0:T(8,128)(2,1)} %get-tuple-element.400), channel_id=1, source_target_pairs={{0,2},{1,3},{2,0},{3,1},{4,6},{5,7},{6,4},{7,5},{8,10},{9,11},{10,... | collective-permute-start | bytes 2359304 | tf_op jit(solution)/shard_map/w_feed_far_tensor2/ppermute | solution.py:66
  235.0 35.5 %collective-permute-start.33 = (bf16[256,3072]{1,0:T(8,128)(2,1)S(1)}, bf16[256,3072]{1,0:T(8,128)(2,1)S(1)}, u32[]{:S(2)}, u32[]{:S(2)}) collective-permute-start(bf16[256,3072]{1,0:T(8,128)(2,1)S(1)} %shard_map.286.refs_0_), channel_id=1, source_target_pairs={{0,8},{4,12},{8,0},{12,4},{16,24},{20,28},{24,16},{28,20},{1,9},{5... | collective-permute-start | bytes 4718600 | tf_op jit(solution)/shard_map/w_feed_far_dp2/ppermute | solution.py:66
  236.6 35.2 %collective-permute-start.32 = (bf16[256,3072]{1,0:T(8,128)(2,1)S(1)}, bf16[256,3072]{1,0:T(8,128)(2,1)S(1)}, u32[]{:S(2)}, u32[]{:S(2)}) collective-permute-start(bf16[256,3072]{1,0:T(8,128)(2,1)S(1)} %shard_map.285.refs_0_), channel_id=1, source_target_pairs={{0,16},{4,20},{8,24},{12,28},{16,0},{20,4},{24,8},{28,12},{1,17},{... | collective-permute-start | bytes 4718600 | tf_op jit(solution)/shard_map/w_feed_far_dp4/ppermute | solution.py:66
  261.3 29.4 %collective-permute-start.35 = (bf16[512,3072]{1,0:T(8,128)(2,1)S(1)}, bf16[512,3072]{1,0:T(8,128)(2,1)}, u32[]{:S(2)}, u32[]{:S(2)}) collective-permute-start(bf16[512,3072]{1,0:T(8,128)(2,1)S(1)} %shard_map.282.refs_4_.refs_2_), channel_id=1, source_target_pairs={{0,4},{4,0},{8,12},{12,8},{16,20},{20,16},{24,28},{28,24},{1,5},{5... | collective-permute-start | bytes 9437192 | tf_op jit(solution)/shard_map/w_feed_near_dp1/ppermute | solution.py:66
  261.4 29.3 %collective-permute-start.36 = (bf16[512,3072]{1,0:T(8,128)(2,1)S(1)}, bf16[512,3072]{1,0:T(8,128)(2,1)}, u32[]{:S(2)}, u32[]{:S(2)}) collective-permute-start(bf16[512,3072]{1,0:T(8,128)(2,1)S(1)} %shard_map.283.refs_5_.refs_3_), channel_id=1, source_target_pairs={{0,4},{4,0},{8,12},{12,8},{16,20},{20,16},{24,28},{28,24},{1,5},{5... | collective-permute-start | bytes 9437192 | tf_op jit(solution)/shard_map/w_feed_near_dp1/ppermute | solution.py:66
  286.3 29.5 %collective-permute-start.37 = (bf16[512,3072]{1,0:T(8,128)(2,1)S(1)}, bf16[512,3072]{1,0:T(8,128)(2,1)}, u32[]{:S(2)}, u32[]{:S(2)}) collective-permute-start(bf16[512,3072]{1,0:T(8,128)(2,1)S(1)} %shard_map.288.refs_8_.refs_6_), channel_id=1, source_target_pairs={{0,4},{4,0},{8,12},{12,8},{16,20},{20,16},{24,28},{28,24},{1,5},{5... | collective-permute-start | bytes 9437192 | tf_op jit(solution)/shard_map/w_feed_far_dp1/ppermute | solution.py:66
  286.4 30.4 %collective-permute-start.38 = (bf16[512,3072]{1,0:T(8,128)(2,1)S(1)}, bf16[512,3072]{1,0:T(8,128)(2,1)}, u32[]{:S(2)}, u32[]{:S(2)}) collective-permute-start(bf16[512,3072]{1,0:T(8,128)(2,1)S(1)} %shard_map.289.refs_9_.refs_7_), channel_id=1, source_target_pairs={{0,4},{4,0},{8,12},{12,8},{16,20},{20,16},{24,28},{28,24},{1,5},{5... | collective-permute-start | bytes 9437192 | tf_op jit(solution)/shard_map/w_feed_far_dp1/ppermute | solution.py:66
  374.7 45.2 %collective-permute-start.43 = (bf16[1024,3072]{1,0:T(8,128)(2,1)}, bf16[1024,3072]{1,0:T(8,128)(2,1)}, u32[]{:S(2)}, u32[]{:S(2)}) collective-permute-start(bf16[1024,3072]{1,0:T(8,128)(2,1)} %shard_map.293), channel_id=1, source_target_pairs={{0,4},{4,0},{8,12},{12,8},{16,20},{20,16},{24,28},{28,24},{1,5},{5... | collective-permute-start | bytes 18874376 | tf_op jit(solution)/shard_map/grad_feed_near_dp1/ppermute | solution.py:66
  405.3 35.7 %collective-permute-start.46 = (bf16[256,3072]{1,0:T(8,128)(2,1)}, bf16[256,3072]{1,0:T(8,128)(2,1)S(1)}, u32[]{:S(2)}, u32[]{:S(2)}) collective-permute-start(bf16[256,3072]{1,0:T(8,128)(2,1)} %get-tuple-element.495), channel_id=1, source_target_pairs={{0,8},{4,12},{8,0},{12,4},{16,24},{20,28},{24,16},{28,20},{1,9},{5... | collective-permute-start | bytes 4718600 | tf_op jit(solution)/shard_map/grad_feed_far_dp2/ppermute | solution.py:66
  406.9 35.4 %collective-permute-start.45 = (bf16[256,3072]{1,0:T(8,128)(2,1)}, bf16[256,3072]{1,0:T(8,128)(2,1)S(1)}, u32[]{:S(2)}, u32[]{:S(2)}) collective-permute-start(bf16[256,3072]{1,0:T(8,128)(2,1)} %get-tuple-element.491), channel_id=1, source_target_pairs={{0,16},{4,20},{8,24},{12,28},{16,0},{20,4},{24,8},{28,12},{1,17},{... | collective-permute-start | bytes 4718600 | tf_op jit(solution)/shard_map/grad_feed_far_dp4/ppermute | solution.py:66
  481.9 32.6 %collective-permute-start.52 = (bf16[256,3072]{1,0:T(8,128)(2,1)}, bf16[256,3072]{1,0:T(8,128)(2,1)S(1)}, u32[]{:S(2)}, u32[]{:S(2)}) collective-permute-start(bf16[256,3072]{1,0:T(8,128)(2,1)} %get-tuple-element.540), channel_id=1, source_target_pairs={{0,8},{4,12},{8,0},{12,4},{16,24},{20,28},{24,16},{28,20},{1,9},{5... | collective-permute-start | bytes 4718600 | tf_op jit(solution)/shard_map/grad_feed_near_dp2/ppermute | solution.py:66
  482.9 32.6 %collective-permute-start.51 = (bf16[256,3072]{1,0:T(8,128)(2,1)}, bf16[256,3072]{1,0:T(8,128)(2,1)S(1)}, u32[]{:S(2)}, u32[]{:S(2)}) collective-permute-start(bf16[256,3072]{1,0:T(8,128)(2,1)} %get-tuple-element.536), channel_id=1, source_target_pairs={{0,16},{4,20},{8,24},{12,28},{16,0},{20,4},{24,8},{28,12},{1,17},{... | collective-permute-start | bytes 4718600 | tf_op jit(solution)/shard_map/grad_feed_near_dp4/ppermute | solution.py:66
  484.1 33.1 %collective-permute-start.50 = (bf16[128,3072]{1,0:T(8,128)(2,1)S(1)}, bf16[128,3072]{1,0:T(8,128)(2,1)}, u32[]{:S(2)}, u32[]{:S(2)}) collective-permute-start(bf16[128,3072]{1,0:T(8,128)(2,1)S(1)} %shard_map.307), channel_id=1, source_target_pairs={{0,2},{1,3},{2,0},{3,1},{4,6},{5,7},{6,4},{7,5},{8,10},{9,11},{10,... | collective-permute-start | bytes 2359304 | tf_op jit(solution)/shard_map/grad_feed_far_tensor2/ppermute | solution.py:66
  517.2 35.4 %collective-permute-start.55 = (bf16[128,3072]{1,0:T(8,128)(2,1)S(1)}, bf16[128,3072]{1,0:T(8,128)(2,1)S(1)}, u32[]{:S(2)}, u32[]{:S(2)}) collective-permute-start(bf16[128,3072]{1,0:T(8,128)(2,1)S(1)} %get-tuple-element.567), channel_id=1, source_target_pairs={{0,8},{4,12},{8,0},{12,4},{16,24},{20,28},{24,16},{28,20},{1,9},{5... | collective-permute-start | bytes 2359304 | tf_op jit(solution)/shard_map/grad_feed_near_dp2/ppermute | solution.py:66
  518.0 34.5 %collective-permute-start.56 = (bf16[128,3072]{1,0:T(8,128)(2,1)S(1)}, bf16[128,3072]{1,0:T(8,128)(2,1)S(1)}, u32[]{:S(2)}, u32[]{:S(2)}) collective-permute-start(bf16[128,3072]{1,0:T(8,128)(2,1)S(1)} %get-tuple-element.568), channel_id=1, source_target_pairs={{0,16},{4,20},{8,24},{12,28},{16,0},{20,4},{24,8},{28,12},{1,17},{... | collective-permute-start | bytes 2359304 | tf_op jit(solution)/shard_map/grad_feed_near_dp4/ppermute | solution.py:66
  519.0 37.1 %collective-permute-start.53 = (bf16[128,3072]{1,0:T(8,128)(2,1)S(1)}, bf16[128,3072]{1,0:T(8,128)(2,1)S(1)}, u32[]{:S(2)}, u32[]{:S(2)}) collective-permute-start(bf16[128,3072]{1,0:T(8,128)(2,1)S(1)} %shard_map.311), channel_id=1, source_target_pairs={{0,2},{1,3},{2,0},{3,1},{4,6},{5,7},{6,4},{7,5},{8,10},{9,11},{10,... | collective-permute-start | bytes 2359304 | tf_op jit(solution)/shard_map/grad_feed_far_tensor2/ppermute | solution.py:66
  585.8 29.8 %collective-permute-start.63 = (bf16[1024,1280]{1,0:T(8,128)(2,1)}, bf16[1024,1280]{1,0:T(8,128)(2,1)}, u32[]{:S(2)}, u32[]{:S(2)}) collective-permute-start(bf16[1024,1280]{1,0:T(8,128)(2,1)} %shard_map.317), channel_id=1, source_target_pairs={{0,4},{4,0},{8,12},{12,8},{16,20},{20,16},{24,28},{28,24},{1,5},{5... | collective-permute-start | bytes 7864328 | tf_op jit(solution)/shard_map/grad_w_out_dp1/ppermute | solution.py:66
  624.4 40.9 %collective-permute-start.71 = (bf16[128,3072]{1,0:T(8,128)(2,1)}, bf16[128,3072]{1,0:T(8,128)(2,1)}, u32[]{:S(2)}, u32[]{:S(2)}) collective-permute-start(bf16[128,3072]{1,0:T(8,128)(2,1)} %shard_map.320), channel_id=1, source_target_pairs={{0,8},{4,12},{8,0},{12,4},{16,24},{20,28},{24,16},{28,20},{1,9},{5... | collective-permute-start | bytes 2359304 | tf_op jit(solution)/shard_map/grad_w_in_dp2/ppermute | solution.py:66
  625.6 41.0 %collective-permute-start.72 = (bf16[128,3072]{1,0:T(8,128)(2,1)}, bf16[128,3072]{1,0:T(8,128)(2,1)S(1)}, u32[]{:S(2)}, u32[]{:S(2)}) collective-permute-start(bf16[128,3072]{1,0:T(8,128)(2,1)} %shard_map.322), channel_id=1, source_target_pairs={{0,16},{4,20},{8,24},{12,28},{16,0},{20,4},{24,8},{28,12},{1,17},{... | collective-permute-start | bytes 2359304 | tf_op jit(solution)/shard_map/grad_w_in_dp4/ppermute | solution.py:66
  629.1 28.8 %collective-permute-start.66 = (bf16[256,1280]{1,0:T(8,128)(2,1)}, bf16[256,1280]{1,0:T(8,128)(2,1)}, u32[]{:S(2)}, u32[]{:S(2)}) collective-permute-start(bf16[256,1280]{1,0:T(8,128)(2,1)} %get-tuple-element.617), channel_id=1, source_target_pairs={{0,8},{4,12},{8,0},{12,4},{16,24},{20,28},{24,16},{28,20},{1,9},{5... | collective-permute-start | bytes 1966088 | tf_op jit(solution)/shard_map/grad_w_out_dp2/ppermute | solution.py:66
  630.0 30.5 %collective-permute-start.65 = (bf16[256,1280]{1,0:T(8,128)(2,1)}, bf16[256,1280]{1,0:T(8,128)(2,1)}, u32[]{:S(2)}, u32[]{:S(2)}) collective-permute-start(bf16[256,1280]{1,0:T(8,128)(2,1)} %get-tuple-element.613), channel_id=1, source_target_pairs={{0,16},{4,20},{8,24},{12,28},{16,0},{20,4},{24,8},{28,12},{1,17},{... | collective-permute-start | bytes 1966088 | tf_op jit(solution)/shard_map/grad_w_out_dp4/ppermute | solution.py:66
  631.0 41.7 %collective-permute-start.64 = (bf16[256,2048]{1,0:T(8,128)(2,1)}, bf16[256,2048]{1,0:T(8,128)(2,1)S(1)}, u32[]{:S(2)}, u32[]{:S(2)}) collective-permute-start(bf16[256,2048]{1,0:T(8,128)(2,1)} %shard_map.318), channel_id=1, source_target_pairs={{0,1},{1,2},{2,3},{3,0},{4,5},{5,6},{6,7},{7,4},{8,9},{9,10},{10,1... | collective-permute-start | bytes 3145736 | tf_op jit(solution)/shard_map/sum_grad_attn_3/ppermute | solution.py:72
  (129 other events, 1658.1 us)

commit v3 on v2

--- a/solution.py
+++ b/solution.py
@@ -108,16 +108,22 @@
     return [*parts, *(swap(part, "dp", 1, name) for part in sync(*parts))]
 
 
+def scatter_send(parts, stage, name):
+    bits = dp_bits(lax.axis_size("dp"))[-1 - stage]
+    return [swap(sent, "dp", bit, name) for (_, sent), bit in zip(sync(*parts), bits)]
+
+
+def scatter_add(parts, came):
+    return [add_split(kept, part) for (kept, _), part in zip(parts, came)]
+
+
 def scatter_step(parts, stage, name, after=None):
-    bits = dp_bits(lax.axis_size("dp"))[-1 - stage]
-    parts = sync(*parts)
-    came = tie([swap(sent, "dp", bit, name) for (_, sent), bit in zip(parts, bits)], after)
-    return [add_split(kept, part) for (kept, _), part in zip(parts, came)]
-
-
-def scatter_rest(parts, stage, name):
+    return scatter_add(parts, tie(scatter_send(parts, stage, name), after))
+
+
+def scatter_rest(parts, stage, name, after=None):
     for step in range(stage, len(dp_bits(lax.axis_size("dp")))):
-        parts = scatter_step(parts, step, name)
+        parts = scatter_step(parts, step, name, after)
     return [half for part in parts for half in part]
 
 
@@ -721,7 +727,7 @@
     )(*hiddens, *[weight for parts in feeds for weight in parts], base)
 
 
-def gradient_kernel(plan, added, places, *refs):
+def gradient_kernel(plan, added, came_steps, places, *refs):
     number = sum(pieces for pieces, _, _ in plan)
     lefts, rights = refs[:number], refs[number : number + sum(len(r) for _, r, _ in plan)]
     rest = refs[number + len(rights) :]
@@ -742,7 +748,7 @@
             def _(right=rights[right_at], depth=pieces * size):
                 result = dot(turned[:, :depth], right[...])
                 if added:
-                    result = result + came[0][...].astype(f32)
+                    result = result + jnp.where(step < came_steps, came[0][...].astype(f32), 0.0)
                 height = result.shape[0] // len(outs)
                 for i, out in enumerate(outs):
                     out[...] = result[i * height : (i + 1) * height].astype(low)
@@ -762,7 +768,9 @@
         plan.append((len(pieces), [right.shape[1] // size for right in given], pieces[0].shape[0]))
         lefts += pieces
         places += at
-        left_specs += [pl.BlockSpec((pieces[0].shape[0], half), lambda t, _: (0, side))] * len(pieces)
+        whole = pieces[0].shape[1] == width
+        spec = pl.BlockSpec((pieces[0].shape[0], half), lambda t, _, whole=whole: (0, side if whole else 0))
+        left_specs += [spec] * len(pieces)
         for right in given:
             steps = right.shape[1] // size
             right_specs.append(
@@ -776,10 +784,12 @@
     parts = 1 if came is None else pieces_out
     tile = lambda height: pl.BlockSpec((height, size), lambda t, _: (0, t))
     more = [] if came is None else [came]
+    came_steps = 0 if came is None else came.shape[1] // size
+    came_specs = [pl.BlockSpec((half, size), lambda t, _: (0, jnp.minimum(t, came_steps - 1)))] * len(more)
     outs = call(
-        functools.partial(gradient_kernel, plan, len(more)),
+        functools.partial(gradient_kernel, plan, len(more), came_steps),
         (columns // size,),
-        left_specs + right_specs + [tile(half)] * len(more),
+        left_specs + right_specs + came_specs,
         [tile(half // parts)] * parts,
         [jax.ShapeDtypeStruct((half // parts, columns), low)] * parts,
         56,
@@ -823,8 +833,6 @@
 
     x_low = reorder(inputs, table)
     normed_one = normed_rows(x_low)
-    cot = reorder(cotangent, table)
-
     stride = 2 * KD + 2 * VD
     head_blocks = []
     for h in range(heads):
@@ -855,56 +863,62 @@
     fine = gains.shape[1] // 2
     gain_one, gain_two = gains[:, :fine].reshape(-1), gains[:, fine:].reshape(-1)
 
-    w_in = gather_step(tie(column_blocks(head_blocks), gains_same), 0, "w_in")
+    w_in = gather_step(column_blocks(head_blocks), 0, "w_in")
+    late_act, late_lin, late_down, late_out, late_cot = tie(
+        (w_act, w_lin, w_down, w_out, cotangent), normed_one
+    )
     feed_parts = column_blocks(
-        [(w_act, 0, hidden_cols), (w_lin, 0, hidden_cols), (w_down.T, 0, hidden_cols)]
-    )
-    wo = column_blocks([(w_out.T, 0, w_out.shape[0])])
+        [(late_act, 0, hidden_cols), (late_lin, 0, hidden_cols), (late_down.T, 0, hidden_cols)]
+    )
+    wo = column_blocks([(late_out.T, 0, w_out.shape[0])])
+    cot = reorder(late_cot, table)
 
     def beside_attn(step, came):
         nonlocal w_in, wo, cot, feed_parts, consts
         if step == 1:
             came, w_in, wo, cot, feed_parts, consts = sync(came, w_in, wo, cot, feed_parts, consts)
             w_in = gather_rest(w_in, 1, "w_in", consts)
+            wo = gather_step(tie(wo, w_in), 0, "w_out")
         return came
 
     pieces = gather_ring(normed_one, "rows_attn", beside_attn)
-    rows_here, w_in, wo = sync(pieces[-1], w_in, wo)
+    rows_here, w_in, wo, feed_parts, gain_one, gain_two = sync(
+        pieces[-1], w_in, wo, feed_parts, gain_one, gain_two
+    )
     pieces[-1] = rows_here
 
     def swap_far(part):
         return {k: swap(part, "tensor", k, "w_feed_far") for k in pair_blocks[1:]}
 
     cot_came = swap(tie(cotangent, rows_here), "tensor", 1, "rows_cot")
+    upper = swap_far(feed_parts[0])
     w_in = gather_core(w_in, "w_in")
-    wo = gather_step(wo, 0, "w_out")
     h_pieces = [scale_rows(piece, gain_one) for piece in pieces]
-    cot_came, wo, w_in, h_pieces, feed_parts = sync(cot_came, wo, w_in, h_pieces, feed_parts)
-
-    upper = swap_far(feed_parts[0])
-    wo = gather_rest(wo, 1, "w_out", upper)
-    near_feed = gather_step(feed_parts, 0, "w_feed_near", upper)
-    cots = [cot, reorder(cot_came, table)]
     pre = project(h_pieces[:-1], w_in, None, ring_places[:-1], tensor_size)
+    wo = gather_rest(wo, 1, "w_out", pre)
+    pre, cot_came, upper, wo, feed_parts = sync(pre, cot_came, upper, wo, feed_parts)
+    wo = gather_core(wo, "w_out")
+
+    lower = swap_far(tie(feed_parts[1], upper))
     pre = project(h_pieces[-1:], w_in, pre, ring_places[-1:], tensor_size)
-    pre, upper, wo, near_feed, cots = sync(pre, upper, wo, near_feed, cots)
-
-    lower = swap_far(tie(feed_parts[1], upper))
-    wo = gather_core(wo, "w_out")
-    near_feed = gather_rest(near_feed, 1, "w_feed_near", lower)
     mixed, kept, grouped, scale = retain(pre, consts, heads)
+    near_feed = gather_step(feed_parts, 0, "w_feed_near", mixed)
+    near_feed = gather_rest(near_feed, 1, "w_feed_near")
     sum_places = scatter_places()
     (total_out,) = terms(mixed, wo, sum_places[:1], rows, [low], None)
     rest_out = terms(tie(mixed, total_out), wo, sum_places[1:], rows, [f32] * (tensor_size - 1), None)
-    total_out, lower, rest_out, near_feed = sync(total_out, lower, rest_out, near_feed)
-    near_feed = gather_core(near_feed, "w_feed_near")
+    cots = [cot, reorder(tie(cot_came, total_out), table)]
+    total_out, lower, cots = sync(total_out, lower, cots)
     far_feeds = {k: gather_step([upper[k], lower[k]], 0, "w_feed_far") for k in upper}
 
     def beside_out(step, total):
-        nonlocal far_feeds
+        nonlocal far_feeds, near_feed
         if step == 1:
             total, far_feeds = sync(total, far_feeds)
             far_feeds = {k: gather_rest(v, 1, "w_feed_far") for k, v in far_feeds.items()}
+        if step == 2:
+            total, near_feed = sync(total, near_feed)
+            near_feed = gather_core(near_feed, "w_feed_near")
         if step == tensor_size - 1:
             total, far_feeds = sync(total, far_feeds)
             far_feeds = {k: gather_core(v, "w_feed_far") for k, v in far_feeds.items()}
@@ -933,7 +947,7 @@
     near_other = weight_gradient(feed_groups(late[0]), 1)
     grad_came, far, near_other = sync(grad_came, far, near_other)
     far_came = {k: swap(other, "dp", 1, "grad_feed_far") for k, other in far.items()}
-    near_came = swap(near_other, "dp", 1, "grad_feed_near")
+    near_came = None
     grad_middle, gain_two_term, grad_mid_low = norm_back_rows(
         middle, cot, gain_two, grad_h, grad_came, True
     )
@@ -949,7 +963,8 @@
                 k: weight_gradient(feed_groups(late[k // 2]), 0, far_came[k])
                 for k in pair_blocks[1:]
             }
-            came, far = sync(came, far)
+            came, far, near_last = sync(came, far, near_other)
+            near_came = swap(near_last, "dp", 1, "grad_feed_near")
             far = {k: scatter_step(v, 0, "grad_feed_far") for k, v in far.items()}
         if step == 2:
             late, weights = tie((results, feeds), mid_pieces[1])
@@ -978,7 +993,7 @@
     gain_columns = jnp.eye(16, TILE, dtype=low)
 
     def out_groups(right):
-        return [(mid_pieces, ring_places, [right]), ([gain_rows], gain_places, [gain_columns])]
+        return [(mid_pieces, ring_places, [right])]
 
     def swap_grad(parts):
         return {k: swap(part, "tensor", k, "grad_feed_far") for k, part in parts.items()}
@@ -988,36 +1003,42 @@
     total_in, more = terms(grad_in, w_in, sum_places[:1], rows, [low], first_pairs)
     late_in = tie(grad_in, total_in)
     in_other = weight_gradient([(h_pieces, ring_places, [late_in])], 1)
-    total_in, upper, in_other, near, lower_sent = sync(total_in, upper, in_other, near, lower_sent)
+    out_other = weight_gradient(out_groups(tie(mixed, in_other)), 1)
+    total_in, upper, in_other, out_other, near, lower_sent = sync(
+        total_in, upper, in_other, out_other, near, lower_sent
+    )
     lower = swap_grad(lower_sent)
     in_other = swap(in_other, "dp", 1, "grad_w_in")
+    out_other = swap(out_other, "dp", 1, "grad_w_out")
     *rest_in, more_rest = terms(
         tie(grad_in, total_in), w_in, sum_places[1:], rows, [f32] * (tensor_size - 1), rest_pairs
     )
     late_in = tie(grad_in, more_rest)
     grads_in = weight_gradient([(h_pieces, ring_places, [late_in])], 0, in_other, 8)
     near = scatter_step(near, 1, "grad_feed_near", grads_in)
-    total_in, lower, rest_in, grads_in, near = sync(total_in, lower, rest_in, grads_in, near)
+    total_in, lower, rest_in, grads_in, near, out_other = sync(
+        total_in, lower, rest_in, grads_in, near, out_other
+    )
     first_bits = dp_bits(dp_size)[-1]
     sent_on = [
         swap(part[3], "dp", bit, "grad_w_in") for part, bit in zip(grads_in, first_bits)
     ]
-    gain_rows = jnp.concatenate(
-        [(more + more_rest) / gain_one, gain_two_term, jnp.zeros((14, width), f32)], axis=0
-    ).astype(low)
-    out_other = weight_gradient(out_groups(tie(mixed, total_in)), 1)
-    grads_out = None
+    gain_rows = jnp.concatenate([(more + more_rest) / gain_one, gain_two_term], axis=0)
+    gain_rows = gain_rows[:, :half] + swap(gain_rows[:, half:], "dp", 1, "gains")
+    gain_rows = jnp.concatenate([gain_rows, jnp.zeros((14, half), f32)], axis=0).astype(low)
+    grads_out = weight_gradient(
+        out_groups(tie(mixed, total_in)) + [([gain_rows], gain_places, [gain_columns])], 0, out_other
+    )
+    out_sent = scatter_send(grads_out, 0, "grad_w_out")
 
     def beside_sum(step, total):
-        nonlocal grads_in, grads_out, out_other, sent_on
+        nonlocal grads_in, grads_out, sent_on
         if step == 1:
-            total, out_other, sent_on = sync(total, out_other, sent_on)
+            total, sent_on, grads_out = sync(total, sent_on, grads_out)
             kept_on = [
                 swap(part[2], "dp", bit, "grad_w_in") for part, bit in zip(grads_in, first_bits)
             ]
-            out_other = swap(out_other, "dp", 1, "grad_w_out")
-            grads_in, sent_on, kept_on = tie((grads_in, sent_on, kept_on), total)
-            grads_out = weight_gradient(out_groups(mixed), 0, out_other)
+            grads_in, sent_on = tie((grads_in, sent_on), total)
             sent_on = [
                 add_rows(part[1], came, low) for part, came in zip(grads_in, sent_on)
             ]
@@ -1025,26 +1046,27 @@
                 [add_rows(part[0], came, low), sent]
                 for part, came, sent in zip(grads_in, kept_on, sent_on)
             ]
-        if step == 2:
-            total, grads_in, grads_out = sync(total, grads_in, grads_out)
-            grads_in = scatter_rest(grads_in, 1, "grad_w_in")
-            grads_out = scatter_rest(grads_out, 0, "grad_w_out")
+            grads_out = scatter_add(grads_out, tie(out_sent, total))
         return total
 
     hattn_came, hattn_own = scatter_ring(total_in, rest_in, "sum_grad_attn", beside_sum)
+    (grad_inputs,) = norm_back_rows(x_low, grad_middle, gain_one, hattn_own, hattn_came, False)
+    grad_inputs = reorder(grad_inputs, back)
+    grads_out = scatter_rest(grads_out, 1, "grad_w_out")
+    grads_in = scatter_rest(tie(grads_in, grads_out), 1, "grad_w_in", grad_inputs)
     near = scatter_rest(near, 2, "grad_feed_near")
     grad_out_own = jnp.concatenate(grads_out, axis=0).astype(f32)
     columns = w_out.shape[0]
-    grad_wo_own, gain_sum = grad_out_own[:, :columns], grad_out_own[:, columns : columns + 128]
-    hattn_came, gain_sum = sync(hattn_came, gain_sum)
-    for b in range(tensor_size.bit_length() - 1):
-        gain_sum = gain_sum + swap(gain_sum, "tensor", 1 << b, "gains")
+    grad_wo_own, gain_sum = grad_out_own[:, :columns], grad_out_own[:, columns : columns + 2].T
+    gain_sums = [gain_sum] + [swap(gain_sum, "tensor", k, "gains") for k in range(1, tensor_size)]
+    while len(gain_sums) > 1:
+        gain_sums = [a + b for a, b in zip(gain_sums[::2], gain_sums[1::2])]
+    gain_sum = gain_sums[0]
     grad_in_own = jnp.concatenate(grads_in, axis=0).astype(f32)
     grad_feed = jnp.concatenate(near, axis=0).astype(f32)
     for k in pair_blocks[1:]:
         grad_feed = grad_feed + jnp.concatenate([upper[k], lower[k]], axis=0).astype(f32)
     outputs = out_own + out_came.astype(f32)
-    (grad_inputs,) = norm_back_rows(x_low, grad_middle, gain_one, hattn_own, hattn_came, False)
 
     def heads_back(first, size):
         return jnp.concatenate(
@@ -1054,14 +1076,14 @@
 
     return (
         reorder(outputs.astype(low), back),
-        reorder(grad_inputs, back),
-        gain_sum[:, 0],
+        grad_inputs,
+        gain_sum[0],
         heads_back(0, KD),
         heads_back(KD, KD),
         heads_back(2 * KD, VD),
         heads_back(2 * KD + VD, VD),
         grad_wo_own.T,
-        gain_sum[:, 1],
+        gain_sum[1],
         grad_feed[:, :hidden_cols],
         grad_feed[:, hidden_cols : 2 * hidden_cols],
         grad_feed[:, 2 * hidden_cols :].T,

time: 699 us -> 651 us (0.931)
  waiting for transfers between devices: 277 us -> 212 us
  starting transfers between devices: 55.7 us -> 66.4 us
    ppermute x12, waiting for transfers between devices: 111 us -> 59.2 us  [shift(): lax.ppermute(values, axis, [(i, (i + step) % size) for i in range(size)])]
    ppermute x61 -> x63, waiting for transfers between devices: 165 us -> 152 us  [swap(): return lax.ppermute(values, axis, [(i, i ^ bits) for i in range(size)])]
    ppermute x61 -> x63, starting transfers between devices: 51.4 us -> 58.4 us  [swap(): return lax.ppermute(values, axis, [(i, i ^ bits) for i in range(size)])]
  transfers between devices with their start and end apart: 73 -> 75, of which waited for: 37 -> 30; matrix products, arithmetic and copies ran while one was open for 4% -> 4% of each run, Pallas kernels for 36% -> 41%
where the time goes in v3:
time: 651 us; the launch traced here: 640 us
  Pallas kernels  300 us (46%)
  waiting for transfers between devices  212 us (33%)
  starting transfers between devices  66.4 us (10%)
  local copies, waits for them, and re-layouts  41.1 us (6%)
  other arithmetic  18 us (3%)
    ppermute x63, waiting for transfers between devices, swap(): return lax.ppermute(values, axis, [(i, i ^ bits) for i in range(size)])  152 us
    pallas_call x8, Pallas kernels, weight_gradient(): call(functools.partial(gradient_kernel, plan, len(more), came_steps), (co...  84.1 us
    ppermute x12, waiting for transfers between devices, shift(): lax.ppermute(values, axis, [(i, (i + step) % size) for i in range(size)])  59.2 us
    ppermute x63, starting transfers between devices, swap(): return lax.ppermute(values, axis, [(i, i ^ bits) for i in range(size)])  58.4 us
    pallas_call x4, Pallas kernels, terms(): call(functools.partial(terms_kernel, number, paired), (4, steps), rows +...  44.6 us
    pallas_call x4, Pallas kernels, project(): call(functools.partial(project_kernel, number), (columns // size,), [rows...  39.1 us
    unnamed x180, local copies, waits for them, and re-layouts  34.1 us
    pallas_call x1, Pallas kernels, feed(): call(functools.partial(feed_kernel, number, steps), (number * steps,), [a...  33.2 us
  transfers between devices with their start and end apart: 75, of which 30 were waited for; matrix products, arithmetic and copies ran while one was open for 4% of the time, Pallas kernels for 41%

profile of v3, /device:TPU:0, one launch (start us, length us, event | category | flops | bytes accessed | tf_op | source)
XLA Modules:
  0.0 640.0 jit_solution(1026329965813707558)
XLA Ops:
  37.6 22.1 %collective-permute-done.3.rows = bf16[256,2048]{1,0:T(8,128)(2,1)} collective-permute-done((bf16[256,2048]{1,0:T(8,128)(2,1)S(1)}, bf16[256,2048]{1,0:T(8,128)(2,1)}, u32[]{:S(2)}, u32[]{:S(2)}) %collective-permute-start.3) | collective-permute-done | bytes 1048608 | tf_op jit(solution)/shard_map/rows_attn_2/ppermute | solution.py:72
  62.6 8.5 %collective-permute-done.9 = bf16[1,256]{1,0:T(2,128)(2,1)S(1)} collective-permute-done((bf16[1,256]{1,0:T(2,128)(2,1)S(1)}, bf16[1,256]{1,0:T(2,128)(2,1)S(1)}, u32[]{:S(2)}, u32[]{:S(2)}) %collective-permute-start.9) | collective-permute-done | bytes 544 | tf_op jit(solution)/shard_map/gains_dp2/ppermute | solution.py:66
  102.9 16.7 %shard_map.272.refs_5_ = f32[1024,3072]{1,0:T(8,128)} custom-call(s32[3]{0:T(128)} %pad_add_fusion.places, bf16[256,2048]{1,0:T(8,128)(2,1)} %copy-done.11, bf16[256,2048]{1,0:T(8,128)(2,1)} %copy-done.10, bf16[256,2048]{1,0:T(8,128)(2,1)} %copy-done.12, bf16[512,3072]{1,0:T(8,128)(2,1)} %copy-done.1, bf16[512,3072]{1,0:T(8,128)(2,1)} %copy-done, ...), custom_call_target="tpu_custom_call" | custom-call | tf_op jit(solution)/shard_map/pallas_call | solution.py:324
  122.8 4.5 collective-permute-done.17.refs_0_
  136.6 9.6 %shard_map.275.pre.gates = f32[1024,3072]{1,0:T(8,128)} custom-call(s32[1]{0:T(128)} %bitcast.8.places, bf16[256,2048]{1,0:T(8,128)(2,1)} %copy-done.9, bf16[512,3072]{1,0:T(8,128)(2,1)} %copy-done.1, bf16[512,3072]{1,0:T(8,128)(2,1)} %copy-done, bf16[512,3072]{1,0:T(8,128)(2,1)} %collective-permute-done.14.refs_5_.refs_3_, ...), custom_call_target="tpu_custom_call", output_to_operand_aliasing={{}: (6, {})} | custom-call | tf_op jit(solution)/shard_map/pallas_call | solution.py:324
  146.1 10.4 %shard_map.276 = (bf16[1024,1024]{1,0:T(8,128)(2,1)}, bf16[1024,2048]{1,0:T(8,128)(2,1)}, f32[1024,1024]{1,0:T(8,128)}, f32[1024,256]{1,0:T(8,128)}) custom-call(f32[2,4]{1,0:T(2,128)} %multiply_exponential_fusion.powers, f32[2]{0:T(128)} %copy-done.83, f32[1024,3072]{1,0:T(8,128)} %shard_map.275.pre.gates, f32[1024,128]{1,0:T(8,128)} %get-tuple-element.328.cosine, ...), custom_call_target="tpu_custom_call" | custom-call | tf_op jit(solution)/shard_map/pallas_call | solution.py:502
  156.6 5.3 shard_map.277
  175.6 8.9 %shard_map.279 = (f32[256,2048]{1,0:T(8,128)}, f32[256,2048]{1,0:T(8,128)}, f32[256,2048]{1,0:T(8,128)}) custom-call(s32[3]{0:T(128)} %pad_add_fusion.1.places, bf16[1024,1024]{1,0:T(8,128)(2,1)} %get-tuple-element.550.refs_0_.refs_1_.refs_2_.refs_4_.refs_5_, bf16[1024,1024]{1,0:T(8,128)(2,1)} %get-tuple-element.550.refs_0_.refs_1_.refs_2_.refs_4_.refs_5_, ...), custom_call_target="tpu_custom_call" | custom-call | tf_op jit(solution)/shard_map/pallas_call | solution.py:374
  196.7 26.5 %collective-permute-done.30.refs_1_ = bf16[256,3072]{1,0:T(8,128)(2,1)} collective-permute-done((bf16[256,3072]{1,0:T(8,128)(2,1)S(1)}, bf16[256,3072]{1,0:T(8,128)(2,1)}, u32[]{:S(2)}, u32[]{:S(2)}) %collective-permute-start.30) | collective-permute-done | bytes 1572896 | tf_op jit(solution)/shard_map/w_feed_near_dp2/ppermute | solution.py:66
  229.9 24.8 %collective-permute-done.33.refs_1_ = bf16[256,3072]{1,0:T(8,128)(2,1)S(1)} collective-permute-done((bf16[256,3072]{1,0:T(8,128)(2,1)S(1)}, bf16[256,3072]{1,0:T(8,128)(2,1)S(1)}, u32[]{:S(2)}, u32[]{:S(2)}) %collective-permute-start.33) | collective-permute-done | bytes 1572896 | tf_op jit(solution)/shard_map/w_feed_far_dp2/ppermute | solution.py:66
  261.7 24.4 %collective-permute-done.34.refs_1_ = bf16[256,2048]{1,0:T(8,128)(2,1)S(1)} collective-permute-done((bf16[256,2048]{1,0:T(8,128)(2,1)S(1)}, bf16[256,2048]{1,0:T(8,128)(2,1)S(1)}, u32[]{:S(2)}, u32[]{:S(2)}) %collective-permute-start.34) | collective-permute-done | bytes 1048608 | tf_op jit(solution)/shard_map/rows_mlp_tensor1/ppermute | solution.py:66
  287.0 33.2 %shard_map.291 = (bf16[512,1024]{1,0:T(8,128)(2,1)}, bf16[512,1024]{1,0:T(8,128)(2,1)}, bf16[512,1024]{1,0:T(8,128)(2,1)}, bf16[512,1024]{1,0:T(8,128)(2,1)}, bf...) custom-call(bf16[256,2048]{1,0:T(8,128)(2,1)} %copy-done.15, ...), custom_call_target="tpu_custom_call" | custom-call | tf_op jit(solution)/shard_map/pallas_call | solution.py:677
  320.6 9.9 %shard_map.293 = bf16[1024,3072]{1,0:T(8,128)(2,1)} custom-call(s32[4]{0:T(128)} %constant.90.clone.1.places, bf16[256,2048]{1,0:T(8,128)(2,1)} %copy-done.15, bf16[256,2048]{1,0:T(8,128)(2,1)} %copy-done.71, bf16[256,2048]{1,0:T(8,128)(2,1)} %copy-done.2, bf16[256,2048]{1,0:T(8,128)(2,1)} %copy-done.4, bf16[512,1024]{1,0:T(8,128)(2,1)} %get-tuple-element.450.refs_4_, ...), custom_call_target="tpu_custom_call" | custom-call | tf_op jit(solution)/shard_map/pallas_call | solution.py:789
  330.5 10.4 %shard_map.292 = bf16[1024,3072]{1,0:T(8,128)(2,1)} custom-call(s32[4]{0:T(128)} %constant.90.clone.1.places, bf16[256,2048]{1,0:T(8,128)(2,1)} %copy-done.15, bf16[256,2048]{1,0:T(8,128)(2,1)} %copy-done.71, bf16[256,2048]{1,0:T(8,128)(2,1)} %copy-done.2, bf16[256,2048]{1,0:T(8,128)(2,1)} %copy-done.4, bf16[512,1024]{1,0:T(8,128)(2,1)} %get-tuple-element.428.refs_4_, ...), custom_call_target="tpu_custom_call" | custom-call | tf_op jit(solution)/shard_map/pallas_call | solution.py:789
  348.2 6.7 %collective-permute-done.41.refs_7_ = bf16[1024,3072]{1,0:T(8,128)(2,1)} collective-permute-done((bf16[1024,3072]{1,0:T(8,128)(2,1)}, bf16[1024,3072]{1,0:T(8,128)(2,1)}, u32[]{:S(2)}, u32[]{:S(2)}) %collective-permute-start.41) | collective-permute-done | bytes 6291488 | tf_op jit(solution)/shard_map/grad_feed_far_dp1/ppermute | solution.py:66
  354.9 11.1 %shard_map.295 = (bf16[256,3072]{1,0:T(8,128)(2,1)}, bf16[256,3072]{1,0:T(8,128)(2,1)}, bf16[256,3072]{1,0:T(8,128)(2,1)}, bf16[256,3072]{1,0:T(8,128)(2,1)}) custom-call(s32[4]{0:T(128)} %constant.90.clone.1.places, bf16[256,2048]{1,0:T(8,128)(2,1)} %copy-done.15, bf16[256,2048]{1,0:T(8,128)(2,1)} %copy-done.71, bf16[256,2048]{1,0:T(8,128)(2,1)} %copy-done.2, ...), custom_call_target="tpu_custom_call" | custom-call | tf_op jit(solution)/shard_map/pallas_call | solution.py:789
  365.9 9.3 %collective-permute-done.40.refs_1_ = bf16[256,2048]{1,0:T(8,128)(2,1)S(1)} collective-permute-done((bf16[256,2048]{1,0:T(8,128)(2,1)S(1)}, bf16[256,2048]{1,0:T(8,128)(2,1)S(1)}, u32[]{:S(2)}, u32[]{:S(2)}) %collective-permute-start.40) | collective-permute-done | bytes 1048608 | tf_op jit(solution)/shard_map/rows_grad_mid_1/ppermute | solution.py:72
  377.7 12.0 %shard_map.296 = (f32[256,2048]{1,0:T(8,128)}, bf16[256,2048]{1,0:T(8,128)(2,1)}) custom-call(bf16[512,1024]{1,0:T(8,128)(2,1)} %get-tuple-element.438.refs_6_.refs_0_, bf16[512,1024]{1,0:T(8,128)(2,1)} %get-tuple-element.439.refs_6_.refs_1_, bf16[512,3072]{1,0:T(8,128)(2,1)} %copy-done.6, bf16[512,3072]{1,0:T(8,128)(2,1)} %copy-done.5, ...), custom_call_target="tpu_custom_call" | custom-call | tf_op jit(solution)/shard_map/pallas_call | solution.py:718
  389.8 11.2 %shard_map.297 = (bf16[256,3072]{1,0:T(8,128)(2,1)}, bf16[256,3072]{1,0:T(8,128)(2,1)}, bf16[256,3072]{1,0:T(8,128)(2,1)}, bf16[256,3072]{1,0:T(8,128)(2,1)}) custom-call(s32[4]{0:T(128)} %constant.90.clone.1.places, bf16[256,2048]{1,0:T(8,128)(2,1)} %copy-done.15, bf16[256,2048]{1,0:T(8,128)(2,1)} %copy-done.71, bf16[256,2048]{1,0:T(8,128)(2,1)} %copy-done.2, ...), custom_call_target="tpu_custom_call" | custom-call | tf_op jit(solution)/shard_map/pallas_call | solution.py:789
  402.8 9.4 %collective-permute-done.46.right = bf16[256,3072]{1,0:T(8,128)(2,1)S(1)} collective-permute-done((bf16[256,3072]{1,0:T(8,128)(2,1)}, bf16[256,3072]{1,0:T(8,128)(2,1)S(1)}, u32[]{:S(2)}, u32[]{:S(2)}) %collective-permute-start.46) | collective-permute-done | bytes 1572896 | tf_op jit(solution)/shard_map/grad_feed_far_dp2/ppermute | solution.py:66
  413.7 8.5 %shard_map.300.refs_5_ = f32[1024,1024]{1,0:T(8,128)} custom-call(s32[3]{0:T(128)} %pad_add_fusion.places, bf16[256,2048]{1,0:T(8,128)(2,1)} %copy-done.19, bf16[256,2048]{1,0:T(8,128)(2,1)} %copy-done.72, bf16[256,2048]{1,0:T(8,128)(2,1)} %collective-permute-done.42.refs_2_, bf16[512,1024]{1,0:T(8,128)(2,1)} %copy-done.14, bf16[512,1024]{1,0:T(8,128)(2,1)} %copy-done.13, ...), custom_call_target="tpu_custom_call" | custom-call | tf_op jit(solution)/shard_map/pallas_call | solution.py:324
  422.2 7.5 %collective-permute-done.44.refs_0_.refs_3_ = bf16[256,2048]{1,0:T(8,128)(2,1)} collective-permute-done((bf16[256,2048]{1,0:T(8,128)(2,1)}, bf16[256,2048]{1,0:T(8,128)(2,1)}, u32[]{:S(2)}, u32[]{:S(2)}) %collective-permute-start.44) | collective-permute-done | bytes 1048608 | tf_op jit(solution)/shard_map/rows_grad_mid_3/ppermute | solution.py:72
  437.1 16.8 %shard_map.302.refs_0_.refs_4_.refs_1_.refs_2_ = bf16[1024,3072]{1,0:T(8,128)(2,1)} custom-call(f32[2,4]{1,0:T(2,128)} %multiply_exponential_fusion.powers, f32[2]{0:T(128)} %copy-done.83, f32[1024,1024]{1,0:T(8,128)} %shard_map.301.grad, f32[1024,3072]{1,0:T(8,128)} %shard_map.275.pre.gates, bf16[1024,2048]{1,0:T(8,128)(2,1)} %get-tuple-element.474.kept, ...), custom_call_target="tpu_custom_call" | custom-call | tf_op jit(solution)/shard_map/pallas_call | solution.py:561
  458.4 11.7 %shard_map.306 = (bf16[256,2048]{1,0:T(8,128)(2,1)}, f32[1,2048]{1,0:T(1,128)}) custom-call(s32[1]{0:T(128)} %bitcast.1.places, bf16[1024,3072]{1,0:T(8,128)(2,1)} %shard_map.302.refs_0_.refs_4_.refs_1_.refs_2_, bf16[512,3072]{1,0:T(8,128)(2,1)} %copy-done.1, bf16[512,3072]{1,0:T(8,128)(2,1)} %copy-done, ...), custom_call_target="tpu_custom_call" | custom-call | tf_op jit(solution)/shard_map/pallas_call | solution.py:374
  470.1 12.6 %shard_map.308 = bf16[1024,3072]{1,0:T(8,128)(2,1)} custom-call(s32[4]{0:T(128)} %pad_add_fusion.2.places, bf16[256,2048]{1,0:T(8,128)(2,1)} %copy-done.11, bf16[256,2048]{1,0:T(8,128)(2,1)} %copy-done.10, bf16[256,2048]{1,0:T(8,128)(2,1)} %copy-done.12, bf16[256,2048]{1,0:T(8,128)(2,1)} %copy-done.9, ...), custom_call_target="tpu_custom_call" | custom-call | tf_op jit(solution)/shard_map/pallas_call | solution.py:789
  482.7 6.8 %shard_map.309 = bf16[1024,1024]{1,0:T(8,128)(2,1)} custom-call(s32[4]{0:T(128)} %pad_add_fusion.2.places, bf16[256,2048]{1,0:T(8,128)(2,1)} %copy-done.19, bf16[256,2048]{1,0:T(8,128)(2,1)} %copy-done.72, bf16[256,2048]{1,0:T(8,128)(2,1)} %collective-permute-done.42.refs_2_, bf16[256,2048]{1,0:T(8,128)(2,1)} %collective-permute-done.44.refs_0_.refs_3_, ...), custom_call_target="tpu_custom_call" | custom-call | tf_op jit(solution)/shard_map/pallas_call | solution.py:789
  497.8 18.7 %shard_map.313 = (f32[256,2048]{1,0:T(8,128)}, f32[256,2048]{1,0:T(8,128)}, f32[256,2048]{1,0:T(8,128)}, f32[1,2048]{1,0:T(1,128)}) custom-call(s32[3]{0:T(128)} %pad_add_fusion.1.places, bf16[1024,3072]{1,0:T(8,128)(2,1)} %shard_map.302.refs_0_.refs_4_.refs_1_.refs_2_, bf16[1024,3072]{1,0:T(8,128)(2,1)} %shard_map.302.refs_0_.refs_4_.refs_1_.refs_2_, ...), custom_call_target="tpu_custom_call" | custom-call | tf_op jit(solution)/shard_map/pallas_call | solution.py:374
  516.5 13.7 %shard_map.314 = (bf16[128,3072]{1,0:T(8,128)(2,1)}, bf16[128,3072]{1,0:T(8,128)(2,1)}, bf16[128,3072]{1,0:T(8,128)(2,1)}, bf16[128,3072]{1,0:T(8,128)(2,1)}, bf...) custom-call(s32[4]{0:T(128)} %pad_add_fusion.2.places, ...), custom_call_target="tpu_custom_call" | custom-call | tf_op jit(solution)/shard_map/pallas_call | solution.py:789
  539.3 8.4 %shard_map.318 = (bf16[256,1280]{1,0:T(8,128)(2,1)}, bf16[256,1280]{1,0:T(8,128)(2,1)}, bf16[256,1280]{1,0:T(8,128)(2,1)}, bf16[256,1280]{1,0:T(8,128)(2,1)}) custom-call(s32[5]{0:T(128)} %stack.26.places, bf16[256,2048]{1,0:T(8,128)(2,1)} %copy-done.19, bf16[256,2048]{1,0:T(8,128)(2,1)} %copy-done.72, bf16[256,2048]{1,0:T(8,128)(2,1)} %collective-permute-done.42.refs_2_, ...), custom_call_target="tpu_custom_call" | custom-call | tf_op jit(solution)/shard_map/pallas_call | solution.py:789
  547.7 13.0 %collective-permute-done.58.left = bf16[256,2048]{1,0:T(8,128)(2,1)S(1)} collective-permute-done((bf16[256,2048]{1,0:T(8,128)(2,1)}, bf16[256,2048]{1,0:T(8,128)(2,1)S(1)}, u32[]{:S(2)}, u32[]{:S(2)}) %collective-permute-start.58) | collective-permute-done | bytes 1048608 | tf_op jit(solution)/shard_map/sum_grad_attn_1/ppermute | solution.py:72
  571.0 8.1 %collective-permute-done.64.right = bf16[256,1280]{1,0:T(8,128)(2,1)} collective-permute-done((bf16[256,1280]{1,0:T(8,128)(2,1)}, bf16[256,1280]{1,0:T(8,128)(2,1)}, u32[]{:S(2)}, u32[]{:S(2)}) %collective-permute-start.64) | collective-permute-done | bytes 655392 | tf_op jit(solution)/shard_map/grad_w_out_dp4/ppermute | solution.py:66
  609.8 7.6 %collective-permute-done.68 = f32[2,256]{0,1:T(8,128)} collective-permute-done((f32[2,256]{0,1:T(8,128)S(1)}, f32[2,256]{0,1:T(8,128)}, u32[]{:S(2)}, u32[]{:S(2)}) %collective-permute-start.68) | collective-permute-done | bytes 2080 | tf_op jit(solution)/shard_map/gains_tensor1/ppermute | solution.py:66
  (419 shorter events, 229.3 us)
Async XLA Ops:
  5.2 28.3 %collective-permute-start = (bf16[256,2048]{1,0:T(8,128)(2,1)S(1)}, bf16[256,2048]{1,0:T(8,128)(2,1)S(1)}, u32[]{:S(2)}, u32[]{:S(2)}) collective-permute-start(bf16[256,2048]{1,0:T(8,128)(2,1)S(1)} %shard_map.257.rows), channel_id=1, source_target_pairs={{0,1},{1,2},{2,3},{3,0},{4,5},{5,6},{6,7},{7,4},{8,9},{9,10},{10,1... | collective-permute-start | bytes 3145736 | tf_op jit(solution)/shard_map/rows_attn_1/ppermute | solution.py:72
  34.6 38.6 %collective-permute-start.5 = (bf16[256,3072]{1,0:T(8,128)(2,1)S(1)}, bf16[256,3072]{1,0:T(8,128)(2,1)S(1)}, u32[]{:S(2)}, u32[]{:S(2)}) collective-permute-start(bf16[256,3072]{1,0:T(8,128)(2,1)S(1)} %shard_map.259.refs_0_), channel_id=1, source_target_pairs={{0,16},{4,20},{8,24},{12,28},{16,0},{20,4},{24,8},{28,12},{1,17},{... | collective-permute-start | bytes 4718600 | tf_op jit(solution)/shard_map/w_in_dp4/ppermute | solution.py:66
  36.1 37.1 %collective-permute-start.6 = (bf16[256,3072]{1,0:T(8,128)(2,1)S(1)}, bf16[256,3072]{1,0:T(8,128)(2,1)S(1)}, u32[]{:S(2)}, u32[]{:S(2)}) collective-permute-start(bf16[256,3072]{1,0:T(8,128)(2,1)S(1)} %shard_map.260.refs_0_), channel_id=1, source_target_pairs={{0,8},{4,12},{8,0},{12,4},{16,24},{20,28},{24,16},{28,20},{1,9},{5... | collective-permute-start | bytes 4718600 | tf_op jit(solution)/shard_map/w_in_dp2/ppermute | solution.py:66
  86.4 42.3 %collective-permute-start.16 = (bf16[256,2048]{1,0:T(8,128)(2,1)}, bf16[256,2048]{1,0:T(8,128)(2,1)}, u32[]{:S(2)}, u32[]{:S(2)}) collective-permute-start(bf16[256,2048]{1,0:T(8,128)(2,1)} %values.2), channel_id=1, source_target_pairs={{0,1},{1,0},{2,3},{3,2},{4,5},{5,4},{6,7},{7,6},{8,9},{9,8},{10,11... | collective-permute-start | bytes 3145736 | tf_op jit(solution)/shard_map/rows_cot_tensor1/ppermute | solution.py:66
  87.4 39.8 %collective-permute-start.17 = (bf16[128,3072]{1,0:T(8,128)(2,1)}, bf16[128,3072]{1,0:T(8,128)(2,1)}, u32[]{:S(2)}, u32[]{:S(2)}) collective-permute-start(bf16[128,3072]{1,0:T(8,128)(2,1)} %get-tuple-element.381), channel_id=1, source_target_pairs={{0,2},{1,3},{2,0},{3,1},{4,6},{5,7},{6,4},{7,5},{8,10},{9,11},{10,... | collective-permute-start | bytes 2359304 | tf_op jit(solution)/shard_map/w_feed_far_tensor2/ppermute | solution.py:66
  90.5 29.2 %collective-permute-start.18 = (bf16[256,1024]{1,0:T(8,128)(2,1)}, bf16[256,1024]{1,0:T(8,128)(2,1)}, u32[]{:S(2)}, u32[]{:S(2)}) collective-permute-start(bf16[256,1024]{1,0:T(8,128)(2,1)} %shard_map.266.refs_0_), channel_id=1, source_target_pairs={{0,16},{4,20},{8,24},{12,28},{16,0},{20,4},{24,8},{28,12},{1,17},{... | collective-permute-start | bytes 1572872 | tf_op jit(solution)/shard_map/w_out_dp4/ppermute | solution.py:66
  129.2 37.3 %collective-permute-start.22 = (bf16[128,3072]{1,0:T(8,128)(2,1)S(1)}, bf16[128,3072]{1,0:T(8,128)(2,1)}, u32[]{:S(2)}, u32[]{:S(2)}) collective-permute-start(bf16[128,3072]{1,0:T(8,128)(2,1)S(1)} %copy-done.47), channel_id=1, source_target_pairs={{0,2},{1,3},{2,0},{3,1},{4,6},{5,7},{6,4},{7,5},{8,10},{9,11},{10,... | collective-permute-start | bytes 2359304 | tf_op jit(solution)/shard_map/w_feed_far_tensor2/ppermute | solution.py:66
  131.2 38.8 %collective-permute-start.27 = (bf16[128,3072]{1,0:T(8,128)(2,1)}, bf16[128,3072]{1,0:T(8,128)(2,1)}, u32[]{:S(2)}, u32[]{:S(2)}) collective-permute-start(bf16[128,3072]{1,0:T(8,128)(2,1)} %get-tuple-element.382.refs_0_), channel_id=1, source_target_pairs={{0,8},{4,12},{8,0},{12,4},{16,24},{20,28},{24,16},{28,20},{1,9},{5... | collective-permute-start | bytes 2359304 | tf_op jit(solution)/shard_map/w_feed_near_dp2/ppermute | solution.py:66
  131.7 38.3 %collective-permute-start.28 = (bf16[128,3072]{1,0:T(8,128)(2,1)S(1)}, bf16[128,3072]{1,0:T(8,128)(2,1)}, u32[]{:S(2)}, u32[]{:S(2)}) collective-permute-start(bf16[128,3072]{1,0:T(8,128)(2,1)S(1)} %copy-done.47), channel_id=1, source_target_pairs={{0,16},{4,20},{8,24},{12,28},{16,0},{20,4},{24,8},{28,12},{1,17},{... | collective-permute-start | bytes 2359304 | tf_op jit(solution)/shard_map/w_feed_near_dp4/ppermute | solution.py:66
  172.8 50.4 %collective-permute-start.30 = (bf16[256,3072]{1,0:T(8,128)(2,1)S(1)}, bf16[256,3072]{1,0:T(8,128)(2,1)}, u32[]{:S(2)}, u32[]{:S(2)}) collective-permute-start(bf16[256,3072]{1,0:T(8,128)(2,1)S(1)} %shard_map.285.refs_0_), channel_id=1, source_target_pairs={{0,8},{4,12},{8,0},{12,4},{16,24},{20,28},{24,16},{28,20},{1,9},{5... | collective-permute-start | bytes 4718600 | tf_op jit(solution)/shard_map/w_feed_near_dp2/ppermute | solution.py:66
  173.6 51.3 %collective-permute-start.29 = (bf16[256,3072]{1,0:T(8,128)(2,1)S(1)}, bf16[256,3072]{1,0:T(8,128)(2,1)}, u32[]{:S(2)}, u32[]{:S(2)}) collective-permute-start(bf16[256,3072]{1,0:T(8,128)(2,1)S(1)} %shard_map.284.refs_0_), channel_id=1, source_target_pairs={{0,16},{4,20},{8,24},{12,28},{16,0},{20,4},{24,8},{28,12},{1,17},{... | collective-permute-start | bytes 4718600 | tf_op jit(solution)/shard_map/w_feed_near_dp4/ppermute | solution.py:66
  194.5 33.2 %collective-permute-start.26 = (bf16[256,2048]{1,0:T(8,128)(2,1)S(1)}, bf16[256,2048]{1,0:T(8,128)(2,1)S(1)}, u32[]{:S(2)}, u32[]{:S(2)}) collective-permute-start(bf16[256,2048]{1,0:T(8,128)(2,1)S(1)} %shard_map.280), channel_id=1, source_target_pairs={{0,1},{1,2},{2,3},{3,0},{4,5},{5,6},{6,7},{7,4},{8,9},{9,10},{10,1... | collective-permute-start | bytes 3145736 | tf_op jit(solution)/shard_map/sum_attn_2/ppermute | solution.py:72
  194.6 60.1 %collective-permute-start.33 = (bf16[256,3072]{1,0:T(8,128)(2,1)S(1)}, bf16[256,3072]{1,0:T(8,128)(2,1)S(1)}, u32[]{:S(2)}, u32[]{:S(2)}) collective-permute-start(bf16[256,3072]{1,0:T(8,128)(2,1)S(1)} %shard_map.282.refs_0_), channel_id=1, source_target_pairs={{0,8},{4,12},{8,0},{12,4},{16,24},{20,28},{24,16},{28,20},{1,9},{5... | collective-permute-start | bytes 4718600 | tf_op jit(solution)/shard_map/w_feed_far_dp2/ppermute | solution.py:66
  195.4 59.6 %collective-permute-start.32 = (bf16[256,3072]{1,0:T(8,128)(2,1)S(1)}, bf16[256,3072]{1,0:T(8,128)(2,1)S(1)}, u32[]{:S(2)}, u32[]{:S(2)}) collective-permute-start(bf16[256,3072]{1,0:T(8,128)(2,1)S(1)} %shard_map.281.refs_0_), channel_id=1, source_target_pairs={{0,16},{4,20},{8,24},{12,28},{16,0},{20,4},{24,8},{28,12},{1,17},{... | collective-permute-start | bytes 4718600 | tf_op jit(solution)/shard_map/w_feed_far_dp4/ppermute | solution.py:66
  229.4 56.6 %collective-permute-start.35 = (bf16[512,3072]{1,0:T(8,128)(2,1)S(1)}, bf16[512,3072]{1,0:T(8,128)(2,1)}, u32[]{:S(2)}, u32[]{:S(2)}) collective-permute-start(bf16[512,3072]{1,0:T(8,128)(2,1)S(1)} %shard_map.286.refs_4_.refs_2_), channel_id=1, source_target_pairs={{0,4},{4,0},{8,12},{12,8},{16,20},{20,16},{24,28},{28,24},{1,5},{5... | collective-permute-start | bytes 9437192 | tf_op jit(solution)/shard_map/w_feed_near_dp1/ppermute | solution.py:66
  229.4 56.6 %collective-permute-start.36 = (bf16[512,3072]{1,0:T(8,128)(2,1)S(1)}, bf16[512,3072]{1,0:T(8,128)(2,1)}, u32[]{:S(2)}, u32[]{:S(2)}) collective-permute-start(bf16[512,3072]{1,0:T(8,128)(2,1)S(1)} %shard_map.287.refs_5_.refs_3_), channel_id=1, source_target_pairs={{0,4},{4,0},{8,12},{12,8},{16,20},{20,16},{24,28},{28,24},{1,5},{5... | collective-permute-start | bytes 9437192 | tf_op jit(solution)/shard_map/w_feed_near_dp1/ppermute | solution.py:66
  255.3 30.8 %collective-permute-start.37 = (bf16[512,3072]{1,0:T(8,128)(2,1)S(1)}, bf16[512,3072]{1,0:T(8,128)(2,1)}, u32[]{:S(2)}, u32[]{:S(2)}) collective-permute-start(bf16[512,3072]{1,0:T(8,128)(2,1)S(1)} %shard_map.288.refs_8_.refs_6_), channel_id=1, source_target_pairs={{0,4},{4,0},{8,12},{12,8},{16,20},{20,16},{24,28},{28,24},{1,5},{5... | collective-permute-start | bytes 9437192 | tf_op jit(solution)/shard_map/w_feed_far_dp1/ppermute | solution.py:66
  256.6 29.5 %collective-permute-start.38 = (bf16[512,3072]{1,0:T(8,128)(2,1)S(1)}, bf16[512,3072]{1,0:T(8,128)(2,1)}, u32[]{:S(2)}, u32[]{:S(2)}) collective-permute-start(bf16[512,3072]{1,0:T(8,128)(2,1)S(1)} %shard_map.289.refs_9_.refs_7_), channel_id=1, source_target_pairs={{0,4},{4,0},{8,12},{12,8},{16,20},{20,16},{24,28},{28,24},{1,5},{5... | collective-permute-start | bytes 9437192 | tf_op jit(solution)/shard_map/w_feed_far_dp1/ppermute | solution.py:66
  375.2 37.0 %collective-permute-start.46 = (bf16[256,3072]{1,0:T(8,128)(2,1)}, bf16[256,3072]{1,0:T(8,128)(2,1)S(1)}, u32[]{:S(2)}, u32[]{:S(2)}) collective-permute-start(bf16[256,3072]{1,0:T(8,128)(2,1)} %get-tuple-element.466), channel_id=1, source_target_pairs={{0,8},{4,12},{8,0},{12,4},{16,24},{20,28},{24,16},{28,20},{1,9},{5... | collective-permute-start | bytes 4718600 | tf_op jit(solution)/shard_map/grad_feed_far_dp2/ppermute | solution.py:66
  376.2 36.7 %collective-permute-start.45 = (bf16[256,3072]{1,0:T(8,128)(2,1)}, bf16[256,3072]{1,0:T(8,128)(2,1)S(1)}, u32[]{:S(2)}, u32[]{:S(2)}) collective-permute-start(bf16[256,3072]{1,0:T(8,128)(2,1)} %get-tuple-element.463), channel_id=1, source_target_pairs={{0,16},{4,20},{8,24},{12,28},{16,0},{20,4},{24,8},{28,12},{1,17},{... | collective-permute-start | bytes 4718600 | tf_op jit(solution)/shard_map/grad_feed_far_dp4/ppermute | solution.py:66
  455.7 34.2 %collective-permute-start.52 = (bf16[256,3072]{1,0:T(8,128)(2,1)}, bf16[256,3072]{1,0:T(8,128)(2,1)S(1)}, u32[]{:S(2)}, u32[]{:S(2)}) collective-permute-start(bf16[256,3072]{1,0:T(8,128)(2,1)} %get-tuple-element.508), channel_id=1, source_target_pairs={{0,8},{4,12},{8,0},{12,4},{16,24},{20,28},{24,16},{28,20},{1,9},{5... | collective-permute-start | bytes 4718600 | tf_op jit(solution)/shard_map/grad_feed_near_dp2/ppermute | solution.py:66
  456.0 35.6 %collective-permute-start.51 = (bf16[256,3072]{1,0:T(8,128)(2,1)}, bf16[256,3072]{1,0:T(8,128)(2,1)S(1)}, u32[]{:S(2)}, u32[]{:S(2)}) collective-permute-start(bf16[256,3072]{1,0:T(8,128)(2,1)} %get-tuple-element.505), channel_id=1, source_target_pairs={{0,16},{4,20},{8,24},{12,28},{16,0},{20,4},{24,8},{28,12},{1,17},{... | collective-permute-start | bytes 4718600 | tf_op jit(solution)/shard_map/grad_feed_near_dp4/ppermute | solution.py:66
  457.2 35.2 %collective-permute-start.50 = (bf16[128,3072]{1,0:T(8,128)(2,1)S(1)}, bf16[128,3072]{1,0:T(8,128)(2,1)}, u32[]{:S(2)}, u32[]{:S(2)}) collective-permute-start(bf16[128,3072]{1,0:T(8,128)(2,1)S(1)} %shard_map.307), channel_id=1, source_target_pairs={{0,2},{1,3},{2,0},{3,1},{4,6},{5,7},{6,4},{7,5},{8,10},{9,11},{10,... | collective-permute-start | bytes 2359304 | tf_op jit(solution)/shard_map/grad_feed_far_tensor2/ppermute | solution.py:66
  492.4 40.3 %collective-permute-start.57 = (bf16[1024,1024]{1,0:T(8,128)(2,1)}, bf16[1024,1024]{1,0:T(8,128)(2,1)S(1)}, u32[]{:S(2)}, u32[]{:S(2)}) collective-permute-start(bf16[1024,1024]{1,0:T(8,128)(2,1)} %shard_map.309), channel_id=1, source_target_pairs={{0,4},{4,0},{8,12},{12,8},{16,20},{20,16},{24,28},{28,24},{1,5},{5... | collective-permute-start | bytes 6291464 | tf_op jit(solution)/shard_map/grad_w_out_dp1/ppermute | solution.py:66
  492.9 37.4 %collective-permute-start.55 = (bf16[128,3072]{1,0:T(8,128)(2,1)S(1)}, bf16[128,3072]{1,0:T(8,128)(2,1)S(1)}, u32[]{:S(2)}, u32[]{:S(2)}) collective-permute-start(bf16[128,3072]{1,0:T(8,128)(2,1)S(1)} %get-tuple-element.534), channel_id=1, source_target_pairs={{0,8},{4,12},{8,0},{12,4},{16,24},{20,28},{24,16},{28,20},{1,9},{5... | collective-permute-start | bytes 2359304 | tf_op jit(solution)/shard_map/grad_feed_near_dp2/ppermute | solution.py:66
  493.4 36.9 %collective-permute-start.56 = (bf16[128,3072]{1,0:T(8,128)(2,1)}, bf16[128,3072]{1,0:T(8,128)(2,1)S(1)}, u32[]{:S(2)}, u32[]{:S(2)}) collective-permute-start(bf16[128,3072]{1,0:T(8,128)(2,1)} %get-tuple-element.535), channel_id=1, source_target_pairs={{0,16},{4,20},{8,24},{12,28},{16,0},{20,4},{24,8},{28,12},{1,17},{... | collective-permute-start | bytes 2359304 | tf_op jit(solution)/shard_map/grad_feed_near_dp4/ppermute | solution.py:66
  494.9 37.8 %collective-permute-start.53 = (bf16[128,3072]{1,0:T(8,128)(2,1)S(1)}, bf16[128,3072]{1,0:T(8,128)(2,1)S(1)}, u32[]{:S(2)}, u32[]{:S(2)}) collective-permute-start(bf16[128,3072]{1,0:T(8,128)(2,1)S(1)} %shard_map.312), channel_id=1, source_target_pairs={{0,2},{1,3},{2,0},{3,1},{4,6},{5,7},{6,4},{7,5},{8,10},{9,11},{10,... | collective-permute-start | bytes 2359304 | tf_op jit(solution)/shard_map/grad_feed_far_tensor2/ppermute | solution.py:66
  563.7 32.4 %collective-permute-start.72 = (bf16[128,3072]{1,0:T(8,128)(2,1)}, bf16[128,3072]{1,0:T(8,128)(2,1)S(1)}, u32[]{:S(2)}, u32[]{:S(2)}) collective-permute-start(bf16[128,3072]{1,0:T(8,128)(2,1)} %get-tuple-element.579), channel_id=1, source_target_pairs={{0,8},{4,12},{8,0},{12,4},{16,24},{20,28},{24,16},{28,20},{1,9},{5... | collective-permute-start | bytes 2359304 | tf_op jit(solution)/shard_map/grad_w_in_dp2/ppermute | solution.py:66
  564.8 31.6 %collective-permute-start.71 = (bf16[128,3072]{1,0:T(8,128)(2,1)}, bf16[128,3072]{1,0:T(8,128)(2,1)S(1)}, u32[]{:S(2)}, u32[]{:S(2)}) collective-permute-start(bf16[128,3072]{1,0:T(8,128)(2,1)} %get-tuple-element.576), channel_id=1, source_target_pairs={{0,16},{4,20},{8,24},{12,28},{16,0},{20,4},{24,8},{28,12},{1,17},{... | collective-permute-start | bytes 2359304 | tf_op jit(solution)/shard_map/grad_w_in_dp4/ppermute | solution.py:66
  587.2 39.4 %collective-permute-start.63 = (bf16[256,2048]{1,0:T(8,128)(2,1)}, bf16[256,2048]{1,0:T(8,128)(2,1)}, u32[]{:S(2)}, u32[]{:S(2)}) collective-permute-start(bf16[256,2048]{1,0:T(8,128)(2,1)} %shard_map.319), channel_id=1, source_target_pairs={{0,1},{1,2},{2,3},{3,0},{4,5},{5,6},{6,7},{7,4},{8,9},{9,10},{10,1... | collective-permute-start | bytes 3145736 | tf_op jit(solution)/shard_map/sum_grad_attn_3/ppermute | solution.py:72
  600.7 34.2 %collective-permute-start.73 = (bf16[128,3072]{1,0:T(8,128)(2,1)}, bf16[128,3072]{1,0:T(8,128)(2,1)}, u32[]{:S(2)}, u32[]{:S(2)}) collective-permute-start(bf16[128,3072]{1,0:T(8,128)(2,1)} %shard_map.327), channel_id=1, source_target_pairs={{0,8},{4,12},{8,0},{12,4},{16,24},{20,28},{24,16},{28,20},{1,9},{5... | collective-permute-start | bytes 2359304 | tf_op jit(solution)/shard_map/grad_w_in_dp2/ppermute | solution.py:66
  601.7 33.1 %collective-permute-start.74 = (bf16[128,3072]{1,0:T(8,128)(2,1)}, bf16[128,3072]{1,0:T(8,128)(2,1)S(1)}, u32[]{:S(2)}, u32[]{:S(2)}) collective-permute-start(bf16[128,3072]{1,0:T(8,128)(2,1)} %shard_map.329), channel_id=1, source_target_pairs={{0,16},{4,20},{8,24},{12,28},{16,0},{20,4},{24,8},{28,12},{1,17},{... | collective-permute-start | bytes 2359304 | tf_op jit(solution)/shard_map/grad_w_in_dp4/ppermute | solution.py:66
  (132 other events, 1580.2 us)

commit v4 on v3

--- a/solution.py
+++ b/solution.py
@@ -1058,7 +1058,8 @@
     grad_out_own = jnp.concatenate(grads_out, axis=0).astype(f32)
     columns = w_out.shape[0]
     grad_wo_own, gain_sum = grad_out_own[:, :columns], grad_out_own[:, columns : columns + 2].T
-    gain_sums = [gain_sum] + [swap(gain_sum, "tensor", k, "gains") for k in range(1, tensor_size)]
+    gain_came = [swap(gain_sum, "tensor", k, "gains") for k in range(1, tensor_size)]
+    gain_sums = [gain_sum] + tie(gain_came, grad_inputs)
     while len(gain_sums) > 1:
         gain_sums = [a + b for a, b in zip(gain_sums[::2], gain_sums[1::2])]
     gain_sum = gain_sums[0]

time: 651 us -> 645 us (level)
  waiting for transfers between devices: 212 us -> 198 us
    ppermute x63, waiting for transfers between devices: 152 us -> 142 us  [swap(): return lax.ppermute(values, axis, [(i, i ^ bits) for i in range(size)])]
    unnamed x180 -> x186, local copies, waits for them, and re-layouts: 34.1 us -> 38 us
  transfers between devices with their start and end apart: 75 -> 75, of which waited for: 30 -> 27; matrix products, arithmetic and copies ran while one was open for 4% -> 4% of each run, Pallas kernels for 41% -> 43%
where the time goes in v4:
time: 645 us; the launch traced here: 634 us
  Pallas kernels  305 us (47%)
  waiting for transfers between devices  198 us (31%)
  starting transfers between devices  67.1 us (10%)
  local copies, waits for them, and re-layouts  44.9 us (7%)
  other arithmetic  15.2 us (2%)
    ppermute x63, waiting for transfers between devices, swap(): return lax.ppermute(values, axis, [(i, i ^ bits) for i in range(size)])  142 us
    pallas_call x8, Pallas kernels, weight_gradient(): call(functools.partial(gradient_kernel, plan, len(more), came_steps), (co...  84 us
    ppermute x63, starting transfers between devices, swap(): return lax.ppermute(values, axis, [(i, i ^ bits) for i in range(size)])  58.8 us
    ppermute x12, waiting for transfers between devices, shift(): lax.ppermute(values, axis, [(i, (i + step) % size) for i in range(size)])  56.3 us
    pallas_call x4, Pallas kernels, terms(): call(functools.partial(terms_kernel, number, paired), (4, steps), rows +...  44.8 us
    pallas_call x4, Pallas kernels, project(): call(functools.partial(project_kernel, number), (columns // size,), [rows...  39.1 us
    unnamed x186, local copies, waits for them, and re-layouts  38 us
    pallas_call x1, Pallas kernels, feed(): call(functools.partial(feed_kernel, number, steps), (number * steps,), [a...  33.1 us
  transfers between devices with their start and end apart: 75, of which 27 were waited for; matrix products, arithmetic and copies ran while one was open for 4% of the time, Pallas kernels for 43%

profile of v4, /device:TPU:0, one launch (start us, length us, event | category | flops | bytes accessed | tf_op | source)
XLA Modules:
  0.0 633.5 jit_solution(6750357824427316905)
XLA Ops:
  37.6 22.1 %collective-permute-done.3.rows = bf16[256,2048]{1,0:T(8,128)(2,1)} collective-permute-done((bf16[256,2048]{1,0:T(8,128)(2,1)S(1)}, bf16[256,2048]{1,0:T(8,128)(2,1)}, u32[]{:S(2)}, u32[]{:S(2)}) %collective-permute-start.3) | collective-permute-done | bytes 1048608 | tf_op jit(solution)/shard_map/rows_attn_2/ppermute | solution.py:72
  62.6 8.5 %collective-permute-done.9 = bf16[1,256]{1,0:T(2,128)(2,1)S(1)} collective-permute-done((bf16[1,256]{1,0:T(2,128)(2,1)S(1)}, bf16[1,256]{1,0:T(2,128)(2,1)S(1)}, u32[]{:S(2)}, u32[]{:S(2)}) %collective-permute-start.9) | collective-permute-done | bytes 544 | tf_op jit(solution)/shard_map/gains_dp2/ppermute | solution.py:66
  102.9 16.7 %shard_map.272.refs_5_ = f32[1024,3072]{1,0:T(8,128)} custom-call(s32[3]{0:T(128)} %pad_add_fusion.places, bf16[256,2048]{1,0:T(8,128)(2,1)} %copy-done.11, bf16[256,2048]{1,0:T(8,128)(2,1)} %copy-done.10, bf16[256,2048]{1,0:T(8,128)(2,1)} %copy-done.12, bf16[512,3072]{1,0:T(8,128)(2,1)} %copy-done.1, bf16[512,3072]{1,0:T(8,128)(2,1)} %copy-done, ...), custom_call_target="tpu_custom_call" | custom-call | tf_op jit(solution)/shard_map/pallas_call | solution.py:324
  122.8 4.5 collective-permute-done.17.refs_0_
  136.6 9.6 %shard_map.275.pre.gates = f32[1024,3072]{1,0:T(8,128)} custom-call(s32[1]{0:T(128)} %bitcast.8.places, bf16[256,2048]{1,0:T(8,128)(2,1)} %copy-done.9, bf16[512,3072]{1,0:T(8,128)(2,1)} %copy-done.1, bf16[512,3072]{1,0:T(8,128)(2,1)} %copy-done, bf16[512,3072]{1,0:T(8,128)(2,1)} %collective-permute-done.14.refs_5_.refs_3_, ...), custom_call_target="tpu_custom_call", output_to_operand_aliasing={{}: (6, {})} | custom-call | tf_op jit(solution)/shard_map/pallas_call | solution.py:324
  146.1 10.4 %shard_map.276 = (bf16[1024,1024]{1,0:T(8,128)(2,1)}, bf16[1024,2048]{1,0:T(8,128)(2,1)}, f32[1024,1024]{1,0:T(8,128)}, f32[1024,256]{1,0:T(8,128)}) custom-call(f32[2,4]{1,0:T(2,128)} %multiply_exponential_fusion.powers, f32[2]{0:T(128)} %copy-done.86, f32[1024,3072]{1,0:T(8,128)} %shard_map.275.pre.gates, f32[1024,128]{1,0:T(8,128)} %get-tuple-element.331.cosine, ...), custom_call_target="tpu_custom_call" | custom-call | tf_op jit(solution)/shard_map/pallas_call | solution.py:502
  156.6 5.3 shard_map.277
  175.5 9.0 %shard_map.279 = (f32[256,2048]{1,0:T(8,128)}, f32[256,2048]{1,0:T(8,128)}, f32[256,2048]{1,0:T(8,128)}) custom-call(s32[3]{0:T(128)} %pad_add_fusion.1.places, bf16[1024,1024]{1,0:T(8,128)(2,1)} %get-tuple-element.553.refs_0_.refs_1_.refs_2_.refs_4_.refs_5_, bf16[1024,1024]{1,0:T(8,128)(2,1)} %get-tuple-element.553.refs_0_.refs_1_.refs_2_.refs_4_.refs_5_, ...), custom_call_target="tpu_custom_call" | custom-call | tf_op jit(solution)/shard_map/pallas_call | solution.py:374
  196.7 26.5 %collective-permute-done.30.refs_1_ = bf16[256,3072]{1,0:T(8,128)(2,1)} collective-permute-done((bf16[256,3072]{1,0:T(8,128)(2,1)S(1)}, bf16[256,3072]{1,0:T(8,128)(2,1)}, u32[]{:S(2)}, u32[]{:S(2)}) %collective-permute-start.30) | collective-permute-done | bytes 1572896 | tf_op jit(solution)/shard_map/w_feed_near_dp2/ppermute | solution.py:66
  229.9 24.8 %collective-permute-done.33.refs_1_ = bf16[256,3072]{1,0:T(8,128)(2,1)S(1)} collective-permute-done((bf16[256,3072]{1,0:T(8,128)(2,1)S(1)}, bf16[256,3072]{1,0:T(8,128)(2,1)S(1)}, u32[]{:S(2)}, u32[]{:S(2)}) %collective-permute-start.33) | collective-permute-done | bytes 1572896 | tf_op jit(solution)/shard_map/w_feed_far_dp2/ppermute | solution.py:66
  261.6 24.4 %collective-permute-done.34.refs_1_ = bf16[256,2048]{1,0:T(8,128)(2,1)S(1)} collective-permute-done((bf16[256,2048]{1,0:T(8,128)(2,1)S(1)}, bf16[256,2048]{1,0:T(8,128)(2,1)S(1)}, u32[]{:S(2)}, u32[]{:S(2)}) %collective-permute-start.34) | collective-permute-done | bytes 1048608 | tf_op jit(solution)/shard_map/rows_mlp_tensor1/ppermute | solution.py:66
  287.0 33.1 %shard_map.291 = (bf16[512,1024]{1,0:T(8,128)(2,1)}, bf16[512,1024]{1,0:T(8,128)(2,1)}, bf16[512,1024]{1,0:T(8,128)(2,1)}, bf16[512,1024]{1,0:T(8,128)(2,1)}, bf...) custom-call(bf16[256,2048]{1,0:T(8,128)(2,1)} %copy-done.15, ...), custom_call_target="tpu_custom_call" | custom-call | tf_op jit(solution)/shard_map/pallas_call | solution.py:677
  320.6 9.9 %shard_map.293 = bf16[1024,3072]{1,0:T(8,128)(2,1)} custom-call(s32[4]{0:T(128)} %constant.90.clone.1.places, bf16[256,2048]{1,0:T(8,128)(2,1)} %copy-done.15, bf16[256,2048]{1,0:T(8,128)(2,1)} %copy-done.73, bf16[256,2048]{1,0:T(8,128)(2,1)} %copy-done.2, bf16[256,2048]{1,0:T(8,128)(2,1)} %copy-done.4, bf16[512,1024]{1,0:T(8,128)(2,1)} %get-tuple-element.453.refs_4_, ...), custom_call_target="tpu_custom_call" | custom-call | tf_op jit(solution)/shard_map/pallas_call | solution.py:789
  330.4 10.4 %shard_map.292 = bf16[1024,3072]{1,0:T(8,128)(2,1)} custom-call(s32[4]{0:T(128)} %constant.90.clone.1.places, bf16[256,2048]{1,0:T(8,128)(2,1)} %copy-done.15, bf16[256,2048]{1,0:T(8,128)(2,1)} %copy-done.73, bf16[256,2048]{1,0:T(8,128)(2,1)} %copy-done.2, bf16[256,2048]{1,0:T(8,128)(2,1)} %copy-done.4, bf16[512,1024]{1,0:T(8,128)(2,1)} %get-tuple-element.431.refs_4_, ...), custom_call_target="tpu_custom_call" | custom-call | tf_op jit(solution)/shard_map/pallas_call | solution.py:789
  348.1 6.6 %collective-permute-done.41.refs_7_ = bf16[1024,3072]{1,0:T(8,128)(2,1)} collective-permute-done((bf16[1024,3072]{1,0:T(8,128)(2,1)}, bf16[1024,3072]{1,0:T(8,128)(2,1)}, u32[]{:S(2)}, u32[]{:S(2)}) %collective-permute-start.41) | collective-permute-done | bytes 6291488 | tf_op jit(solution)/shard_map/grad_feed_far_dp1/ppermute | solution.py:66
  354.8 11.0 %shard_map.295 = (bf16[256,3072]{1,0:T(8,128)(2,1)}, bf16[256,3072]{1,0:T(8,128)(2,1)}, bf16[256,3072]{1,0:T(8,128)(2,1)}, bf16[256,3072]{1,0:T(8,128)(2,1)}) custom-call(s32[4]{0:T(128)} %constant.90.clone.1.places, bf16[256,2048]{1,0:T(8,128)(2,1)} %copy-done.15, bf16[256,2048]{1,0:T(8,128)(2,1)} %copy-done.73, bf16[256,2048]{1,0:T(8,128)(2,1)} %copy-done.2, ...), custom_call_target="tpu_custom_call" | custom-call | tf_op jit(solution)/shard_map/pallas_call | solution.py:789
  365.8 9.3 %collective-permute-done.40.refs_1_ = bf16[256,2048]{1,0:T(8,128)(2,1)S(1)} collective-permute-done((bf16[256,2048]{1,0:T(8,128)(2,1)S(1)}, bf16[256,2048]{1,0:T(8,128)(2,1)S(1)}, u32[]{:S(2)}, u32[]{:S(2)}) %collective-permute-start.40) | collective-permute-done | bytes 1048608 | tf_op jit(solution)/shard_map/rows_grad_mid_1/ppermute | solution.py:72
  377.6 12.0 %shard_map.296 = (f32[256,2048]{1,0:T(8,128)}, bf16[256,2048]{1,0:T(8,128)(2,1)}) custom-call(bf16[512,1024]{1,0:T(8,128)(2,1)} %get-tuple-element.441.refs_6_.refs_0_, bf16[512,1024]{1,0:T(8,128)(2,1)} %get-tuple-element.442.refs_6_.refs_1_, bf16[512,3072]{1,0:T(8,128)(2,1)} %copy-done.6, bf16[512,3072]{1,0:T(8,128)(2,1)} %copy-done.5, ...), custom_call_target="tpu_custom_call" | custom-call | tf_op jit(solution)/shard_map/pallas_call | solution.py:718
  389.6 11.2 %shard_map.297 = (bf16[256,3072]{1,0:T(8,128)(2,1)}, bf16[256,3072]{1,0:T(8,128)(2,1)}, bf16[256,3072]{1,0:T(8,128)(2,1)}, bf16[256,3072]{1,0:T(8,128)(2,1)}) custom-call(s32[4]{0:T(128)} %constant.90.clone.1.places, bf16[256,2048]{1,0:T(8,128)(2,1)} %copy-done.15, bf16[256,2048]{1,0:T(8,128)(2,1)} %copy-done.73, bf16[256,2048]{1,0:T(8,128)(2,1)} %copy-done.2, ...), custom_call_target="tpu_custom_call" | custom-call | tf_op jit(solution)/shard_map/pallas_call | solution.py:789
  402.8 9.4 %collective-permute-done.46.right = bf16[256,3072]{1,0:T(8,128)(2,1)S(1)} collective-permute-done((bf16[256,3072]{1,0:T(8,128)(2,1)}, bf16[256,3072]{1,0:T(8,128)(2,1)S(1)}, u32[]{:S(2)}, u32[]{:S(2)}) %collective-permute-start.46) | collective-permute-done | bytes 1572896 | tf_op jit(solution)/shard_map/grad_feed_far_dp2/ppermute | solution.py:66
  413.6 8.5 %shard_map.300.refs_5_ = f32[1024,1024]{1,0:T(8,128)} custom-call(s32[3]{0:T(128)} %pad_add_fusion.places, bf16[256,2048]{1,0:T(8,128)(2,1)} %copy-done.19, bf16[256,2048]{1,0:T(8,128)(2,1)} %copy-done.74, bf16[256,2048]{1,0:T(8,128)(2,1)} %collective-permute-done.42.refs_2_, bf16[512,1024]{1,0:T(8,128)(2,1)} %copy-done.14, bf16[512,1024]{1,0:T(8,128)(2,1)} %copy-done.13, ...), custom_call_target="tpu_custom_call" | custom-call | tf_op jit(solution)/shard_map/pallas_call | solution.py:324
  422.2 7.5 %collective-permute-done.44.refs_0_.refs_3_ = bf16[256,2048]{1,0:T(8,128)(2,1)} collective-permute-done((bf16[256,2048]{1,0:T(8,128)(2,1)}, bf16[256,2048]{1,0:T(8,128)(2,1)}, u32[]{:S(2)}, u32[]{:S(2)}) %collective-permute-start.44) | collective-permute-done | bytes 1048608 | tf_op jit(solution)/shard_map/rows_grad_mid_3/ppermute | solution.py:72
  432.7 4.3 shard_map.301.grad
  437.0 16.8 %shard_map.302.refs_0_.refs_4_.refs_1_.refs_2_ = bf16[1024,3072]{1,0:T(8,128)(2,1)} custom-call(f32[2,4]{1,0:T(2,128)} %multiply_exponential_fusion.powers, f32[2]{0:T(128)} %copy-done.86, f32[1024,1024]{1,0:T(8,128)} %shard_map.301.grad, f32[1024,3072]{1,0:T(8,128)} %shard_map.275.pre.gates, bf16[1024,2048]{1,0:T(8,128)(2,1)} %get-tuple-element.477.kept, ...), custom_call_target="tpu_custom_call" | custom-call | tf_op jit(solution)/shard_map/pallas_call | solution.py:561
  459.0 11.7 %shard_map.306 = (bf16[256,2048]{1,0:T(8,128)(2,1)}, f32[1,2048]{1,0:T(1,128)}) custom-call(s32[1]{0:T(128)} %bitcast.1.places, bf16[1024,3072]{1,0:T(8,128)(2,1)} %shard_map.302.refs_0_.refs_4_.refs_1_.refs_2_, bf16[512,3072]{1,0:T(8,128)(2,1)} %copy-done.1, bf16[512,3072]{1,0:T(8,128)(2,1)} %copy-done, ...), custom_call_target="tpu_custom_call" | custom-call | tf_op jit(solution)/shard_map/pallas_call | solution.py:374
  470.7 12.6 %shard_map.308 = bf16[1024,3072]{1,0:T(8,128)(2,1)} custom-call(s32[4]{0:T(128)} %pad_add_fusion.2.places, bf16[256,2048]{1,0:T(8,128)(2,1)} %copy-done.11, bf16[256,2048]{1,0:T(8,128)(2,1)} %copy-done.10, bf16[256,2048]{1,0:T(8,128)(2,1)} %copy-done.12, bf16[256,2048]{1,0:T(8,128)(2,1)} %copy-done.9, ...), custom_call_target="tpu_custom_call" | custom-call | tf_op jit(solution)/shard_map/pallas_call | solution.py:789
  483.3 6.8 %shard_map.309 = bf16[1024,1024]{1,0:T(8,128)(2,1)} custom-call(s32[4]{0:T(128)} %pad_add_fusion.2.places, bf16[256,2048]{1,0:T(8,128)(2,1)} %copy-done.19, bf16[256,2048]{1,0:T(8,128)(2,1)} %copy-done.74, bf16[256,2048]{1,0:T(8,128)(2,1)} %collective-permute-done.42.refs_2_, bf16[256,2048]{1,0:T(8,128)(2,1)} %collective-permute-done.44.refs_0_.refs_3_, ...), custom_call_target="tpu_custom_call" | custom-call | tf_op jit(solution)/shard_map/pallas_call | solution.py:789
  498.4 18.8 %shard_map.313 = (f32[256,2048]{1,0:T(8,128)}, f32[256,2048]{1,0:T(8,128)}, f32[256,2048]{1,0:T(8,128)}, f32[1,2048]{1,0:T(1,128)}) custom-call(s32[3]{0:T(128)} %pad_add_fusion.1.places, bf16[1024,3072]{1,0:T(8,128)(2,1)} %shard_map.302.refs_0_.refs_4_.refs_1_.refs_2_, bf16[1024,3072]{1,0:T(8,128)(2,1)} %shard_map.302.refs_0_.refs_4_.refs_1_.refs_2_, ...), custom_call_target="tpu_custom_call" | custom-call | tf_op jit(solution)/shard_map/pallas_call | solution.py:374
  517.2 13.7 %shard_map.314 = (bf16[128,3072]{1,0:T(8,128)(2,1)}, bf16[128,3072]{1,0:T(8,128)(2,1)}, bf16[128,3072]{1,0:T(8,128)(2,1)}, bf16[128,3072]{1,0:T(8,128)(2,1)}, bf...) custom-call(s32[4]{0:T(128)} %pad_add_fusion.2.places, ...), custom_call_target="tpu_custom_call" | custom-call | tf_op jit(solution)/shard_map/pallas_call | solution.py:789
  539.7 8.3 %shard_map.318 = (bf16[256,1280]{1,0:T(8,128)(2,1)}, bf16[256,1280]{1,0:T(8,128)(2,1)}, bf16[256,1280]{1,0:T(8,128)(2,1)}, bf16[256,1280]{1,0:T(8,128)(2,1)}) custom-call(s32[5]{0:T(128)} %stack.26.places, bf16[256,2048]{1,0:T(8,128)(2,1)} %copy-done.19, bf16[256,2048]{1,0:T(8,128)(2,1)} %copy-done.74, bf16[256,2048]{1,0:T(8,128)(2,1)} %collective-permute-done.42.refs_2_, ...), custom_call_target="tpu_custom_call" | custom-call | tf_op jit(solution)/shard_map/pallas_call | solution.py:789
  548.1 13.0 %collective-permute-done.58.left = bf16[256,2048]{1,0:T(8,128)(2,1)S(1)} collective-permute-done((bf16[256,2048]{1,0:T(8,128)(2,1)}, bf16[256,2048]{1,0:T(8,128)(2,1)S(1)}, u32[]{:S(2)}, u32[]{:S(2)}) %collective-permute-start.58) | collective-permute-done | bytes 1048608 | tf_op jit(solution)/shard_map/sum_grad_attn_1/ppermute | solution.py:72
  566.2 13.3 %collective-permute-done.64.right = bf16[256,1280]{1,0:T(8,128)(2,1)} collective-permute-done((bf16[256,1280]{1,0:T(8,128)(2,1)}, bf16[256,1280]{1,0:T(8,128)(2,1)}, u32[]{:S(2)}, u32[]{:S(2)}) %collective-permute-start.64) | collective-permute-done | bytes 655392 | tf_op jit(solution)/shard_map/grad_w_out_dp4/ppermute | solution.py:66
  (425 shorter events, 220.9 us)
Async XLA Ops:
  5.2 28.3 %collective-permute-start = (bf16[256,2048]{1,0:T(8,128)(2,1)S(1)}, bf16[256,2048]{1,0:T(8,128)(2,1)S(1)}, u32[]{:S(2)}, u32[]{:S(2)}) collective-permute-start(bf16[256,2048]{1,0:T(8,128)(2,1)S(1)} %shard_map.257.rows), channel_id=1, source_target_pairs={{0,1},{1,2},{2,3},{3,0},{4,5},{5,6},{6,7},{7,4},{8,9},{9,10},{10,1... | collective-permute-start | bytes 3145736 | tf_op jit(solution)/shard_map/rows_attn_1/ppermute | solution.py:72
  34.6 38.6 %collective-permute-start.5 = (bf16[256,3072]{1,0:T(8,128)(2,1)S(1)}, bf16[256,3072]{1,0:T(8,128)(2,1)S(1)}, u32[]{:S(2)}, u32[]{:S(2)}) collective-permute-start(bf16[256,3072]{1,0:T(8,128)(2,1)S(1)} %shard_map.259.refs_0_), channel_id=1, source_target_pairs={{0,16},{4,20},{8,24},{12,28},{16,0},{20,4},{24,8},{28,12},{1,17},{... | collective-permute-start | bytes 4718600 | tf_op jit(solution)/shard_map/w_in_dp4/ppermute | solution.py:66
  36.1 37.1 %collective-permute-start.6 = (bf16[256,3072]{1,0:T(8,128)(2,1)S(1)}, bf16[256,3072]{1,0:T(8,128)(2,1)S(1)}, u32[]{:S(2)}, u32[]{:S(2)}) collective-permute-start(bf16[256,3072]{1,0:T(8,128)(2,1)S(1)} %shard_map.260.refs_0_), channel_id=1, source_target_pairs={{0,8},{4,12},{8,0},{12,4},{16,24},{20,28},{24,16},{28,20},{1,9},{5... | collective-permute-start | bytes 4718600 | tf_op jit(solution)/shard_map/w_in_dp2/ppermute | solution.py:66
  86.4 42.3 %collective-permute-start.16 = (bf16[256,2048]{1,0:T(8,128)(2,1)}, bf16[256,2048]{1,0:T(8,128)(2,1)}, u32[]{:S(2)}, u32[]{:S(2)}) collective-permute-start(bf16[256,2048]{1,0:T(8,128)(2,1)} %values.2), channel_id=1, source_target_pairs={{0,1},{1,0},{2,3},{3,2},{4,5},{5,4},{6,7},{7,6},{8,9},{9,8},{10,11... | collective-permute-start | bytes 3145736 | tf_op jit(solution)/shard_map/rows_cot_tensor1/ppermute | solution.py:66
  87.4 39.8 %collective-permute-start.17 = (bf16[128,3072]{1,0:T(8,128)(2,1)}, bf16[128,3072]{1,0:T(8,128)(2,1)}, u32[]{:S(2)}, u32[]{:S(2)}) collective-permute-start(bf16[128,3072]{1,0:T(8,128)(2,1)} %get-tuple-element.384), channel_id=1, source_target_pairs={{0,2},{1,3},{2,0},{3,1},{4,6},{5,7},{6,4},{7,5},{8,10},{9,11},{10,... | collective-permute-start | bytes 2359304 | tf_op jit(solution)/shard_map/w_feed_far_tensor2/ppermute | solution.py:66
  90.5 29.2 %collective-permute-start.18 = (bf16[256,1024]{1,0:T(8,128)(2,1)}, bf16[256,1024]{1,0:T(8,128)(2,1)}, u32[]{:S(2)}, u32[]{:S(2)}) collective-permute-start(bf16[256,1024]{1,0:T(8,128)(2,1)} %shard_map.266.refs_0_), channel_id=1, source_target_pairs={{0,16},{4,20},{8,24},{12,28},{16,0},{20,4},{24,8},{28,12},{1,17},{... | collective-permute-start | bytes 1572872 | tf_op jit(solution)/shard_map/w_out_dp4/ppermute | solution.py:66
  128.7 27.9 %collective-permute-start.20 = (bf16[512,1024]{1,0:T(8,128)(2,1)S(1)}, bf16[512,1024]{1,0:T(8,128)(2,1)}, u32[]{:S(2)}, u32[]{:S(2)}) collective-permute-start(bf16[512,1024]{1,0:T(8,128)(2,1)S(1)} %shard_map.273.refs_1_.refs_3_), channel_id=1, source_target_pairs={{0,4},{4,0},{8,12},{12,8},{16,20},{20,16},{24,28},{28,24},{1,5},{5... | collective-permute-start | bytes 3145736 | tf_op jit(solution)/shard_map/w_out_dp1/ppermute | solution.py:66
  128.7 27.9 %collective-permute-start.21 = (bf16[512,1024]{1,0:T(8,128)(2,1)S(1)}, bf16[512,1024]{1,0:T(8,128)(2,1)}, u32[]{:S(2)}, u32[]{:S(2)}) collective-permute-start(bf16[512,1024]{1,0:T(8,128)(2,1)S(1)} %shard_map.274.refs_2_.refs_4_), channel_id=1, source_target_pairs={{0,4},{4,0},{8,12},{12,8},{16,20},{20,16},{24,28},{28,24},{1,5},{5... | collective-permute-start | bytes 3145736 | tf_op jit(solution)/shard_map/w_out_dp1/ppermute | solution.py:66
  129.2 37.3 %collective-permute-start.22 = (bf16[128,3072]{1,0:T(8,128)(2,1)S(1)}, bf16[128,3072]{1,0:T(8,128)(2,1)}, u32[]{:S(2)}, u32[]{:S(2)}) collective-permute-start(bf16[128,3072]{1,0:T(8,128)(2,1)S(1)} %copy-done.47), channel_id=1, source_target_pairs={{0,2},{1,3},{2,0},{3,1},{4,6},{5,7},{6,4},{7,5},{8,10},{9,11},{10,... | collective-permute-start | bytes 2359304 | tf_op jit(solution)/shard_map/w_feed_far_tensor2/ppermute | solution.py:66
  131.1 38.8 %collective-permute-start.27 = (bf16[128,3072]{1,0:T(8,128)(2,1)}, bf16[128,3072]{1,0:T(8,128)(2,1)}, u32[]{:S(2)}, u32[]{:S(2)}) collective-permute-start(bf16[128,3072]{1,0:T(8,128)(2,1)} %get-tuple-element.385.refs_0_), channel_id=1, source_target_pairs={{0,8},{4,12},{8,0},{12,4},{16,24},{20,28},{24,16},{28,20},{1,9},{5... | collective-permute-start | bytes 2359304 | tf_op jit(solution)/shard_map/w_feed_near_dp2/ppermute | solution.py:66
  131.7 38.2 %collective-permute-start.28 = (bf16[128,3072]{1,0:T(8,128)(2,1)S(1)}, bf16[128,3072]{1,0:T(8,128)(2,1)}, u32[]{:S(2)}, u32[]{:S(2)}) collective-permute-start(bf16[128,3072]{1,0:T(8,128)(2,1)S(1)} %copy-done.47), channel_id=1, source_target_pairs={{0,16},{4,20},{8,24},{12,28},{16,0},{20,4},{24,8},{28,12},{1,17},{... | collective-permute-start | bytes 2359304 | tf_op jit(solution)/shard_map/w_feed_near_dp4/ppermute | solution.py:66
  172.7 50.4 %collective-permute-start.30 = (bf16[256,3072]{1,0:T(8,128)(2,1)S(1)}, bf16[256,3072]{1,0:T(8,128)(2,1)}, u32[]{:S(2)}, u32[]{:S(2)}) collective-permute-start(bf16[256,3072]{1,0:T(8,128)(2,1)S(1)} %shard_map.285.refs_0_), channel_id=1, source_target_pairs={{0,8},{4,12},{8,0},{12,4},{16,24},{20,28},{24,16},{28,20},{1,9},{5... | collective-permute-start | bytes 4718600 | tf_op jit(solution)/shard_map/w_feed_near_dp2/ppermute | solution.py:66
  173.6 51.3 %collective-permute-start.29 = (bf16[256,3072]{1,0:T(8,128)(2,1)S(1)}, bf16[256,3072]{1,0:T(8,128)(2,1)}, u32[]{:S(2)}, u32[]{:S(2)}) collective-permute-start(bf16[256,3072]{1,0:T(8,128)(2,1)S(1)} %shard_map.284.refs_0_), channel_id=1, source_target_pairs={{0,16},{4,20},{8,24},{12,28},{16,0},{20,4},{24,8},{28,12},{1,17},{... | collective-permute-start | bytes 4718600 | tf_op jit(solution)/shard_map/w_feed_near_dp4/ppermute | solution.py:66
  194.5 33.2 %collective-permute-start.26 = (bf16[256,2048]{1,0:T(8,128)(2,1)S(1)}, bf16[256,2048]{1,0:T(8,128)(2,1)S(1)}, u32[]{:S(2)}, u32[]{:S(2)}) collective-permute-start(bf16[256,2048]{1,0:T(8,128)(2,1)S(1)} %shard_map.280), channel_id=1, source_target_pairs={{0,1},{1,2},{2,3},{3,0},{4,5},{5,6},{6,7},{7,4},{8,9},{9,10},{10,1... | collective-permute-start | bytes 3145736 | tf_op jit(solution)/shard_map/sum_attn_2/ppermute | solution.py:72
  194.6 60.1 %collective-permute-start.33 = (bf16[256,3072]{1,0:T(8,128)(2,1)S(1)}, bf16[256,3072]{1,0:T(8,128)(2,1)S(1)}, u32[]{:S(2)}, u32[]{:S(2)}) collective-permute-start(bf16[256,3072]{1,0:T(8,128)(2,1)S(1)} %shard_map.282.refs_0_), channel_id=1, source_target_pairs={{0,8},{4,12},{8,0},{12,4},{16,24},{20,28},{24,16},{28,20},{1,9},{5... | collective-permute-start | bytes 4718600 | tf_op jit(solution)/shard_map/w_feed_far_dp2/ppermute | solution.py:66
  195.3 59.6 %collective-permute-start.32 = (bf16[256,3072]{1,0:T(8,128)(2,1)S(1)}, bf16[256,3072]{1,0:T(8,128)(2,1)S(1)}, u32[]{:S(2)}, u32[]{:S(2)}) collective-permute-start(bf16[256,3072]{1,0:T(8,128)(2,1)S(1)} %shard_map.281.refs_0_), channel_id=1, source_target_pairs={{0,16},{4,20},{8,24},{12,28},{16,0},{20,4},{24,8},{28,12},{1,17},{... | collective-permute-start | bytes 4718600 | tf_op jit(solution)/shard_map/w_feed_far_dp4/ppermute | solution.py:66
  229.4 56.6 %collective-permute-start.35 = (bf16[512,3072]{1,0:T(8,128)(2,1)S(1)}, bf16[512,3072]{1,0:T(8,128)(2,1)}, u32[]{:S(2)}, u32[]{:S(2)}) collective-permute-start(bf16[512,3072]{1,0:T(8,128)(2,1)S(1)} %shard_map.286.refs_4_.refs_2_), channel_id=1, source_target_pairs={{0,4},{4,0},{8,12},{12,8},{16,20},{20,16},{24,28},{28,24},{1,5},{5... | collective-permute-start | bytes 9437192 | tf_op jit(solution)/shard_map/w_feed_near_dp1/ppermute | solution.py:66
  229.4 56.6 %collective-permute-start.36 = (bf16[512,3072]{1,0:T(8,128)(2,1)S(1)}, bf16[512,3072]{1,0:T(8,128)(2,1)}, u32[]{:S(2)}, u32[]{:S(2)}) collective-permute-start(bf16[512,3072]{1,0:T(8,128)(2,1)S(1)} %shard_map.287.refs_5_.refs_3_), channel_id=1, source_target_pairs={{0,4},{4,0},{8,12},{12,8},{16,20},{20,16},{24,28},{28,24},{1,5},{5... | collective-permute-start | bytes 9437192 | tf_op jit(solution)/shard_map/w_feed_near_dp1/ppermute | solution.py:66
  255.2 30.8 %collective-permute-start.37 = (bf16[512,3072]{1,0:T(8,128)(2,1)S(1)}, bf16[512,3072]{1,0:T(8,128)(2,1)}, u32[]{:S(2)}, u32[]{:S(2)}) collective-permute-start(bf16[512,3072]{1,0:T(8,128)(2,1)S(1)} %shard_map.288.refs_8_.refs_6_), channel_id=1, source_target_pairs={{0,4},{4,0},{8,12},{12,8},{16,20},{20,16},{24,28},{28,24},{1,5},{5... | collective-permute-start | bytes 9437192 | tf_op jit(solution)/shard_map/w_feed_far_dp1/ppermute | solution.py:66
  256.6 29.4 %collective-permute-start.38 = (bf16[512,3072]{1,0:T(8,128)(2,1)S(1)}, bf16[512,3072]{1,0:T(8,128)(2,1)}, u32[]{:S(2)}, u32[]{:S(2)}) collective-permute-start(bf16[512,3072]{1,0:T(8,128)(2,1)S(1)} %shard_map.289.refs_9_.refs_7_), channel_id=1, source_target_pairs={{0,4},{4,0},{8,12},{12,8},{16,20},{20,16},{24,28},{28,24},{1,5},{5... | collective-permute-start | bytes 9437192 | tf_op jit(solution)/shard_map/w_feed_far_dp1/ppermute | solution.py:66
  375.1 37.0 %collective-permute-start.46 = (bf16[256,3072]{1,0:T(8,128)(2,1)}, bf16[256,3072]{1,0:T(8,128)(2,1)S(1)}, u32[]{:S(2)}, u32[]{:S(2)}) collective-permute-start(bf16[256,3072]{1,0:T(8,128)(2,1)} %get-tuple-element.469), channel_id=1, source_target_pairs={{0,8},{4,12},{8,0},{12,4},{16,24},{20,28},{24,16},{28,20},{1,9},{5... | collective-permute-start | bytes 4718600 | tf_op jit(solution)/shard_map/grad_feed_far_dp2/ppermute | solution.py:66
  376.1 36.8 %collective-permute-start.45 = (bf16[256,3072]{1,0:T(8,128)(2,1)}, bf16[256,3072]{1,0:T(8,128)(2,1)S(1)}, u32[]{:S(2)}, u32[]{:S(2)}) collective-permute-start(bf16[256,3072]{1,0:T(8,128)(2,1)} %get-tuple-element.466), channel_id=1, source_target_pairs={{0,16},{4,20},{8,24},{12,28},{16,0},{20,4},{24,8},{28,12},{1,17},{... | collective-permute-start | bytes 4718600 | tf_op jit(solution)/shard_map/grad_feed_far_dp4/ppermute | solution.py:66
  456.4 34.2 %collective-permute-start.52 = (bf16[256,3072]{1,0:T(8,128)(2,1)}, bf16[256,3072]{1,0:T(8,128)(2,1)S(1)}, u32[]{:S(2)}, u32[]{:S(2)}) collective-permute-start(bf16[256,3072]{1,0:T(8,128)(2,1)} %get-tuple-element.511), channel_id=1, source_target_pairs={{0,8},{4,12},{8,0},{12,4},{16,24},{20,28},{24,16},{28,20},{1,9},{5... | collective-permute-start | bytes 4718600 | tf_op jit(solution)/shard_map/grad_feed_near_dp2/ppermute | solution.py:66
  456.7 35.5 %collective-permute-start.51 = (bf16[256,3072]{1,0:T(8,128)(2,1)}, bf16[256,3072]{1,0:T(8,128)(2,1)S(1)}, u32[]{:S(2)}, u32[]{:S(2)}) collective-permute-start(bf16[256,3072]{1,0:T(8,128)(2,1)} %get-tuple-element.508), channel_id=1, source_target_pairs={{0,16},{4,20},{8,24},{12,28},{16,0},{20,4},{24,8},{28,12},{1,17},{... | collective-permute-start | bytes 4718600 | tf_op jit(solution)/shard_map/grad_feed_near_dp4/ppermute | solution.py:66
  457.5 35.4 %collective-permute-start.50 = (bf16[128,3072]{1,0:T(8,128)(2,1)S(1)}, bf16[128,3072]{1,0:T(8,128)(2,1)}, u32[]{:S(2)}, u32[]{:S(2)}) collective-permute-start(bf16[128,3072]{1,0:T(8,128)(2,1)S(1)} %shard_map.307), channel_id=1, source_target_pairs={{0,2},{1,3},{2,0},{3,1},{4,6},{5,7},{6,4},{7,5},{8,10},{9,11},{10,... | collective-permute-start | bytes 2359304 | tf_op jit(solution)/shard_map/grad_feed_far_tensor2/ppermute | solution.py:66
  493.0 40.3 %collective-permute-start.57 = (bf16[1024,1024]{1,0:T(8,128)(2,1)}, bf16[1024,1024]{1,0:T(8,128)(2,1)S(1)}, u32[]{:S(2)}, u32[]{:S(2)}) collective-permute-start(bf16[1024,1024]{1,0:T(8,128)(2,1)} %shard_map.309), channel_id=1, source_target_pairs={{0,4},{4,0},{8,12},{12,8},{16,20},{20,16},{24,28},{28,24},{1,5},{5... | collective-permute-start | bytes 6291464 | tf_op jit(solution)/shard_map/grad_w_out_dp1/ppermute | solution.py:66
  493.5 37.4 %collective-permute-start.55 = (bf16[128,3072]{1,0:T(8,128)(2,1)S(1)}, bf16[128,3072]{1,0:T(8,128)(2,1)S(1)}, u32[]{:S(2)}, u32[]{:S(2)}) collective-permute-start(bf16[128,3072]{1,0:T(8,128)(2,1)S(1)} %get-tuple-element.537), channel_id=1, source_target_pairs={{0,8},{4,12},{8,0},{12,4},{16,24},{20,28},{24,16},{28,20},{1,9},{5... | collective-permute-start | bytes 2359304 | tf_op jit(solution)/shard_map/grad_feed_near_dp2/ppermute | solution.py:66
  494.0 36.9 %collective-permute-start.56 = (bf16[128,3072]{1,0:T(8,128)(2,1)}, bf16[128,3072]{1,0:T(8,128)(2,1)S(1)}, u32[]{:S(2)}, u32[]{:S(2)}) collective-permute-start(bf16[128,3072]{1,0:T(8,128)(2,1)} %get-tuple-element.538), channel_id=1, source_target_pairs={{0,16},{4,20},{8,24},{12,28},{16,0},{20,4},{24,8},{28,12},{1,17},{... | collective-permute-start | bytes 2359304 | tf_op jit(solution)/shard_map/grad_feed_near_dp4/ppermute | solution.py:66
  495.6 37.7 %collective-permute-start.53 = (bf16[128,3072]{1,0:T(8,128)(2,1)S(1)}, bf16[128,3072]{1,0:T(8,128)(2,1)S(1)}, u32[]{:S(2)}, u32[]{:S(2)}) collective-permute-start(bf16[128,3072]{1,0:T(8,128)(2,1)S(1)} %shard_map.312), channel_id=1, source_target_pairs={{0,2},{1,3},{2,0},{3,1},{4,6},{5,7},{6,4},{7,5},{8,10},{9,11},{10,... | collective-permute-start | bytes 2359304 | tf_op jit(solution)/shard_map/grad_feed_far_tensor2/ppermute | solution.py:66
  562.5 34.1 %collective-permute-start.72 = (bf16[128,3072]{1,0:T(8,128)(2,1)}, bf16[128,3072]{1,0:T(8,128)(2,1)}, u32[]{:S(2)}, u32[]{:S(2)}) collective-permute-start(bf16[128,3072]{1,0:T(8,128)(2,1)} %get-tuple-element.585), channel_id=1, source_target_pairs={{0,8},{4,12},{8,0},{12,4},{16,24},{20,28},{24,16},{28,20},{1,9},{5... | collective-permute-start | bytes 2359304 | tf_op jit(solution)/shard_map/grad_w_in_dp2/ppermute | solution.py:66
  563.8 34.1 %collective-permute-start.71 = (bf16[128,3072]{1,0:T(8,128)(2,1)}, bf16[128,3072]{1,0:T(8,128)(2,1)}, u32[]{:S(2)}, u32[]{:S(2)}) collective-permute-start(bf16[128,3072]{1,0:T(8,128)(2,1)} %get-tuple-element.582), channel_id=1, source_target_pairs={{0,16},{4,20},{8,24},{12,28},{16,0},{20,4},{24,8},{28,12},{1,17},{... | collective-permute-start | bytes 2359304 | tf_op jit(solution)/shard_map/grad_w_in_dp4/ppermute | solution.py:66
  588.7 29.2 %collective-permute-start.63 = (bf16[256,2048]{1,0:T(8,128)(2,1)}, bf16[256,2048]{1,0:T(8,128)(2,1)}, u32[]{:S(2)}, u32[]{:S(2)}) collective-permute-start(bf16[256,2048]{1,0:T(8,128)(2,1)} %shard_map.319), channel_id=1, source_target_pairs={{0,1},{1,2},{2,3},{3,0},{4,5},{5,6},{6,7},{7,4},{8,9},{9,10},{10,1... | collective-permute-start | bytes 3145736 | tf_op jit(solution)/shard_map/sum_grad_attn_3/ppermute | solution.py:72
  (135 other events, 1578.2 us)

commit v5 on v4

--- a/solution.py
+++ b/solution.py
@@ -139,7 +139,7 @@
     return pieces
 
 
-def call(kernel, grid, in_specs, out_specs, out_shape, vmem=40, scratch=(), scalars=0, aliases=None):
+def call(kernel, grid, in_specs, out_specs, out_shape, vmem=32, scratch=(), scalars=0, aliases=None):
     return pl.pallas_call(
         kernel,
         grid_spec=pltpu.PrefetchScalarGridSpec(
@@ -189,7 +189,7 @@
         specs,
         pl.BlockSpec((height, columns), lambda t: (t, 0)),
         jax.ShapeDtypeStruct((first * height, columns), parts[0].dtype),
-        40,
+        32,
     )(*parts)
 
 
@@ -232,7 +232,7 @@
         [whole, whole],
         [half, half],
         [jax.ShapeDtypeStruct((count // 2, columns), low)] * 2,
-        40,
+        32,
     )(left, right)
 
 
@@ -294,7 +294,7 @@
         [spec],
         spec,
         jax.ShapeDtypeStruct(values.shape, values.dtype),
-        40,
+        32,
         scalars=1,
     )(table, values)
 
@@ -412,7 +412,7 @@
         [rows, rows, rows, pl.BlockSpec((1, width), lambda i: (0, 0))],
         [rows, rows],
         [jax.ShapeDtypeStruct((count, width), f32), jax.ShapeDtypeStruct((count, width), low)],
-        40,
+        32,
     )(values, came, added, gain[None])
 
 
@@ -447,7 +447,7 @@
         [rows, rows, line, rows, rows],
         [rows] + [line, rows] * more,
         [shape(count, f32)] + [shape(1, f32), shape(count, low)] * more,
-        40,
+        32,
     )(values, base, gain[None], grad, came)
 
 

time: 645 us -> 644 us (level)
    unnamed x186 -> x190, local copies, waits for them, and re-layouts: 38 us -> 40.1 us
  transfers between devices with their start and end apart: 75 -> 75, of which waited for: 27 -> 26; matrix products, arithmetic and copies ran while one was open for 4% -> 4% of each run, Pallas kernels for 43% -> 43%
where the time goes in v5:
time: 644 us; the launch traced here: 633 us
  Pallas kernels  306 us (48%)
  waiting for transfers between devices  195 us (30%)
  starting transfers between devices  67.2 us (10%)
  local copies, waits for them, and re-layouts  47.1 us (7%)
  other arithmetic  15.3 us (2%)
    ppermute x63, waiting for transfers between devices, swap(): return lax.ppermute(values, axis, [(i, i ^ bits) for i in range(size)])  138 us
    pallas_call x8, Pallas kernels, weight_gradient(): call(functools.partial(gradient_kernel, plan, len(more), came_steps), (co...  84 us
    ppermute x63, starting transfers between devices, swap(): return lax.ppermute(values, axis, [(i, i ^ bits) for i in range(size)])  58.3 us
    ppermute x12, waiting for transfers between devices, shift(): lax.ppermute(values, axis, [(i, (i + step) % size) for i in range(size)])  56.5 us
    pallas_call x4, Pallas kernels, terms(): call(functools.partial(terms_kernel, number, paired), (4, steps), rows +...  44.8 us
    unnamed x190, local copies, waits for them, and re-layouts  40.1 us
    pallas_call x4, Pallas kernels, project(): call(functools.partial(project_kernel, number), (columns // size,), [rows...  39.1 us
    pallas_call x1, Pallas kernels, feed(): call(functools.partial(feed_kernel, number, steps), (number * steps,), [a...  33.1 us
  transfers between devices with their start and end apart: 75, of which 26 were waited for; matrix products, arithmetic and copies ran while one was open for 4% of the time, Pallas kernels for 43%

profile of v5, /device:TPU:0, one launch (start us, length us, event | category | flops | bytes accessed | tf_op | source)
XLA Modules:
  0.0 632.6 jit_solution(15920801367937197915)
XLA Ops:
  37.6 22.1 %collective-permute-done.3.rows = bf16[256,2048]{1,0:T(8,128)(2,1)} collective-permute-done((bf16[256,2048]{1,0:T(8,128)(2,1)S(1)}, bf16[256,2048]{1,0:T(8,128)(2,1)}, u32[]{:S(2)}, u32[]{:S(2)}) %collective-permute-start.3) | collective-permute-done | bytes 1048608 | tf_op jit(solution)/shard_map/rows_attn_2/ppermute | solution.py:72
  62.6 8.5 %collective-permute-done.9 = bf16[1,256]{1,0:T(2,128)(2,1)S(1)} collective-permute-done((bf16[1,256]{1,0:T(2,128)(2,1)S(1)}, bf16[1,256]{1,0:T(2,128)(2,1)S(1)}, u32[]{:S(2)}, u32[]{:S(2)}) %collective-permute-start.9) | collective-permute-done | bytes 544 | tf_op jit(solution)/shard_map/gains_dp2/ppermute | solution.py:66
  103.0 16.7 %shard_map.272.refs_5_ = f32[1024,3072]{1,0:T(8,128)} custom-call(s32[3]{0:T(128)} %pad_add_fusion.places, bf16[256,2048]{1,0:T(8,128)(2,1)} %copy-done.11, bf16[256,2048]{1,0:T(8,128)(2,1)} %copy-done.10, bf16[256,2048]{1,0:T(8,128)(2,1)} %copy-done.12, bf16[512,3072]{1,0:T(8,128)(2,1)} %copy-done.1, bf16[512,3072]{1,0:T(8,128)(2,1)} %copy-done, ...), custom_call_target="tpu_custom_call" | custom-call | tf_op jit(solution)/shard_map/pallas_call | solution.py:324
  122.8 4.4 collective-permute-done.17.refs_0_
  136.6 9.6 %shard_map.275.pre.gates = f32[1024,3072]{1,0:T(8,128)} custom-call(s32[1]{0:T(128)} %bitcast.8.places, bf16[256,2048]{1,0:T(8,128)(2,1)} %copy-done.9, bf16[512,3072]{1,0:T(8,128)(2,1)} %copy-done.1, bf16[512,3072]{1,0:T(8,128)(2,1)} %copy-done, bf16[512,3072]{1,0:T(8,128)(2,1)} %collective-permute-done.14.refs_5_.refs_3_, ...), custom_call_target="tpu_custom_call", output_to_operand_aliasing={{}: (6, {})} | custom-call | tf_op jit(solution)/shard_map/pallas_call | solution.py:324
  146.2 10.5 %shard_map.276 = (bf16[1024,1024]{1,0:T(8,128)(2,1)}, bf16[1024,2048]{1,0:T(8,128)(2,1)}, f32[1024,1024]{1,0:T(8,128)}, f32[1024,256]{1,0:T(8,128)}) custom-call(f32[2,4]{1,0:T(2,128)} %multiply_exponential_fusion.powers, f32[2]{0:T(128)} %copy-done.88, f32[1024,3072]{1,0:T(8,128)} %shard_map.275.pre.gates, f32[1024,128]{1,0:T(8,128)} %get-tuple-element.331.cosine, ...), custom_call_target="tpu_custom_call" | custom-call | tf_op jit(solution)/shard_map/pallas_call | solution.py:502
  156.7 5.3 shard_map.277
  175.6 9.1 %shard_map.279 = (f32[256,2048]{1,0:T(8,128)}, f32[256,2048]{1,0:T(8,128)}, f32[256,2048]{1,0:T(8,128)}) custom-call(s32[3]{0:T(128)} %pad_add_fusion.1.places, bf16[1024,1024]{1,0:T(8,128)(2,1)} %get-tuple-element.553.refs_0_.refs_1_.refs_2_.refs_4_.refs_5_, bf16[1024,1024]{1,0:T(8,128)(2,1)} %get-tuple-element.553.refs_0_.refs_1_.refs_2_.refs_4_.refs_5_, ...), custom_call_target="tpu_custom_call" | custom-call | tf_op jit(solution)/shard_map/pallas_call | solution.py:374
  196.7 26.6 %collective-permute-done.30.refs_1_ = bf16[256,3072]{1,0:T(8,128)(2,1)} collective-permute-done((bf16[256,3072]{1,0:T(8,128)(2,1)S(1)}, bf16[256,3072]{1,0:T(8,128)(2,1)}, u32[]{:S(2)}, u32[]{:S(2)}) %collective-permute-start.30) | collective-permute-done | bytes 1572896 | tf_op jit(solution)/shard_map/w_feed_near_dp2/ppermute | solution.py:66
  230.0 24.7 %collective-permute-done.33.refs_1_ = bf16[256,3072]{1,0:T(8,128)(2,1)S(1)} collective-permute-done((bf16[256,3072]{1,0:T(8,128)(2,1)S(1)}, bf16[256,3072]{1,0:T(8,128)(2,1)S(1)}, u32[]{:S(2)}, u32[]{:S(2)}) %collective-permute-start.33) | collective-permute-done | bytes 1572896 | tf_op jit(solution)/shard_map/w_feed_far_dp2/ppermute | solution.py:66
  261.7 22.7 %collective-permute-done.34.refs_1_ = bf16[256,2048]{1,0:T(8,128)(2,1)S(1)} collective-permute-done((bf16[256,2048]{1,0:T(8,128)(2,1)S(1)}, bf16[256,2048]{1,0:T(8,128)(2,1)S(1)}, u32[]{:S(2)}, u32[]{:S(2)}) %collective-permute-start.34) | collective-permute-done | bytes 1048608 | tf_op jit(solution)/shard_map/rows_mlp_tensor1/ppermute | solution.py:66
  287.4 33.1 %shard_map.291 = (bf16[512,1024]{1,0:T(8,128)(2,1)}, bf16[512,1024]{1,0:T(8,128)(2,1)}, bf16[512,1024]{1,0:T(8,128)(2,1)}, bf16[512,1024]{1,0:T(8,128)(2,1)}, bf...) custom-call(bf16[256,2048]{1,0:T(8,128)(2,1)} %copy-done.15, ...), custom_call_target="tpu_custom_call" | custom-call | tf_op jit(solution)/shard_map/pallas_call | solution.py:677
  321.2 9.9 %shard_map.293 = bf16[1024,3072]{1,0:T(8,128)(2,1)} custom-call(s32[4]{0:T(128)} %constant.90.clone.1.places, bf16[256,2048]{1,0:T(8,128)(2,1)} %copy-done.15, bf16[256,2048]{1,0:T(8,128)(2,1)} %copy-done.73, bf16[256,2048]{1,0:T(8,128)(2,1)} %copy-done.2, bf16[256,2048]{1,0:T(8,128)(2,1)} %copy-done.4, bf16[512,1024]{1,0:T(8,128)(2,1)} %get-tuple-element.453.refs_4_, ...), custom_call_target="tpu_custom_call" | custom-call | tf_op jit(solution)/shard_map/pallas_call | solution.py:789
  331.0 10.4 %shard_map.292 = bf16[1024,3072]{1,0:T(8,128)(2,1)} custom-call(s32[4]{0:T(128)} %constant.90.clone.1.places, bf16[256,2048]{1,0:T(8,128)(2,1)} %copy-done.15, bf16[256,2048]{1,0:T(8,128)(2,1)} %copy-done.73, bf16[256,2048]{1,0:T(8,128)(2,1)} %copy-done.2, bf16[256,2048]{1,0:T(8,128)(2,1)} %copy-done.4, bf16[512,1024]{1,0:T(8,128)(2,1)} %get-tuple-element.431.refs_4_, ...), custom_call_target="tpu_custom_call" | custom-call | tf_op jit(solution)/shard_map/pallas_call | solution.py:789
  347.2 6.2 collective-permute-done.41.refs_7_
  353.4 11.0 %shard_map.295 = (bf16[256,3072]{1,0:T(8,128)(2,1)}, bf16[256,3072]{1,0:T(8,128)(2,1)}, bf16[256,3072]{1,0:T(8,128)(2,1)}, bf16[256,3072]{1,0:T(8,128)(2,1)}) custom-call(s32[4]{0:T(128)} %constant.90.clone.1.places, bf16[256,2048]{1,0:T(8,128)(2,1)} %copy-done.15, bf16[256,2048]{1,0:T(8,128)(2,1)} %copy-done.73, bf16[256,2048]{1,0:T(8,128)(2,1)} %copy-done.2, ...), custom_call_target="tpu_custom_call" | custom-call | tf_op jit(solution)/shard_map/pallas_call | solution.py:789
  364.4 10.1 %collective-permute-done.40.refs_1_ = bf16[256,2048]{1,0:T(8,128)(2,1)S(1)} collective-permute-done((bf16[256,2048]{1,0:T(8,128)(2,1)S(1)}, bf16[256,2048]{1,0:T(8,128)(2,1)S(1)}, u32[]{:S(2)}, u32[]{:S(2)}) %collective-permute-start.40) | collective-permute-done | bytes 1048608 | tf_op jit(solution)/shard_map/rows_grad_mid_1/ppermute | solution.py:72
  376.4 12.0 %shard_map.296 = (f32[256,2048]{1,0:T(8,128)}, bf16[256,2048]{1,0:T(8,128)(2,1)}) custom-call(bf16[512,1024]{1,0:T(8,128)(2,1)} %get-tuple-element.441.refs_6_.refs_0_, bf16[512,1024]{1,0:T(8,128)(2,1)} %get-tuple-element.442.refs_6_.refs_1_, bf16[512,3072]{1,0:T(8,128)(2,1)} %copy-done.6, bf16[512,3072]{1,0:T(8,128)(2,1)} %copy-done.5, ...), custom_call_target="tpu_custom_call" | custom-call | tf_op jit(solution)/shard_map/pallas_call | solution.py:718
  388.4 11.2 %shard_map.297 = (bf16[256,3072]{1,0:T(8,128)(2,1)}, bf16[256,3072]{1,0:T(8,128)(2,1)}, bf16[256,3072]{1,0:T(8,128)(2,1)}, bf16[256,3072]{1,0:T(8,128)(2,1)}) custom-call(s32[4]{0:T(128)} %constant.90.clone.1.places, bf16[256,2048]{1,0:T(8,128)(2,1)} %copy-done.15, bf16[256,2048]{1,0:T(8,128)(2,1)} %copy-done.73, bf16[256,2048]{1,0:T(8,128)(2,1)} %copy-done.2, ...), custom_call_target="tpu_custom_call" | custom-call | tf_op jit(solution)/shard_map/pallas_call | solution.py:789
  402.2 9.4 %collective-permute-done.46.right = bf16[256,3072]{1,0:T(8,128)(2,1)S(1)} collective-permute-done((bf16[256,3072]{1,0:T(8,128)(2,1)}, bf16[256,3072]{1,0:T(8,128)(2,1)S(1)}, u32[]{:S(2)}, u32[]{:S(2)}) %collective-permute-start.46) | collective-permute-done | bytes 1572896 | tf_op jit(solution)/shard_map/grad_feed_far_dp2/ppermute | solution.py:66
  413.1 8.5 %shard_map.300.refs_5_ = f32[1024,1024]{1,0:T(8,128)} custom-call(s32[3]{0:T(128)} %pad_add_fusion.places, bf16[256,2048]{1,0:T(8,128)(2,1)} %copy-done.19, bf16[256,2048]{1,0:T(8,128)(2,1)} %copy-done.76, bf16[256,2048]{1,0:T(8,128)(2,1)} %collective-permute-done.42.refs_2_, bf16[512,1024]{1,0:T(8,128)(2,1)} %copy-done.14, bf16[512,1024]{1,0:T(8,128)(2,1)} %copy-done.13, ...), custom_call_target="tpu_custom_call" | custom-call | tf_op jit(solution)/shard_map/pallas_call | solution.py:324
  421.6 8.0 %collective-permute-done.44.refs_0_.refs_3_ = bf16[256,2048]{1,0:T(8,128)(2,1)} collective-permute-done((bf16[256,2048]{1,0:T(8,128)(2,1)}, bf16[256,2048]{1,0:T(8,128)(2,1)}, u32[]{:S(2)}, u32[]{:S(2)}) %collective-permute-start.44) | collective-permute-done | bytes 1048608 | tf_op jit(solution)/shard_map/rows_grad_mid_3/ppermute | solution.py:72
  430.9 4.3 shard_map.301.grad
  435.2 16.8 %shard_map.302.refs_0_.refs_4_.refs_1_.refs_2_ = bf16[1024,3072]{1,0:T(8,128)(2,1)} custom-call(f32[2,4]{1,0:T(2,128)} %multiply_exponential_fusion.powers, f32[2]{0:T(128)} %copy-done.88, f32[1024,1024]{1,0:T(8,128)} %shard_map.301.grad, f32[1024,3072]{1,0:T(8,128)} %shard_map.275.pre.gates, bf16[1024,2048]{1,0:T(8,128)(2,1)} %get-tuple-element.477.kept, ...), custom_call_target="tpu_custom_call" | custom-call | tf_op jit(solution)/shard_map/pallas_call | solution.py:561
  458.2 11.7 %shard_map.306 = (bf16[256,2048]{1,0:T(8,128)(2,1)}, f32[1,2048]{1,0:T(1,128)}) custom-call(s32[1]{0:T(128)} %bitcast.1.places, bf16[1024,3072]{1,0:T(8,128)(2,1)} %shard_map.302.refs_0_.refs_4_.refs_1_.refs_2_, bf16[512,3072]{1,0:T(8,128)(2,1)} %copy-done.1, bf16[512,3072]{1,0:T(8,128)(2,1)} %copy-done, ...), custom_call_target="tpu_custom_call" | custom-call | tf_op jit(solution)/shard_map/pallas_call | solution.py:374
  470.0 12.6 %shard_map.308 = bf16[1024,3072]{1,0:T(8,128)(2,1)} custom-call(s32[4]{0:T(128)} %pad_add_fusion.2.places, bf16[256,2048]{1,0:T(8,128)(2,1)} %copy-done.11, bf16[256,2048]{1,0:T(8,128)(2,1)} %copy-done.10, bf16[256,2048]{1,0:T(8,128)(2,1)} %copy-done.12, bf16[256,2048]{1,0:T(8,128)(2,1)} %copy-done.9, ...), custom_call_target="tpu_custom_call" | custom-call | tf_op jit(solution)/shard_map/pallas_call | solution.py:789
  482.6 6.9 %shard_map.309 = bf16[1024,1024]{1,0:T(8,128)(2,1)} custom-call(s32[4]{0:T(128)} %pad_add_fusion.2.places, bf16[256,2048]{1,0:T(8,128)(2,1)} %copy-done.19, bf16[256,2048]{1,0:T(8,128)(2,1)} %copy-done.76, bf16[256,2048]{1,0:T(8,128)(2,1)} %collective-permute-done.42.refs_2_, bf16[256,2048]{1,0:T(8,128)(2,1)} %collective-permute-done.44.refs_0_.refs_3_, ...), custom_call_target="tpu_custom_call" | custom-call | tf_op jit(solution)/shard_map/pallas_call | solution.py:789
  496.6 18.7 %shard_map.313 = (f32[256,2048]{1,0:T(8,128)}, f32[256,2048]{1,0:T(8,128)}, f32[256,2048]{1,0:T(8,128)}, f32[1,2048]{1,0:T(1,128)}) custom-call(s32[3]{0:T(128)} %pad_add_fusion.1.places, bf16[1024,3072]{1,0:T(8,128)(2,1)} %shard_map.302.refs_0_.refs_4_.refs_1_.refs_2_, bf16[1024,3072]{1,0:T(8,128)(2,1)} %shard_map.302.refs_0_.refs_4_.refs_1_.refs_2_, ...), custom_call_target="tpu_custom_call" | custom-call | tf_op jit(solution)/shard_map/pallas_call | solution.py:374
  515.4 13.7 %shard_map.314 = (bf16[128,3072]{1,0:T(8,128)(2,1)}, bf16[128,3072]{1,0:T(8,128)(2,1)}, bf16[128,3072]{1,0:T(8,128)(2,1)}, bf16[128,3072]{1,0:T(8,128)(2,1)}, bf...) custom-call(s32[4]{0:T(128)} %pad_add_fusion.2.places, ...), custom_call_target="tpu_custom_call" | custom-call | tf_op jit(solution)/shard_map/pallas_call | solution.py:789
  539.7 8.3 %shard_map.318 = (bf16[256,1280]{1,0:T(8,128)(2,1)}, bf16[256,1280]{1,0:T(8,128)(2,1)}, bf16[256,1280]{1,0:T(8,128)(2,1)}, bf16[256,1280]{1,0:T(8,128)(2,1)}) custom-call(s32[5]{0:T(128)} %stack.26.places, bf16[256,2048]{1,0:T(8,128)(2,1)} %copy-done.19, bf16[256,2048]{1,0:T(8,128)(2,1)} %copy-done.76, bf16[256,2048]{1,0:T(8,128)(2,1)} %collective-permute-done.42.refs_2_, ...), custom_call_target="tpu_custom_call" | custom-call | tf_op jit(solution)/shard_map/pallas_call | solution.py:789
  548.1 11.2 %collective-permute-done.58.left = bf16[256,2048]{1,0:T(8,128)(2,1)S(1)} collective-permute-done((bf16[256,2048]{1,0:T(8,128)(2,1)}, bf16[256,2048]{1,0:T(8,128)(2,1)S(1)}, u32[]{:S(2)}, u32[]{:S(2)}) %collective-permute-start.58) | collective-permute-done | bytes 1048608 | tf_op jit(solution)/shard_map/sum_grad_attn_1/ppermute | solution.py:72
  564.5 13.3 %collective-permute-done.64.right = bf16[256,1280]{1,0:T(8,128)(2,1)} collective-permute-done((bf16[256,1280]{1,0:T(8,128)(2,1)}, bf16[256,1280]{1,0:T(8,128)(2,1)}, u32[]{:S(2)}, u32[]{:S(2)}) %collective-permute-start.64) | collective-permute-done | bytes 655392 | tf_op jit(solution)/shard_map/grad_w_out_dp4/ppermute | solution.py:66
  (429 shorter events, 222.4 us)
Async XLA Ops:
  5.2 28.3 %collective-permute-start = (bf16[256,2048]{1,0:T(8,128)(2,1)S(1)}, bf16[256,2048]{1,0:T(8,128)(2,1)S(1)}, u32[]{:S(2)}, u32[]{:S(2)}) collective-permute-start(bf16[256,2048]{1,0:T(8,128)(2,1)S(1)} %shard_map.257.rows), channel_id=1, source_target_pairs={{0,1},{1,2},{2,3},{3,0},{4,5},{5,6},{6,7},{7,4},{8,9},{9,10},{10,1... | collective-permute-start | bytes 3145736 | tf_op jit(solution)/shard_map/rows_attn_1/ppermute | solution.py:72
  34.6 38.6 %collective-permute-start.5 = (bf16[256,3072]{1,0:T(8,128)(2,1)S(1)}, bf16[256,3072]{1,0:T(8,128)(2,1)S(1)}, u32[]{:S(2)}, u32[]{:S(2)}) collective-permute-start(bf16[256,3072]{1,0:T(8,128)(2,1)S(1)} %shard_map.259.refs_0_), channel_id=1, source_target_pairs={{0,16},{4,20},{8,24},{12,28},{16,0},{20,4},{24,8},{28,12},{1,17},{... | collective-permute-start | bytes 4718600 | tf_op jit(solution)/shard_map/w_in_dp4/ppermute | solution.py:66
  36.1 37.1 %collective-permute-start.6 = (bf16[256,3072]{1,0:T(8,128)(2,1)S(1)}, bf16[256,3072]{1,0:T(8,128)(2,1)S(1)}, u32[]{:S(2)}, u32[]{:S(2)}) collective-permute-start(bf16[256,3072]{1,0:T(8,128)(2,1)S(1)} %shard_map.260.refs_0_), channel_id=1, source_target_pairs={{0,8},{4,12},{8,0},{12,4},{16,24},{20,28},{24,16},{28,20},{1,9},{5... | collective-permute-start | bytes 4718600 | tf_op jit(solution)/shard_map/w_in_dp2/ppermute | solution.py:66
  86.4 42.3 %collective-permute-start.16 = (bf16[256,2048]{1,0:T(8,128)(2,1)}, bf16[256,2048]{1,0:T(8,128)(2,1)}, u32[]{:S(2)}, u32[]{:S(2)}) collective-permute-start(bf16[256,2048]{1,0:T(8,128)(2,1)} %values.2), channel_id=1, source_target_pairs={{0,1},{1,0},{2,3},{3,2},{4,5},{5,4},{6,7},{7,6},{8,9},{9,8},{10,11... | collective-permute-start | bytes 3145736 | tf_op jit(solution)/shard_map/rows_cot_tensor1/ppermute | solution.py:66
  87.4 39.8 %collective-permute-start.17 = (bf16[128,3072]{1,0:T(8,128)(2,1)}, bf16[128,3072]{1,0:T(8,128)(2,1)}, u32[]{:S(2)}, u32[]{:S(2)}) collective-permute-start(bf16[128,3072]{1,0:T(8,128)(2,1)} %get-tuple-element.384), channel_id=1, source_target_pairs={{0,2},{1,3},{2,0},{3,1},{4,6},{5,7},{6,4},{7,5},{8,10},{9,11},{10,... | collective-permute-start | bytes 2359304 | tf_op jit(solution)/shard_map/w_feed_far_tensor2/ppermute | solution.py:66
  90.5 29.2 %collective-permute-start.18 = (bf16[256,1024]{1,0:T(8,128)(2,1)}, bf16[256,1024]{1,0:T(8,128)(2,1)}, u32[]{:S(2)}, u32[]{:S(2)}) collective-permute-start(bf16[256,1024]{1,0:T(8,128)(2,1)} %shard_map.266.refs_0_), channel_id=1, source_target_pairs={{0,16},{4,20},{8,24},{12,28},{16,0},{20,4},{24,8},{28,12},{1,17},{... | collective-permute-start | bytes 1572872 | tf_op jit(solution)/shard_map/w_out_dp4/ppermute | solution.py:66
  128.7 28.0 %collective-permute-start.21 = (bf16[512,1024]{1,0:T(8,128)(2,1)S(1)}, bf16[512,1024]{1,0:T(8,128)(2,1)}, u32[]{:S(2)}, u32[]{:S(2)}) collective-permute-start(bf16[512,1024]{1,0:T(8,128)(2,1)S(1)} %shard_map.274.refs_2_.refs_4_), channel_id=1, source_target_pairs={{0,4},{4,0},{8,12},{12,8},{16,20},{20,16},{24,28},{28,24},{1,5},{5... | collective-permute-start | bytes 3145736 | tf_op jit(solution)/shard_map/w_out_dp1/ppermute | solution.py:66
  129.2 37.3 %collective-permute-start.22 = (bf16[128,3072]{1,0:T(8,128)(2,1)S(1)}, bf16[128,3072]{1,0:T(8,128)(2,1)}, u32[]{:S(2)}, u32[]{:S(2)}) collective-permute-start(bf16[128,3072]{1,0:T(8,128)(2,1)S(1)} %copy-done.47), channel_id=1, source_target_pairs={{0,2},{1,3},{2,0},{3,1},{4,6},{5,7},{6,4},{7,5},{8,10},{9,11},{10,... | collective-permute-start | bytes 2359304 | tf_op jit(solution)/shard_map/w_feed_far_tensor2/ppermute | solution.py:66
  131.1 38.9 %collective-permute-start.27 = (bf16[128,3072]{1,0:T(8,128)(2,1)}, bf16[128,3072]{1,0:T(8,128)(2,1)}, u32[]{:S(2)}, u32[]{:S(2)}) collective-permute-start(bf16[128,3072]{1,0:T(8,128)(2,1)} %get-tuple-element.385.refs_0_), channel_id=1, source_target_pairs={{0,8},{4,12},{8,0},{12,4},{16,24},{20,28},{24,16},{28,20},{1,9},{5... | collective-permute-start | bytes 2359304 | tf_op jit(solution)/shard_map/w_feed_near_dp2/ppermute | solution.py:66
  131.7 38.3 %collective-permute-start.28 = (bf16[128,3072]{1,0:T(8,128)(2,1)S(1)}, bf16[128,3072]{1,0:T(8,128)(2,1)}, u32[]{:S(2)}, u32[]{:S(2)}) collective-permute-start(bf16[128,3072]{1,0:T(8,128)(2,1)S(1)} %copy-done.47), channel_id=1, source_target_pairs={{0,16},{4,20},{8,24},{12,28},{16,0},{20,4},{24,8},{28,12},{1,17},{... | collective-permute-start | bytes 2359304 | tf_op jit(solution)/shard_map/w_feed_near_dp4/ppermute | solution.py:66
  172.8 50.4 %collective-permute-start.30 = (bf16[256,3072]{1,0:T(8,128)(2,1)S(1)}, bf16[256,3072]{1,0:T(8,128)(2,1)}, u32[]{:S(2)}, u32[]{:S(2)}) collective-permute-start(bf16[256,3072]{1,0:T(8,128)(2,1)S(1)} %shard_map.285.refs_0_), channel_id=1, source_target_pairs={{0,8},{4,12},{8,0},{12,4},{16,24},{20,28},{24,16},{28,20},{1,9},{5... | collective-permute-start | bytes 4718600 | tf_op jit(solution)/shard_map/w_feed_near_dp2/ppermute | solution.py:66
  173.7 51.3 %collective-permute-start.29 = (bf16[256,3072]{1,0:T(8,128)(2,1)S(1)}, bf16[256,3072]{1,0:T(8,128)(2,1)}, u32[]{:S(2)}, u32[]{:S(2)}) collective-permute-start(bf16[256,3072]{1,0:T(8,128)(2,1)S(1)} %shard_map.284.refs_0_), channel_id=1, source_target_pairs={{0,16},{4,20},{8,24},{12,28},{16,0},{20,4},{24,8},{28,12},{1,17},{... | collective-permute-start | bytes 4718600 | tf_op jit(solution)/shard_map/w_feed_near_dp4/ppermute | solution.py:66
  194.5 33.3 %collective-permute-start.26 = (bf16[256,2048]{1,0:T(8,128)(2,1)S(1)}, bf16[256,2048]{1,0:T(8,128)(2,1)S(1)}, u32[]{:S(2)}, u32[]{:S(2)}) collective-permute-start(bf16[256,2048]{1,0:T(8,128)(2,1)S(1)} %shard_map.280), channel_id=1, source_target_pairs={{0,1},{1,2},{2,3},{3,0},{4,5},{5,6},{6,7},{7,4},{8,9},{9,10},{10,1... | collective-permute-start | bytes 3145736 | tf_op jit(solution)/shard_map/sum_attn_2/ppermute | solution.py:72
  194.6 60.1 %collective-permute-start.33 = (bf16[256,3072]{1,0:T(8,128)(2,1)S(1)}, bf16[256,3072]{1,0:T(8,128)(2,1)S(1)}, u32[]{:S(2)}, u32[]{:S(2)}) collective-permute-start(bf16[256,3072]{1,0:T(8,128)(2,1)S(1)} %shard_map.282.refs_0_), channel_id=1, source_target_pairs={{0,8},{4,12},{8,0},{12,4},{16,24},{20,28},{24,16},{28,20},{1,9},{5... | collective-permute-start | bytes 4718600 | tf_op jit(solution)/shard_map/w_feed_far_dp2/ppermute | solution.py:66
  195.4 59.5 %collective-permute-start.32 = (bf16[256,3072]{1,0:T(8,128)(2,1)S(1)}, bf16[256,3072]{1,0:T(8,128)(2,1)S(1)}, u32[]{:S(2)}, u32[]{:S(2)}) collective-permute-start(bf16[256,3072]{1,0:T(8,128)(2,1)S(1)} %shard_map.281.refs_0_), channel_id=1, source_target_pairs={{0,16},{4,20},{8,24},{12,28},{16,0},{20,4},{24,8},{28,12},{1,17},{... | collective-permute-start | bytes 4718600 | tf_op jit(solution)/shard_map/w_feed_far_dp4/ppermute | solution.py:66
  229.5 54.9 %collective-permute-start.35 = (bf16[512,3072]{1,0:T(8,128)(2,1)S(1)}, bf16[512,3072]{1,0:T(8,128)(2,1)S(1)}, u32[]{:S(2)}, u32[]{:S(2)}) collective-permute-start(bf16[512,3072]{1,0:T(8,128)(2,1)S(1)} %shard_map.286.refs_4_.refs_2_), channel_id=1, source_target_pairs={{0,4},{4,0},{8,12},{12,8},{16,20},{20,16},{24,28},{28,24},{1,5},{5... | collective-permute-start | bytes 9437192 | tf_op jit(solution)/shard_map/w_feed_near_dp1/ppermute | solution.py:66
  229.5 54.9 %collective-permute-start.36 = (bf16[512,3072]{1,0:T(8,128)(2,1)S(1)}, bf16[512,3072]{1,0:T(8,128)(2,1)S(1)}, u32[]{:S(2)}, u32[]{:S(2)}) collective-permute-start(bf16[512,3072]{1,0:T(8,128)(2,1)S(1)} %shard_map.287.refs_5_.refs_3_), channel_id=1, source_target_pairs={{0,4},{4,0},{8,12},{12,8},{16,20},{20,16},{24,28},{28,24},{1,5},{5... | collective-permute-start | bytes 9437192 | tf_op jit(solution)/shard_map/w_feed_near_dp1/ppermute | solution.py:66
  255.2 29.2 %collective-permute-start.37 = (bf16[512,3072]{1,0:T(8,128)(2,1)S(1)}, bf16[512,3072]{1,0:T(8,128)(2,1)}, u32[]{:S(2)}, u32[]{:S(2)}) collective-permute-start(bf16[512,3072]{1,0:T(8,128)(2,1)S(1)} %shard_map.288.refs_8_.refs_6_), channel_id=1, source_target_pairs={{0,4},{4,0},{8,12},{12,8},{16,20},{20,16},{24,28},{28,24},{1,5},{5... | collective-permute-start | bytes 9437192 | tf_op jit(solution)/shard_map/w_feed_far_dp1/ppermute | solution.py:66
  256.6 29.6 %collective-permute-start.38 = (bf16[512,3072]{1,0:T(8,128)(2,1)S(1)}, bf16[512,3072]{1,0:T(8,128)(2,1)}, u32[]{:S(2)}, u32[]{:S(2)}) collective-permute-start(bf16[512,3072]{1,0:T(8,128)(2,1)S(1)} %shard_map.289.refs_9_.refs_7_), channel_id=1, source_target_pairs={{0,4},{4,0},{8,12},{12,8},{16,20},{20,16},{24,28},{28,24},{1,5},{5... | collective-permute-start | bytes 9437192 | tf_op jit(solution)/shard_map/w_feed_far_dp1/ppermute | solution.py:66
  346.0 28.6 %collective-permute-start.40 = (bf16[256,2048]{1,0:T(8,128)(2,1)S(1)}, bf16[256,2048]{1,0:T(8,128)(2,1)S(1)}, u32[]{:S(2)}, u32[]{:S(2)}) collective-permute-start(bf16[256,2048]{1,0:T(8,128)(2,1)S(1)} %get-tuple-element.472.refs_0_), channel_id=1, source_target_pairs={{0,1},{1,2},{2,3},{3,0},{4,5},{5,6},{6,7},{7,4},{8,9},{9,10},{10,1... | collective-permute-start | bytes 3145736 | tf_op jit(solution)/shard_map/rows_grad_mid_1/ppermute | solution.py:72
  374.7 36.9 %collective-permute-start.46 = (bf16[256,3072]{1,0:T(8,128)(2,1)}, bf16[256,3072]{1,0:T(8,128)(2,1)S(1)}, u32[]{:S(2)}, u32[]{:S(2)}) collective-permute-start(bf16[256,3072]{1,0:T(8,128)(2,1)} %get-tuple-element.469), channel_id=1, source_target_pairs={{0,8},{4,12},{8,0},{12,4},{16,24},{20,28},{24,16},{28,20},{1,9},{5... | collective-permute-start | bytes 4718600 | tf_op jit(solution)/shard_map/grad_feed_far_dp2/ppermute | solution.py:66
  375.2 37.1 %collective-permute-start.45 = (bf16[256,3072]{1,0:T(8,128)(2,1)}, bf16[256,3072]{1,0:T(8,128)(2,1)S(1)}, u32[]{:S(2)}, u32[]{:S(2)}) collective-permute-start(bf16[256,3072]{1,0:T(8,128)(2,1)} %get-tuple-element.466), channel_id=1, source_target_pairs={{0,16},{4,20},{8,24},{12,28},{16,0},{20,4},{24,8},{28,12},{1,17},{... | collective-permute-start | bytes 4718600 | tf_op jit(solution)/shard_map/grad_feed_far_dp4/ppermute | solution.py:66
  454.6 35.0 %collective-permute-start.52 = (bf16[256,3072]{1,0:T(8,128)(2,1)}, bf16[256,3072]{1,0:T(8,128)(2,1)S(1)}, u32[]{:S(2)}, u32[]{:S(2)}) collective-permute-start(bf16[256,3072]{1,0:T(8,128)(2,1)} %get-tuple-element.511), channel_id=1, source_target_pairs={{0,8},{4,12},{8,0},{12,4},{16,24},{20,28},{24,16},{28,20},{1,9},{5... | collective-permute-start | bytes 4718600 | tf_op jit(solution)/shard_map/grad_feed_near_dp2/ppermute | solution.py:66
  455.6 35.7 %collective-permute-start.51 = (bf16[256,3072]{1,0:T(8,128)(2,1)}, bf16[256,3072]{1,0:T(8,128)(2,1)S(1)}, u32[]{:S(2)}, u32[]{:S(2)}) collective-permute-start(bf16[256,3072]{1,0:T(8,128)(2,1)} %get-tuple-element.508), channel_id=1, source_target_pairs={{0,16},{4,20},{8,24},{12,28},{16,0},{20,4},{24,8},{28,12},{1,17},{... | collective-permute-start | bytes 4718600 | tf_op jit(solution)/shard_map/grad_feed_near_dp4/ppermute | solution.py:66
  457.5 34.6 %collective-permute-start.50 = (bf16[128,3072]{1,0:T(8,128)(2,1)S(1)}, bf16[128,3072]{1,0:T(8,128)(2,1)}, u32[]{:S(2)}, u32[]{:S(2)}) collective-permute-start(bf16[128,3072]{1,0:T(8,128)(2,1)S(1)} %shard_map.307), channel_id=1, source_target_pairs={{0,2},{1,3},{2,0},{3,1},{4,6},{5,7},{6,4},{7,5},{8,10},{9,11},{10,... | collective-permute-start | bytes 2359304 | tf_op jit(solution)/shard_map/grad_feed_far_tensor2/ppermute | solution.py:66
  492.1 39.5 %collective-permute-start.57 = (bf16[1024,1024]{1,0:T(8,128)(2,1)}, bf16[1024,1024]{1,0:T(8,128)(2,1)S(1)}, u32[]{:S(2)}, u32[]{:S(2)}) collective-permute-start(bf16[1024,1024]{1,0:T(8,128)(2,1)} %shard_map.309), channel_id=1, source_target_pairs={{0,4},{4,0},{8,12},{12,8},{16,20},{20,16},{24,28},{28,24},{1,5},{5... | collective-permute-start | bytes 6291464 | tf_op jit(solution)/shard_map/grad_w_out_dp1/ppermute | solution.py:66
  492.6 36.5 %collective-permute-start.55 = (bf16[128,3072]{1,0:T(8,128)(2,1)S(1)}, bf16[128,3072]{1,0:T(8,128)(2,1)S(1)}, u32[]{:S(2)}, u32[]{:S(2)}) collective-permute-start(bf16[128,3072]{1,0:T(8,128)(2,1)S(1)} %get-tuple-element.537), channel_id=1, source_target_pairs={{0,8},{4,12},{8,0},{12,4},{16,24},{20,28},{24,16},{28,20},{1,9},{5... | collective-permute-start | bytes 2359304 | tf_op jit(solution)/shard_map/grad_feed_near_dp2/ppermute | solution.py:66
  493.0 36.1 %collective-permute-start.56 = (bf16[128,3072]{1,0:T(8,128)(2,1)}, bf16[128,3072]{1,0:T(8,128)(2,1)S(1)}, u32[]{:S(2)}, u32[]{:S(2)}) collective-permute-start(bf16[128,3072]{1,0:T(8,128)(2,1)} %get-tuple-element.538), channel_id=1, source_target_pairs={{0,16},{4,20},{8,24},{12,28},{16,0},{20,4},{24,8},{28,12},{1,17},{... | collective-permute-start | bytes 2359304 | tf_op jit(solution)/shard_map/grad_feed_near_dp4/ppermute | solution.py:66
  494.6 37.0 %collective-permute-start.53 = (bf16[128,3072]{1,0:T(8,128)(2,1)S(1)}, bf16[128,3072]{1,0:T(8,128)(2,1)S(1)}, u32[]{:S(2)}, u32[]{:S(2)}) collective-permute-start(bf16[128,3072]{1,0:T(8,128)(2,1)S(1)} %shard_map.312), channel_id=1, source_target_pairs={{0,2},{1,3},{2,0},{3,1},{4,6},{5,7},{6,4},{7,5},{8,10},{9,11},{10,... | collective-permute-start | bytes 2359304 | tf_op jit(solution)/shard_map/grad_feed_far_tensor2/ppermute | solution.py:66
  562.6 33.2 %collective-permute-start.72 = (bf16[128,3072]{1,0:T(8,128)(2,1)}, bf16[128,3072]{1,0:T(8,128)(2,1)}, u32[]{:S(2)}, u32[]{:S(2)}) collective-permute-start(bf16[128,3072]{1,0:T(8,128)(2,1)} %get-tuple-element.585), channel_id=1, source_target_pairs={{0,8},{4,12},{8,0},{12,4},{16,24},{20,28},{24,16},{28,20},{1,9},{5... | collective-permute-start | bytes 2359304 | tf_op jit(solution)/shard_map/grad_w_in_dp2/ppermute | solution.py:66
  563.0 34.1 %collective-permute-start.71 = (bf16[128,3072]{1,0:T(8,128)(2,1)}, bf16[128,3072]{1,0:T(8,128)(2,1)}, u32[]{:S(2)}, u32[]{:S(2)}) collective-permute-start(bf16[128,3072]{1,0:T(8,128)(2,1)} %get-tuple-element.582), channel_id=1, source_target_pairs={{0,16},{4,20},{8,24},{12,28},{16,0},{20,4},{24,8},{28,12},{1,17},{... | collective-permute-start | bytes 2359304 | tf_op jit(solution)/shard_map/grad_w_in_dp4/ppermute | solution.py:66
  587.7 29.2 %collective-permute-start.63 = (bf16[256,2048]{1,0:T(8,128)(2,1)}, bf16[256,2048]{1,0:T(8,128)(2,1)}, u32[]{:S(2)}, u32[]{:S(2)}) collective-permute-start(bf16[256,2048]{1,0:T(8,128)(2,1)} %shard_map.319), channel_id=1, source_target_pairs={{0,1},{1,2},{2,3},{3,0},{4,5},{5,6},{6,7},{7,4},{8,9},{9,10},{10,1... | collective-permute-start | bytes 3145736 | tf_op jit(solution)/shard_map/sum_grad_attn_3/ppermute | solution.py:72
  (137 other events, 1574.0 us)
